TPU v7x, 256 devices: a whole 4x4x8 slice. The times are simulated.
256 devices in a mesh: tm: 8 (over x, z_lo), space: 32 (over y, z_hi, core).
Axes of the slice: x: 4, y: 4, z: 8 (z_hi: 4, z_lo: 2; z = z_hi * 2 + z_lo), core: 2. Of those that a mesh axis runs over, the one named last changes fastest.
Arguments:
- vectors: bfloat16 [8, 96, 2, 3, 4096], P('tm', None, None, None, 'space'), may hold values from -3 to 3
- gauge_links: bfloat16 [8, 3, 2, 3, 3, 4096], P('tm', None, None, None, None, 'space'), may hold values from -2.6875 to 2.6875
- momentum: int32 [3], replicated, may hold values from -2 to 2
- direction: int32 [8], P('tm'), may hold values from 0 to 2, as said below
Outputs:
- elementals: float32 [96, 8, 2, 9216], P('space', None, None, 'tm')
Inputs may be any that keep to these rules, and one draw needn't show every extreme that they name: `direction`: entry t is 2 for even t; for odd t the entries alternate between 0 and 1 with a drawn first value.
All inputs are finite; a program needn't handle non-finite values.
Results may differ from a plain program's by a relative error of at most 0.0041.
Values may be sent and summed in bfloat16 or wider, within the bound.
No kernel may reach another device: no remote copies, remote signals or barrier semaphores. Data moves between devices by JAX's collectives and lax.ppermute only.
A program may use at most 128 MiB of HBM per device.

v0:
```python
import math

import jax
import jax.numpy as jnp
from jax import lax
from jax.experimental import pallas as pl
from jax.experimental.pallas import tpu as pltpu
from jax.sharding import Mesh
from jax.sharding import PartitionSpec as P

NEV = 96
LX = 16
LY = 8
LZ = 32
SITES = 128
AXES = ("x", "zl", "y", "zh", "c")
SIZES = (4, 2, 4, 4, 2)
DEPTH = 6 * SITES


def ring_pairs(target):
    pairs = []
    for x in range(4):
        for zl in range(2):
            for s in range(32):
                to = target(zl, s)
                if to is not None:
                    head = (x * 2 + zl) * 32
                    pairs.append((head + s, head + to))
    return pairs


def outer_plane(zl, s):
    if zl == 1:
        return None
    return (s + 1) % 32 if s % 2 == 1 else (s - 1) % 32


def phased_kernel(numbers, own, other, outer, out, field, ahead, behind):
    links = own[6 * NEV :, :].astype(jnp.float32)
    direction = numbers[3]
    core = lax.axis_index("c")
    plane = (lax.axis_index("y") * 4 + lax.axis_index("zh")) * 2 + core
    lane = lax.broadcasted_iota(jnp.int32, (1, SITES), 1)
    x_coord = lane % LX
    y_coord = lane // LX
    turns = (
        2 * jnp.bitwise_and(numbers[0] * x_coord, LX - 1)
        + 4 * jnp.bitwise_and(numbers[1] * y_coord, LY - 1)
        + jnp.bitwise_and(numbers[2] * plane, LZ - 1)
    )
    angle = (2.0 * math.pi / LZ) * jnp.bitwise_and(turns, LZ - 1).astype(jnp.float32)
    cos_part = jnp.cos(angle)
    sin_part = -jnp.sin(angle)

    @pl.when(direction == 2)
    def _():
        for comp in range(6):
            near = other[NEV * comp : NEV * comp + NEV, :].astype(jnp.float32)
            far = outer[NEV * comp : NEV * comp + NEV, :].astype(jnp.float32)
            ahead[comp] = jnp.where(core == 0, near, far)
            behind[comp] = jnp.where(core == 0, far, near)

    @pl.when(direction != 2)
    def _():
        step = jnp.where(direction == 0, 1, LX)
        last = jnp.logical_and(x_coord == LX - 1, direction == 0)
        first = jnp.logical_and(x_coord == 0, direction == 0)
        for comp in range(6):
            here = own[NEV * comp : NEV * comp + NEV, :].astype(jnp.float32)
            ahead[comp] = jnp.where(
                last, pltpu.roll(here, LX - 1, 1), pltpu.roll(here, SITES - step, 1)
            )
            behind[comp] = jnp.where(
                first, pltpu.roll(here, SITES - LX + 1, 1), pltpu.roll(here, step, 1)
            )

    z_back = jnp.where(
        core == 0,
        outer[6 * NEV :, :].astype(jnp.float32),
        other[6 * NEV :, :].astype(jnp.float32),
    )
    x_roll = jnp.where(
        x_coord == 0, pltpu.roll(links, SITES - LX + 1, 1), pltpu.roll(links, 1, 1)
    )
    y_roll = pltpu.roll(links, LX, 1)

    def matrix(table, part, row, column):
        return table[6 * row + 2 * column + part]

    here_link = []
    back_link = []
    for at in range(18):
        x_at, y_at, z_at = (slice(at + 18 * d, at + 18 * d + 1) for d in range(3))
        here_link.append(
            jnp.where(
                direction == 0, links[x_at], jnp.where(direction == 1, links[y_at], links[z_at])
            )
        )
        back_link.append(
            jnp.where(
                direction == 0,
                x_roll[x_at],
                jnp.where(direction == 1, y_roll[y_at], z_back[z_at]),
            )
        )

    for a in range(3):
        front_re = front_im = rear_re = rear_im = 0.0
        for b in range(3):
            u_re, u_im = matrix(here_link, 0, a, b), matrix(here_link, 1, a, b)
            v_re, v_im = ahead[b], ahead[3 + b]
            front_re += u_re * v_re - u_im * v_im
            front_im += u_re * v_im + u_im * v_re
            w_re, w_im = matrix(back_link, 0, b, a), matrix(back_link, 1, b, a)
            v_re, v_im = behind[b], behind[3 + b]
            rear_re += w_re * v_re + w_im * v_im
            rear_im += w_re * v_im - w_im * v_re
        moved_re = front_re - rear_re
        moved_im = front_im - rear_im
        field[a] = cos_part * moved_re - sin_part * moved_im
        field[3 + a] = cos_part * moved_im + sin_part * moved_re

    for comp in range(6):
        for rows in range(6):
            both = [field[comp, pl.ds(2 * rows + k, 8, 12), :] for k in range(2)]
            out[comp, 16 * rows : 16 * rows + 16, :] = jnp.concatenate(both, 0).astype(
                jnp.bfloat16
            )


def left_operand(phased, left):
    for a in range(3):
        real = phased[a]
        imag = phased[3 + a]
        column = a * SITES
        left[:NEV, column : column + SITES] = real
        left[NEV:, column : column + SITES] = imag
        column += 3 * SITES
        left[:NEV, column : column + SITES] = -imag
        left[NEV:, column : column + SITES] = real


def times(crossed, left):
    return lax.dot_general(
        crossed, left[...], (((1,), (1,)), ((), ())), preferred_element_type=jnp.float32
    )


def six_rows(step, vectors, out):
    core = lax.axis_index("c")
    keeper = jnp.where(step < 2, 1 - core, core)
    first = 24 * lax.axis_index("y") + 12 * (step % 2) + 3 * keeper
    for high in range(2):
        for low in range(3):
            mine = [vectors[comp, pl.ds(first + 6 * high + low, 1), :] for comp in range(9)]
            mine = [jnp.broadcast_to(m, (16, SITES)) for m in mine]
            my_re, my_im, my_sum = mine[:3], mine[3:6], mine[6:]
            for chunk in range(6):
                rows = slice(16 * chunk, 16 * chunk + 16)
                re, total, gap = (
                    [vectors[comp + colour, rows, :] for colour in range(3)]
                    for comp in (0, 6, 9)
                )
                at = 96 * low + 16 * chunk
                at = 256 * high + at if at < 256 else 256 + 32 * high + at
                for a in range(3):
                    b = (a + 1) % 3
                    c = (a + 2) % 3
                    shared = my_sum[b] * re[c] - my_sum[c] * re[b]
                    real = shared - (my_im[b] * total[c] - my_im[c] * total[b])
                    imag = shared + (my_re[b] * gap[c] - my_re[c] * gap[b])
                    column = a * SITES
                    out[step, at : at + 16, column : column + SITES] = real.astype(
                        jnp.bfloat16
                    )
                    column += 3 * SITES
                    out[step, at : at + 16, column : column + SITES] = imag.astype(
                        jnp.bfloat16
                    )


def spread(source, vectors):
    for colour in range(3):
        real = source[colour].astype(jnp.float32)
        imag = source[3 + colour].astype(jnp.float32)
        vectors[colour] = real
        vectors[3 + colour] = imag
        vectors[6 + colour] = real + imag
        vectors[9 + colour] = imag - real


def crossed_kernel(source, out, vectors):
    spread(source, vectors)

    def one_step(step, carry):
        six_rows(step, vectors, out)
        return carry

    lax.fori_loop(0, 4, one_step, 0)


def both_kernel(source, phased, previous, *rest):
    sums = rest[0] if len(rest) == 5 else None
    out, total, vectors, left = rest[-4:]
    spread(source, vectors)
    left_operand(phased, left)

    def one_step(step, carry):
        term = times(previous[step], left)
        total[step] = term if sums is None else sums[step] + term
        six_rows(step, vectors, out)
        return carry

    lax.fori_loop(0, 4, one_step, 0)


def last_kernel(phased, crossed, sums, theirs, mine, left):
    left_operand(phased, left)
    for out, half in ((theirs, 0), (mine, 1)):
        tails = []
        for part in range(2):
            step = 2 * half + part
            total = sums[step] + times(crossed[step], left)
            out[:, 512 * part : 512 * part + 512] = total[:512].T.astype(out.dtype)
            tails.append(total[512:])
        out[:, 1024:] = jnp.concatenate(tails, 0).T.astype(out.dtype)


def pack_kernel(mine, received, out, total):
    lane = lax.broadcasted_iota(jnp.int32, (8, SITES), 1)
    for tile in range(9):
        lanes = slice(SITES * tile, SITES * tile + SITES)
        total[tile] = mine[:, lanes] + received[:, lanes].astype(jnp.float32)
    for q in range(8):
        for zh in range(4):
            for half in range(2):
                out[4 * q + zh, 24 * half : 24 * half + 24, :] = total[
                    2 * zh + half, pl.ds(q, 24, 8), :
                ].astype(jnp.bfloat16)
        tail = total[8, pl.ds(q, 24, 8), :]
        for zh in range(4):
            joined = jnp.zeros((8, SITES), jnp.float32)
            for g in range(3):
                moved = pltpu.roll(tail[8 * g : 8 * g + 8], (32 * (g - zh)) % SITES, 1)
                joined = jnp.where(lane // 32 == g, moved, joined)
            out[4 * q + zh, 48:56, :] = joined.astype(jnp.bfloat16)


def final_kernel(parts, out, rows):
    scale = 1.0 / math.sqrt(LX * LY * LZ)
    for t in range(8):
        total = parts[4 * t].astype(jnp.float32)
        for zh in range(1, 4):
            total += parts[4 * t + zh].astype(jnp.float32)
        total *= scale
        rows[0, pl.ds(t, 24, 8), :] = total[:24]
        rows[1, pl.ds(t, 24, 8), :] = total[24:48]
        for g in range(3):
            tail = total[48:56]
            if g:
                tail = pltpu.roll(tail, SITES - 32 * g, 1)
            rows[2, pl.ds(64 * g + t, 8, 8), :] = tail
    for ri in range(2):
        pieces = [[], [], []]
        for i in range(12):
            at = 8 * (12 * ri + i)
            one, two, three = (rows[part, at : at + 8, :] for part in range(3))
            pieces[0].append(one[:, :96])
            pieces[1].append(one[:, 96:])
            pieces[1].append(two[:, :64])
            pieces[2].append(two[:, 64:])
            pieces[2].append(three[:, :32])
        for r in range(3):
            out[r, :, ri, :] = jnp.concatenate(pieces[r], axis=1)


def vmem():
    return pl.BlockSpec(memory_space=pltpu.VMEM)


def smem():
    return pl.BlockSpec(memory_space=pltpu.SMEM)


def params(mib):
    return pltpu.CompilerParams(vmem_limit_bytes=mib << 20)


def from_y(block, by):
    return lax.ppermute(block, "y", [(i, (i + by) % 4) for i in range(4)])


def on_device(vectors, gauge_links, momentum, direction):
    f32 = jnp.float32
    bf16 = jnp.bfloat16
    swap = [(0, 1), (1, 0)]
    own = jnp.transpose(vectors[0], (1, 2, 0, 3)).reshape(6, NEV, SITES)
    joined = jnp.concatenate(
        [
            own.reshape(6 * NEV, SITES),
            jnp.transpose(gauge_links[0], (0, 2, 3, 1, 4)).reshape(54, SITES),
            jnp.zeros((10, SITES), bf16),
        ]
    )
    outer = lax.ppermute(joined, AXES, ring_pairs(outer_plane))
    other = lax.ppermute(joined, "c", swap)
    before = from_y(own, 1)
    after = from_y(own, 3)
    opposite = from_y(own, 2)
    phased = pl.pallas_call(
        phased_kernel,
        out_shape=jax.ShapeDtypeStruct((6, NEV, SITES), bf16),
        in_specs=[vmem()] * 4,
        out_specs=vmem(),
        scratch_shapes=[pltpu.VMEM((6, NEV, SITES), f32)] * 3,
        compiler_params=params(8),
    )(jnp.concatenate([momentum, direction]), joined, other, outer)
    phased_before = from_y(phased, 1)
    phased_after = from_y(phased, 3)
    phased_opposite = from_y(phased, 2)
    before, after, opposite = lax.optimization_barrier((before, after, opposite))

    crossed_shape = jax.ShapeDtypeStruct((4, 576, DEPTH), bf16)
    sums_shape = jax.ShapeDtypeStruct((4, 576, 192), f32)
    spread_scratch = pltpu.VMEM((12, NEV, SITES), f32)
    left_scratch = pltpu.VMEM((192, DEPTH), bf16)
    short = pl.CostEstimate(flops=0, bytes_accessed=0, transcendentals=0)

    def both(source, phased_plane, previous, *sums):
        return pl.pallas_call(
            both_kernel,
            out_shape=(crossed_shape, sums_shape),
            in_specs=[vmem()] * (3 + len(sums)),
            out_specs=(vmem(), vmem()),
            scratch_shapes=[spread_scratch, left_scratch],
            compiler_params=params(6),
            cost_estimate=short,
        )(source, phased_plane, previous, *sums)

    crossed = pl.pallas_call(
        crossed_kernel,
        out_shape=crossed_shape,
        in_specs=[vmem()],
        out_specs=vmem(),
        scratch_shapes=[spread_scratch],
        compiler_params=params(4),
        cost_estimate=short,
    )(own)
    crossed, sums = both(before, phased, crossed)
    crossed, sums = both(after, phased_before, crossed, sums)
    crossed, sums = both(opposite, phased_after, crossed, sums)
    sent, mine = pl.pallas_call(
        last_kernel,
        out_shape=(
            jax.ShapeDtypeStruct((192, 1152), bf16),
            jax.ShapeDtypeStruct((192, 1152), f32),
        ),
        in_specs=[vmem()] * 3,
        out_specs=(vmem(), vmem()),
        scratch_shapes=[left_scratch],
        compiler_params=params(6),
    )(phased_opposite, crossed, sums)
    received = lax.ppermute(sent, "c", swap)
    packed = pl.pallas_call(
        pack_kernel,
        out_shape=jax.ShapeDtypeStruct((32, 56, SITES), bf16),
        in_specs=[vmem()] * 2,
        out_specs=vmem(),
        scratch_shapes=[pltpu.VMEM((9, 192, SITES), f32)],
        compiler_params=params(16),
    )(mine, received)
    packed = lax.all_to_all(packed, ("x", "zl", "zh"), 0, 0, tiled=True)
    return pl.pallas_call(
        final_kernel,
        out_shape=jax.ShapeDtypeStruct((3, 8, 2, 12 * NEV), f32),
        in_specs=[vmem()],
        out_specs=vmem(),
        scratch_shapes=[pltpu.VMEM((3, 192, SITES), f32)],
        compiler_params=params(16),
    )(packed)


def solution(mesh):
    cut = Mesh(mesh.devices.reshape(SIZES), AXES)
    return jax.shard_map(
        on_device,
        mesh=cut,
        in_specs=(
            P(("x", "zl"), None, None, None, ("y", "zh", "c")),
            P(("x", "zl"), None, None, None, None, ("y", "zh", "c")),
            P(),
            P(("x", "zl")),
        ),
        out_specs=P(("y", "zh", "c"), None, None, ("x", "zl")),
        check_vma=False,
    )
```

profile of v0, /device:TPU:64, one launch (start us, length us, event | category | flops | bytes accessed | tf_op | source)
XLA Modules:
  0.0 57.2 jit_solution(5711422427756201875)
XLA Ops:
  0.0 0.9 %copy.5 = bf16[2,3,96,128]{3,2,1,0:T(8,128)(2,1)S(1)} copy(bf16[2,3,96,128]{3,0,1,2:T(2,128)(2,1)} %bitcast.13) | data formatting | bytes 294912 | tf_op jit(solution)/shard_map/transpose | solution.py:298
  0.9 0.7 %reshape.6 = bf16[54,128]{1,0:T(8,128)(2,1)S(1)} reshape(bf16[3,3,3,2,128]{4,3,2,1,0:T(2,128)(2,1)} %bitcast.14) | data formatting | bytes 27648 | tf_op jit(solution)/shard_map/reshape | solution.py:302
  1.7 0.1 pad.2.clone
  1.8 0.2 maximum_maximum_fusion.own
  1.9 0.1 collective-permute-start
  2.0 3.4 %collective-permute-start.1 = (bf16[640,128]{1,0:T(8,128)(2,1)S(1)}, bf16[640,128]{1,0:T(8,128)(2,1)S(1)}, u32[]{:S(2)}, u32[]{:S(2)}) collective-permute-start(bf16[640,128]{1,0:T(8,128)(2,1)S(1)} %maximum_maximum_fusion.own), channel_id=1, source_target_pairs={{0,31},{1,2},{2,1},{3,4},{4,3},{5,6},{6,5},{7,8},{8,7},{9,10},{10,... | collective-permute-start | bytes 491528 | tf_op jit(solution)/shard_map/ppermute | solution.py:306
  5.4 0.2 collective-permute-start.3
  5.6 3.1 %collective-permute-start.4 = (bf16[6,96,128]{2,1,0:T(8,128)(2,1)S(1)}, bf16[6,96,128]{2,1,0:T(8,128)(2,1)S(1)}, u32[]{:S(2)}, u32[]{:S(2)}) collective-permute-start(bf16[6,96,128]{2,1,0:T(8,128)(2,1)S(1)} %bitcast.10), channel_id=1, source_target_pairs={{0,24},{8,0},{16,8},{24,16},{1,25},{9,1},{17,9},{25,17},{2,26},{10... | collective-permute-start | bytes 442376 | tf_op jit(solution)/shard_map/ppermute | solution.py:291
  8.7 0.5 collective-permute-start.5
  9.9 0.7 %pad_add_fusion.numbers = s32[4]{0:T(128)S(1)} fusion(s32[1]{0:T(128)S(6)} %copy.7, s32[3]{0:T(128)} %param.6), kind=kLoop, calls=%fused_computation.1 | loop fusion | flops 4 | bytes 32 | tf_op jit(solution)/shard_map/concatenate | solution.py:318
  10.6 0.0 collective-permute-done.other
  10.6 0.0 collective-permute-done.1.outer
  10.6 0.5 shard_map.46.phased
  11.1 0.8 %collective-permute-start.7 = (bf16[6,96,128]{2,1,0:T(8,128)(2,1)S(1)}, bf16[6,96,128]{2,1,0:T(8,128)(2,1)S(1)}, u32[]{:S(2)}, u32[]{:S(2)}) collective-permute-start(bf16[6,96,128]{2,1,0:T(8,128)(2,1)S(1)} %shard_map.46.phased), channel_id=1, source_target_pairs={{0,8},{8,16},{16,24},{24,0},{1,9},{9,17},{17,25},{25,1},{2,10},{10... | collective-permute-start | bytes 442376 | tf_op jit(solution)/shard_map/ppermute | solution.py:291
  11.9 2.6 %collective-permute-start.6 = (bf16[6,96,128]{2,1,0:T(8,128)(2,1)S(1)}, bf16[6,96,128]{2,1,0:T(8,128)(2,1)S(1)}, u32[]{:S(2)}, u32[]{:S(2)}) collective-permute-start(bf16[6,96,128]{2,1,0:T(8,128)(2,1)S(1)} %shard_map.46.phased), channel_id=1, source_target_pairs={{0,24},{8,0},{16,8},{24,16},{1,25},{9,1},{17,9},{25,17},{2,26},{10... | collective-permute-start | bytes 442376 | tf_op jit(solution)/shard_map/ppermute | solution.py:291
  14.5 0.0 collective-permute-done.3.source
  14.5 1.8 %collective-permute-start.2 = (bf16[6,96,128]{2,1,0:T(8,128)(2,1)S(1)}, bf16[6,96,128]{2,1,0:T(8,128)(2,1)S(1)}, u32[]{:S(2)}, u32[]{:S(2)}) collective-permute-start(bf16[6,96,128]{2,1,0:T(8,128)(2,1)S(1)} %shard_map.46.phased), channel_id=1, source_target_pairs={{0,16},{8,24},{16,0},{24,8},{1,17},{9,25},{17,1},{25,9},{2,18},{10... | collective-permute-start | bytes 442376 | tf_op jit(solution)/shard_map/ppermute | solution.py:291
  16.3 1.6 %shard_map.47.previous = bf16[4,576,768]{2,1,0:T(8,128)(2,1)S(1)} custom-call(bf16[6,96,128]{2,1,0:T(8,128)(2,1)S(1)} %bitcast.12), custom_call_target="tpu_custom_call" | custom-call | tf_op jit(solution)/shard_map/pallas_call | solution.py:341
  17.9 0.0 collective-permute-done.4.source
  17.9 0.0 collective-permute-done.5.source
  17.9 2.2 %shard_map.48 = (bf16[4,576,768]{2,1,0:T(8,128)(2,1)S(1)}, f32[4,576,192]{2,1,0:T(8,128)S(1)}) custom-call(bf16[6,96,128]{2,1,0:T(8,128)(2,1)S(1)} %collective-permute-done.3.source, bf16[6,96,128]{2,1,0:T(8,128)(2,1)S(1)} %shard_map.46.phased, bf16[4,576,768]{2,1,0:T(8,128)(2,1)S(1)} %shard_map.47.previous), custom_call_target="tpu_custom_call" | custom-call | tf_op jit(solution)/shard_map/pallas_call | solution.py:331
  20.1 0.0 collective-permute-done.7.phased
  20.1 2.2 %shard_map.49 = (bf16[4,576,768]{2,1,0:T(8,128)(2,1)S(1)}, f32[4,576,192]{2,1,0:T(8,128)S(1)}) custom-call(bf16[6,96,128]{2,1,0:T(8,128)(2,1)S(1)} %collective-permute-done.4.source, bf16[6,96,128]{2,1,0:T(8,128)(2,1)S(1)} %collective-permute-done.7.phased, bf16[4,576,768]{2,1,0:T(8,128)(2,1)S(1)} %get-tuple-element.19.previous, ...), custom_call_target="tpu_custom_call" | custom-call | tf_op jit(solution)/shard_map/pallas_call | solution.py:331
  22.4 0.0 collective-permute-done.6.phased
  22.4 2.2 %shard_map.50 = (bf16[4,576,768]{2,1,0:T(8,128)(2,1)S(1)}, f32[4,576,192]{2,1,0:T(8,128)S(1)}) custom-call(bf16[6,96,128]{2,1,0:T(8,128)(2,1)S(1)} %collective-permute-done.5.source, bf16[6,96,128]{2,1,0:T(8,128)(2,1)S(1)} %collective-permute-done.6.phased, bf16[4,576,768]{2,1,0:T(8,128)(2,1)S(1)} %get-tuple-element.21.previous, ...), custom_call_target="tpu_custom_call" | custom-call | tf_op jit(solution)/shard_map/pallas_call | solution.py:331
  24.6 0.0 collective-permute-done.2.phased
  24.6 1.3 %shard_map.51 = (bf16[192,1152]{1,0:T(8,128)(2,1)S(1)}, f32[192,1152]{1,0:T(8,128)S(1)}) custom-call(bf16[6,96,128]{2,1,0:T(8,128)(2,1)S(1)} %collective-permute-done.2.phased, bf16[4,576,768]{2,1,0:T(8,128)(2,1)S(1)} %get-tuple-element.23.crossed, f32[4,576,192]{2,1,0:T(8,128)S(1)} %get-tuple-element.24.sums), custom_call_target="tpu_custom_call" | custom-call | tf_op jit(solution)/shard_map/pallas_call | solution.py:353
  26.0 2.4 %collective-permute-start.8 = (bf16[192,1152]{1,0:T(8,128)(2,1)S(1)}, bf16[192,1152]{1,0:T(8,128)(2,1)S(1)}, u32[]{:S(2)}, u32[]{:S(2)}) collective-permute-start(bf16[192,1152]{1,0:T(8,128)(2,1)S(1)} %get-tuple-element.26), channel_id=1, source_target_pairs={{0,1},{1,0},{2,3},{3,2},{4,5},{5,4},{6,7},{7,6},{8,9},{9,8},{10,11... | collective-permute-start | bytes 1327112 | tf_op jit(solution)/shard_map/ppermute | solution.py:364
  28.3 1.4 %collective-permute-done.8.received = bf16[192,1152]{1,0:T(8,128)(2,1)S(1)} collective-permute-done((bf16[192,1152]{1,0:T(8,128)(2,1)S(1)}, bf16[192,1152]{1,0:T(8,128)(2,1)S(1)}, u32[]{:S(2)}, u32[]{:S(2)}) %collective-permute-start.8) | collective-permute-done | bytes 442400 | tf_op jit(solution)/shard_map/ppermute | solution.py:364
  29.8 0.3 shard_map.52
  30.1 26.2 %all_to_all.5.parts = bf16[32,56,128]{2,1,0:T(8,128)(2,1)S(1)} all-to-all(bf16[32,56,128]{2,1,0:T(8,128)(2,1)S(1)} %shard_map.52), channel_id=1, replica_groups=mesh['x'=4,'zl'=2,'y'=4,'zh'=4,'c'=2] {'x','zl','zh'}, dimensions={0} | all-to-all | bytes 917504 | tf_op jit(solution)/shard_map/all_to_all | solution.py:373
  56.3 0.9 %shard_map.53 = f32[3,8,2,1152]{3,2,1,0:T(2,128)} custom-call(bf16[32,56,128]{2,1,0:T(8,128)(2,1)S(1)} %all_to_all.5.parts), custom_call_target="tpu_custom_call" | custom-call | tf_op jit(solution)/shard_map/pallas_call | solution.py:374
  (1 shorter events, 0.0 us)
Async XLA Ops:
  1.9 8.7 %collective-permute-start = (bf16[640,128]{1,0:T(8,128)(2,1)S(1)}, bf16[640,128]{1,0:T(8,128)(2,1)S(1)}, u32[]{:S(2)}, u32[]{:S(2)}) collective-permute-start(bf16[640,128]{1,0:T(8,128)(2,1)S(1)} %maximum_maximum_fusion.own), channel_id=1, source_target_pairs={{0,1},{1,0},{2,3},{3,2},{4,5},{5,4},{6,7},{7,6},{8,9},{9,8},{10,11... | collective-permute-start | bytes 491528 | tf_op jit(solution)/shard_map/ppermute | solution.py:307
  2.0 8.6 %collective-permute-start.1 = (bf16[640,128]{1,0:T(8,128)(2,1)S(1)}, bf16[640,128]{1,0:T(8,128)(2,1)S(1)}, u32[]{:S(2)}, u32[]{:S(2)}) collective-permute-start(bf16[640,128]{1,0:T(8,128)(2,1)S(1)} %maximum_maximum_fusion.own), channel_id=1, source_target_pairs={{0,31},{1,2},{2,1},{3,4},{4,3},{5,6},{6,5},{7,8},{8,7},{9,10},{10,... | collective-permute-start | bytes 491528 | tf_op jit(solution)/shard_map/ppermute | solution.py:306
  5.4 9.0 %collective-permute-start.3 = (bf16[6,96,128]{2,1,0:T(8,128)(2,1)S(1)}, bf16[6,96,128]{2,1,0:T(8,128)(2,1)S(1)}, u32[]{:S(2)}, u32[]{:S(2)}) collective-permute-start(bf16[6,96,128]{2,1,0:T(8,128)(2,1)S(1)} %bitcast.9), channel_id=1, source_target_pairs={{0,8},{8,16},{16,24},{24,0},{1,9},{9,17},{17,25},{25,1},{2,10},{10... | collective-permute-start | bytes 442376 | tf_op jit(solution)/shard_map/ppermute | solution.py:291
  5.6 12.3 %collective-permute-start.4 = (bf16[6,96,128]{2,1,0:T(8,128)(2,1)S(1)}, bf16[6,96,128]{2,1,0:T(8,128)(2,1)S(1)}, u32[]{:S(2)}, u32[]{:S(2)}) collective-permute-start(bf16[6,96,128]{2,1,0:T(8,128)(2,1)S(1)} %bitcast.10), channel_id=1, source_target_pairs={{0,24},{8,0},{16,8},{24,16},{1,25},{9,1},{17,9},{25,17},{2,26},{10... | collective-permute-start | bytes 442376 | tf_op jit(solution)/shard_map/ppermute | solution.py:291
  8.7 9.1 %collective-permute-start.5 = (bf16[6,96,128]{2,1,0:T(8,128)(2,1)S(1)}, bf16[6,96,128]{2,1,0:T(8,128)(2,1)S(1)}, u32[]{:S(2)}, u32[]{:S(2)}) collective-permute-start(bf16[6,96,128]{2,1,0:T(8,128)(2,1)S(1)} %bitcast.11), channel_id=1, source_target_pairs={{0,16},{8,24},{16,0},{24,8},{1,17},{9,25},{17,1},{25,9},{2,18},{10... | collective-permute-start | bytes 442376 | tf_op jit(solution)/shard_map/ppermute | solution.py:291
  11.1 9.0 %collective-permute-start.7 = (bf16[6,96,128]{2,1,0:T(8,128)(2,1)S(1)}, bf16[6,96,128]{2,1,0:T(8,128)(2,1)S(1)}, u32[]{:S(2)}, u32[]{:S(2)}) collective-permute-start(bf16[6,96,128]{2,1,0:T(8,128)(2,1)S(1)} %shard_map.46.phased), channel_id=1, source_target_pairs={{0,8},{8,16},{16,24},{24,0},{1,9},{9,17},{17,25},{25,1},{2,10},{10... | collective-permute-start | bytes 442376 | tf_op jit(solution)/shard_map/ppermute | solution.py:291
  11.9 10.5 %collective-permute-start.6 = (bf16[6,96,128]{2,1,0:T(8,128)(2,1)S(1)}, bf16[6,96,128]{2,1,0:T(8,128)(2,1)S(1)}, u32[]{:S(2)}, u32[]{:S(2)}) collective-permute-start(bf16[6,96,128]{2,1,0:T(8,128)(2,1)S(1)} %shard_map.46.phased), channel_id=1, source_target_pairs={{0,24},{8,0},{16,8},{24,16},{1,25},{9,1},{17,9},{25,17},{2,26},{10... | collective-permute-start | bytes 442376 | tf_op jit(solution)/shard_map/ppermute | solution.py:291
  14.5 10.2 %collective-permute-start.2 = (bf16[6,96,128]{2,1,0:T(8,128)(2,1)S(1)}, bf16[6,96,128]{2,1,0:T(8,128)(2,1)S(1)}, u32[]{:S(2)}, u32[]{:S(2)}) collective-permute-start(bf16[6,96,128]{2,1,0:T(8,128)(2,1)S(1)} %shard_map.46.phased), channel_id=1, source_target_pairs={{0,16},{8,24},{16,0},{24,8},{1,17},{9,25},{17,1},{25,9},{2,18},{10... | collective-permute-start | bytes 442376 | tf_op jit(solution)/shard_map/ppermute | solution.py:291
  26.0 3.8 %collective-permute-start.8 = (bf16[192,1152]{1,0:T(8,128)(2,1)S(1)}, bf16[192,1152]{1,0:T(8,128)(2,1)S(1)}, u32[]{:S(2)}, u32[]{:S(2)}) collective-permute-start(bf16[192,1152]{1,0:T(8,128)(2,1)S(1)} %get-tuple-element.26), channel_id=1, source_target_pairs={{0,1},{1,0},{2,3},{3,2},{4,5},{5,4},{6,7},{7,6},{8,9},{9,8},{10,11... | collective-permute-start | bytes 1327112 | tf_op jit(solution)/shard_map/ppermute | solution.py:364
where the time goes:
time: 58.1 us; the launch traced here: 57.2 us
  blocking collectives  26.2 us (45%)
  starting transfers between devices  14.8 us (25%)
  Pallas kernels  11.4 us (20%)
  local copies, waits for them, and re-layouts  1.75 us (3%)
  waiting for transfers between devices  1.44 us (2%)
  other arithmetic  0.88 us (2%)
  between operations  0.77 us (1%)
    all_to_all x1, blocking collectives, on_device(): packed = lax.all_to_all(packed, ('x', 'zl', 'zh'), 0, 0, tiled=True)  26.2 us
    ppermute x6, starting transfers between devices, from_y(): return lax.ppermute(block, 'y', [(i, (i + by) % 4) for i in range(4)])  8.95 us
    pallas_call x3, Pallas kernels, both(): pl.pallas_call(both_kernel, out_shape=(crossed_shape, sums_shape), in_spe...  6.7 us
    ppermute x1, starting transfers between devices, on_device(): outer = lax.ppermute(joined, AXES, ring_pairs(outer_plane))  3.39 us
    ppermute x1, starting transfers between devices, on_device(): received = lax.ppermute(sent, 'c', swap)  2.38 us
    pallas_call x1, Pallas kernels, on_device(): pl.pallas_call(crossed_kernel, out_shape=crossed_shape, in_specs=[vmem()]...  1.6 us
    ppermute x1, waiting for transfers between devices, on_device(): received = lax.ppermute(sent, 'c', swap)  1.42 us
    pallas_call x1, Pallas kernels, on_device(): pl.pallas_call(last_kernel, out_shape=(jax.ShapeDtypeStruct((192, 1152),...  1.33 us
  transfers between devices with their start and end apart: 9, of which 1 were waited for; matrix products, arithmetic and copies ran while one was open for 1% of the time, Pallas kernels for 15%

commit v1 on v0

--- a/solution.py
+++ b/solution.py
@@ -36,7 +36,7 @@
     return (s + 1) % 32 if s % 2 == 1 else (s - 1) % 32
 
 
-def phased_kernel(numbers, own, other, outer, out, field, ahead, behind):
+def phased_kernel(numbers, own, outer, other, out, field, ahead, behind):
     links = own[6 * NEV :, :].astype(jnp.float32)
     direction = numbers[3]
     core = lax.axis_index("c")
@@ -303,8 +303,8 @@
             jnp.zeros((10, SITES), bf16),
         ]
     )
+    other = lax.ppermute(joined, "c", swap)
     outer = lax.ppermute(joined, AXES, ring_pairs(outer_plane))
-    other = lax.ppermute(joined, "c", swap)
     before = from_y(own, 1)
     after = from_y(own, 3)
     opposite = from_y(own, 2)
@@ -315,7 +315,7 @@
         out_specs=vmem(),
         scratch_shapes=[pltpu.VMEM((6, NEV, SITES), f32)] * 3,
         compiler_params=params(8),
-    )(jnp.concatenate([momentum, direction]), joined, other, outer)
+    )(jnp.concatenate([momentum, direction]), joined, outer, other)
     phased_before = from_y(phased, 1)
     phased_after = from_y(phased, 3)
     phased_opposite = from_y(phased, 2)

time: 58.1 us -> 58.3 us (level); the launches traced: 57.2 us -> 58.1 us
  starting transfers between devices: 14.8 us -> 16.1 us
  blocking collectives: 26.2 us -> 25.1 us
  waiting for transfers between devices: 1.44 us -> 2.1 us
    ppermute x1, starting transfers between devices: 0.09 us -> 4.67 us  [on_device(): other = lax.ppermute(joined, 'c', swap)]
    ppermute x1, starting transfers between devices: 2.38 us -> 0.09 us  [on_device(): received = lax.ppermute(sent, 'c', swap)]
    ppermute x1, starting transfers between devices: 3.39 us -> 1.92 us  [on_device(): outer = lax.ppermute(joined, AXES, ring_pairs(outer_plane))]
    all_to_all x1, blocking collectives: 26.2 us -> 25.1 us  [on_device(): packed = lax.all_to_all(packed, ('x', 'zl', 'zh'), 0, 0, tiled=True)]
  transfers between devices with their start and end apart: 9 -> 9, of which waited for: 1 -> 2; matrix products, arithmetic and copies ran while one was open for 1% -> 1% of each run, Pallas kernels for 15% -> 15%
where the time goes in v1:
time: 58.3 us; the launch traced here: 58.1 us
  blocking collectives  25.1 us (43%)
  starting transfers between devices  16.1 us (28%)
  Pallas kernels  11.4 us (20%)
  waiting for transfers between devices  2.1 us (4%)
  local copies, waits for them, and re-layouts  1.75 us (3%)
  other arithmetic  0.88 us (2%)
  between operations  0.76 us (1%)
    all_to_all x1, blocking collectives, on_device(): packed = lax.all_to_all(packed, ('x', 'zl', 'zh'), 0, 0, tiled=True)  25.1 us
    ppermute x6, starting transfers between devices, from_y(): return lax.ppermute(block, 'y', [(i, (i + by) % 4) for i in range(4)])  9.43 us
    pallas_call x3, Pallas kernels, both(): pl.pallas_call(both_kernel, out_shape=(crossed_shape, sums_shape), in_spe...  6.69 us
    ppermute x1, starting transfers between devices, on_device(): other = lax.ppermute(joined, 'c', swap)  4.67 us
    ppermute x1, starting transfers between devices, on_device(): outer = lax.ppermute(joined, AXES, ring_pairs(outer_plane))  1.92 us
    ppermute x1, waiting for transfers between devices, on_device(): received = lax.ppermute(sent, 'c', swap)  1.78 us
    pallas_call x1, Pallas kernels, on_device(): pl.pallas_call(crossed_kernel, out_shape=crossed_shape, in_specs=[vmem()]...  1.6 us
    pallas_call x1, Pallas kernels, on_device(): pl.pallas_call(last_kernel, out_shape=(jax.ShapeDtypeStruct((192, 1152),...  1.33 us
  transfers between devices with their start and end apart: 9, of which 2 were waited for; matrix products, arithmetic and copies ran while one was open for 1% of the time, Pallas kernels for 15%

profile of v1, /device:TPU:64, one launch (start us, length us, event | category | flops | bytes accessed | tf_op | source)
XLA Modules:
  0.0 58.1 jit_solution(6316853668039051248)
XLA Ops:
  0.0 0.9 %copy.5 = bf16[2,3,96,128]{3,2,1,0:T(8,128)(2,1)S(1)} copy(bf16[2,3,96,128]{3,0,1,2:T(2,128)(2,1)} %bitcast.13) | data formatting | bytes 294912 | tf_op jit(solution)/shard_map/transpose | solution.py:298
  0.9 0.7 %reshape.6 = bf16[54,128]{1,0:T(8,128)(2,1)S(1)} reshape(bf16[3,3,3,2,128]{4,3,2,1,0:T(2,128)(2,1)} %bitcast.14) | data formatting | bytes 27648 | tf_op jit(solution)/shard_map/reshape | solution.py:302
  1.7 0.1 pad.2.clone
  1.8 0.2 maximum_maximum_fusion.own
  1.9 1.9 %collective-permute-start = (bf16[640,128]{1,0:T(8,128)(2,1)S(1)}, bf16[640,128]{1,0:T(8,128)(2,1)S(1)}, u32[]{:S(2)}, u32[]{:S(2)}) collective-permute-start(bf16[640,128]{1,0:T(8,128)(2,1)S(1)} %maximum_maximum_fusion.own), channel_id=1, source_target_pairs={{0,31},{1,2},{2,1},{3,4},{4,3},{5,6},{6,5},{7,8},{8,7},{9,10},{10,... | collective-permute-start | bytes 491528 | tf_op jit(solution)/shard_map/ppermute | solution.py:307
  3.8 4.7 %collective-permute-start.1 = (bf16[640,128]{1,0:T(8,128)(2,1)S(1)}, bf16[640,128]{1,0:T(8,128)(2,1)S(1)}, u32[]{:S(2)}, u32[]{:S(2)}) collective-permute-start(bf16[640,128]{1,0:T(8,128)(2,1)S(1)} %maximum_maximum_fusion.own), channel_id=1, source_target_pairs={{0,1},{1,0},{2,3},{3,2},{4,5},{5,4},{6,7},{7,6},{8,9},{9,8},{10,11... | collective-permute-start | bytes 491528 | tf_op jit(solution)/shard_map/ppermute | solution.py:306
  8.5 1.6 %collective-permute-start.3 = (bf16[6,96,128]{2,1,0:T(8,128)(2,1)S(1)}, bf16[6,96,128]{2,1,0:T(8,128)(2,1)S(1)}, u32[]{:S(2)}, u32[]{:S(2)}) collective-permute-start(bf16[6,96,128]{2,1,0:T(8,128)(2,1)S(1)} %bitcast.9), channel_id=1, source_target_pairs={{0,8},{8,16},{16,24},{24,0},{1,9},{9,17},{17,25},{25,1},{2,10},{10... | collective-permute-start | bytes 442376 | tf_op jit(solution)/shard_map/ppermute | solution.py:291
  10.1 1.7 %collective-permute-start.4 = (bf16[6,96,128]{2,1,0:T(8,128)(2,1)S(1)}, bf16[6,96,128]{2,1,0:T(8,128)(2,1)S(1)}, u32[]{:S(2)}, u32[]{:S(2)}) collective-permute-start(bf16[6,96,128]{2,1,0:T(8,128)(2,1)S(1)} %bitcast.10), channel_id=1, source_target_pairs={{0,24},{8,0},{16,8},{24,16},{1,25},{9,1},{17,9},{25,17},{2,26},{10... | collective-permute-start | bytes 442376 | tf_op jit(solution)/shard_map/ppermute | solution.py:291
  11.8 2.0 %collective-permute-start.5 = (bf16[6,96,128]{2,1,0:T(8,128)(2,1)S(1)}, bf16[6,96,128]{2,1,0:T(8,128)(2,1)S(1)}, u32[]{:S(2)}, u32[]{:S(2)}) collective-permute-start(bf16[6,96,128]{2,1,0:T(8,128)(2,1)S(1)} %bitcast.11), channel_id=1, source_target_pairs={{0,16},{8,24},{16,0},{24,8},{1,17},{9,25},{17,1},{25,9},{2,18},{10... | collective-permute-start | bytes 442376 | tf_op jit(solution)/shard_map/ppermute | solution.py:291
  14.4 0.7 %pad_add_fusion.numbers = s32[4]{0:T(128)S(1)} fusion(s32[1]{0:T(128)S(6)} %copy.7, s32[3]{0:T(128)} %param.6), kind=kLoop, calls=%fused_computation.1 | loop fusion | flops 4 | bytes 32 | tf_op jit(solution)/shard_map/concatenate | solution.py:318
  15.1 0.0 collective-permute-done.outer
  15.1 0.0 collective-permute-done.1.other
  15.1 0.5 shard_map.46.phased
  15.6 0.8 %collective-permute-start.7 = (bf16[6,96,128]{2,1,0:T(8,128)(2,1)S(1)}, bf16[6,96,128]{2,1,0:T(8,128)(2,1)S(1)}, u32[]{:S(2)}, u32[]{:S(2)}) collective-permute-start(bf16[6,96,128]{2,1,0:T(8,128)(2,1)S(1)} %shard_map.46.phased), channel_id=1, source_target_pairs={{0,8},{8,16},{16,24},{24,0},{1,9},{9,17},{17,25},{25,1},{2,10},{10... | collective-permute-start | bytes 442376 | tf_op jit(solution)/shard_map/ppermute | solution.py:291
  16.4 2.6 %collective-permute-start.6 = (bf16[6,96,128]{2,1,0:T(8,128)(2,1)S(1)}, bf16[6,96,128]{2,1,0:T(8,128)(2,1)S(1)}, u32[]{:S(2)}, u32[]{:S(2)}) collective-permute-start(bf16[6,96,128]{2,1,0:T(8,128)(2,1)S(1)} %shard_map.46.phased), channel_id=1, source_target_pairs={{0,24},{8,0},{16,8},{24,16},{1,25},{9,1},{17,9},{25,17},{2,26},{10... | collective-permute-start | bytes 442376 | tf_op jit(solution)/shard_map/ppermute | solution.py:291
  18.9 0.0 collective-permute-done.3.source
  19.0 0.9 %collective-permute-start.2 = (bf16[6,96,128]{2,1,0:T(8,128)(2,1)S(1)}, bf16[6,96,128]{2,1,0:T(8,128)(2,1)S(1)}, u32[]{:S(2)}, u32[]{:S(2)}) collective-permute-start(bf16[6,96,128]{2,1,0:T(8,128)(2,1)S(1)} %shard_map.46.phased), channel_id=1, source_target_pairs={{0,16},{8,24},{16,0},{24,8},{1,17},{9,25},{17,1},{25,9},{2,18},{10... | collective-permute-start | bytes 442376 | tf_op jit(solution)/shard_map/ppermute | solution.py:291
  19.9 1.6 %shard_map.47.previous = bf16[4,576,768]{2,1,0:T(8,128)(2,1)S(1)} custom-call(bf16[6,96,128]{2,1,0:T(8,128)(2,1)S(1)} %bitcast.12), custom_call_target="tpu_custom_call" | custom-call | tf_op jit(solution)/shard_map/pallas_call | solution.py:341
  21.5 0.0 collective-permute-done.4.source
  21.5 0.0 collective-permute-done.5.source
  21.5 2.2 %shard_map.48 = (bf16[4,576,768]{2,1,0:T(8,128)(2,1)S(1)}, f32[4,576,192]{2,1,0:T(8,128)S(1)}) custom-call(bf16[6,96,128]{2,1,0:T(8,128)(2,1)S(1)} %collective-permute-done.3.source, bf16[6,96,128]{2,1,0:T(8,128)(2,1)S(1)} %shard_map.46.phased, bf16[4,576,768]{2,1,0:T(8,128)(2,1)S(1)} %shard_map.47.previous), custom_call_target="tpu_custom_call" | custom-call | tf_op jit(solution)/shard_map/pallas_call | solution.py:331
  23.7 0.3 collective-permute-done.7.phased
  24.0 2.2 %shard_map.49 = (bf16[4,576,768]{2,1,0:T(8,128)(2,1)S(1)}, f32[4,576,192]{2,1,0:T(8,128)S(1)}) custom-call(bf16[6,96,128]{2,1,0:T(8,128)(2,1)S(1)} %collective-permute-done.4.source, bf16[6,96,128]{2,1,0:T(8,128)(2,1)S(1)} %collective-permute-done.7.phased, bf16[4,576,768]{2,1,0:T(8,128)(2,1)S(1)} %get-tuple-element.19.previous, ...), custom_call_target="tpu_custom_call" | custom-call | tf_op jit(solution)/shard_map/pallas_call | solution.py:331
  26.2 0.0 collective-permute-done.6.phased
  26.2 2.2 %shard_map.50 = (bf16[4,576,768]{2,1,0:T(8,128)(2,1)S(1)}, f32[4,576,192]{2,1,0:T(8,128)S(1)}) custom-call(bf16[6,96,128]{2,1,0:T(8,128)(2,1)S(1)} %collective-permute-done.5.source, bf16[6,96,128]{2,1,0:T(8,128)(2,1)S(1)} %collective-permute-done.6.phased, bf16[4,576,768]{2,1,0:T(8,128)(2,1)S(1)} %get-tuple-element.21.previous, ...), custom_call_target="tpu_custom_call" | custom-call | tf_op jit(solution)/shard_map/pallas_call | solution.py:331
  28.5 0.0 collective-permute-done.2.phased
  28.5 1.3 %shard_map.51 = (bf16[192,1152]{1,0:T(8,128)(2,1)S(1)}, f32[192,1152]{1,0:T(8,128)S(1)}) custom-call(bf16[6,96,128]{2,1,0:T(8,128)(2,1)S(1)} %collective-permute-done.2.phased, bf16[4,576,768]{2,1,0:T(8,128)(2,1)S(1)} %get-tuple-element.23.crossed, f32[4,576,192]{2,1,0:T(8,128)S(1)} %get-tuple-element.24.sums), custom_call_target="tpu_custom_call" | custom-call | tf_op jit(solution)/shard_map/pallas_call | solution.py:353
  29.8 0.1 collective-permute-start.8
  29.9 1.8 %collective-permute-done.8.received = bf16[192,1152]{1,0:T(8,128)(2,1)S(1)} collective-permute-done((bf16[192,1152]{1,0:T(8,128)(2,1)S(1)}, bf16[192,1152]{1,0:T(8,128)(2,1)S(1)}, u32[]{:S(2)}, u32[]{:S(2)}) %collective-permute-start.8) | collective-permute-done | bytes 442400 | tf_op jit(solution)/shard_map/ppermute | solution.py:364
  31.7 0.3 shard_map.52
  32.1 25.1 %all_to_all.5.parts = bf16[32,56,128]{2,1,0:T(8,128)(2,1)S(1)} all-to-all(bf16[32,56,128]{2,1,0:T(8,128)(2,1)S(1)} %shard_map.52), channel_id=1, replica_groups=mesh['x'=4,'zl'=2,'y'=4,'zh'=4,'c'=2] {'x','zl','zh'}, dimensions={0} | all-to-all | bytes 917504 | tf_op jit(solution)/shard_map/all_to_all | solution.py:373
  57.2 0.9 %shard_map.53 = f32[3,8,2,1152]{3,2,1,0:T(2,128)} custom-call(bf16[32,56,128]{2,1,0:T(8,128)(2,1)S(1)} %all_to_all.5.parts), custom_call_target="tpu_custom_call" | custom-call | tf_op jit(solution)/shard_map/pallas_call | solution.py:374
  (1 shorter events, 0.0 us)
Async XLA Ops:
  1.9 13.2 %collective-permute-start = (bf16[640,128]{1,0:T(8,128)(2,1)S(1)}, bf16[640,128]{1,0:T(8,128)(2,1)S(1)}, u32[]{:S(2)}, u32[]{:S(2)}) collective-permute-start(bf16[640,128]{1,0:T(8,128)(2,1)S(1)} %maximum_maximum_fusion.own), channel_id=1, source_target_pairs={{0,31},{1,2},{2,1},{3,4},{4,3},{5,6},{6,5},{7,8},{8,7},{9,10},{10,... | collective-permute-start | bytes 491528 | tf_op jit(solution)/shard_map/ppermute | solution.py:307
  3.8 11.3 %collective-permute-start.1 = (bf16[640,128]{1,0:T(8,128)(2,1)S(1)}, bf16[640,128]{1,0:T(8,128)(2,1)S(1)}, u32[]{:S(2)}, u32[]{:S(2)}) collective-permute-start(bf16[640,128]{1,0:T(8,128)(2,1)S(1)} %maximum_maximum_fusion.own), channel_id=1, source_target_pairs={{0,1},{1,0},{2,3},{3,2},{4,5},{5,4},{6,7},{7,6},{8,9},{9,8},{10,11... | collective-permute-start | bytes 491528 | tf_op jit(solution)/shard_map/ppermute | solution.py:306
  8.5 10.4 %collective-permute-start.3 = (bf16[6,96,128]{2,1,0:T(8,128)(2,1)S(1)}, bf16[6,96,128]{2,1,0:T(8,128)(2,1)S(1)}, u32[]{:S(2)}, u32[]{:S(2)}) collective-permute-start(bf16[6,96,128]{2,1,0:T(8,128)(2,1)S(1)} %bitcast.9), channel_id=1, source_target_pairs={{0,8},{8,16},{16,24},{24,0},{1,9},{9,17},{17,25},{25,1},{2,10},{10... | collective-permute-start | bytes 442376 | tf_op jit(solution)/shard_map/ppermute | solution.py:291
  10.1 11.4 %collective-permute-start.4 = (bf16[6,96,128]{2,1,0:T(8,128)(2,1)S(1)}, bf16[6,96,128]{2,1,0:T(8,128)(2,1)S(1)}, u32[]{:S(2)}, u32[]{:S(2)}) collective-permute-start(bf16[6,96,128]{2,1,0:T(8,128)(2,1)S(1)} %bitcast.10), channel_id=1, source_target_pairs={{0,24},{8,0},{16,8},{24,16},{1,25},{9,1},{17,9},{25,17},{2,26},{10... | collective-permute-start | bytes 442376 | tf_op jit(solution)/shard_map/ppermute | solution.py:291
  11.8 9.7 %collective-permute-start.5 = (bf16[6,96,128]{2,1,0:T(8,128)(2,1)S(1)}, bf16[6,96,128]{2,1,0:T(8,128)(2,1)S(1)}, u32[]{:S(2)}, u32[]{:S(2)}) collective-permute-start(bf16[6,96,128]{2,1,0:T(8,128)(2,1)S(1)} %bitcast.11), channel_id=1, source_target_pairs={{0,16},{8,24},{16,0},{24,8},{1,17},{9,25},{17,1},{25,9},{2,18},{10... | collective-permute-start | bytes 442376 | tf_op jit(solution)/shard_map/ppermute | solution.py:291
  15.6 8.4 %collective-permute-start.7 = (bf16[6,96,128]{2,1,0:T(8,128)(2,1)S(1)}, bf16[6,96,128]{2,1,0:T(8,128)(2,1)S(1)}, u32[]{:S(2)}, u32[]{:S(2)}) collective-permute-start(bf16[6,96,128]{2,1,0:T(8,128)(2,1)S(1)} %shard_map.46.phased), channel_id=1, source_target_pairs={{0,8},{8,16},{16,24},{24,0},{1,9},{9,17},{17,25},{25,1},{2,10},{10... | collective-permute-start | bytes 442376 | tf_op jit(solution)/shard_map/ppermute | solution.py:291
  16.4 9.9 %collective-permute-start.6 = (bf16[6,96,128]{2,1,0:T(8,128)(2,1)S(1)}, bf16[6,96,128]{2,1,0:T(8,128)(2,1)S(1)}, u32[]{:S(2)}, u32[]{:S(2)}) collective-permute-start(bf16[6,96,128]{2,1,0:T(8,128)(2,1)S(1)} %shard_map.46.phased), channel_id=1, source_target_pairs={{0,24},{8,0},{16,8},{24,16},{1,25},{9,1},{17,9},{25,17},{2,26},{10... | collective-permute-start | bytes 442376 | tf_op jit(solution)/shard_map/ppermute | solution.py:291
  19.0 9.5 %collective-permute-start.2 = (bf16[6,96,128]{2,1,0:T(8,128)(2,1)S(1)}, bf16[6,96,128]{2,1,0:T(8,128)(2,1)S(1)}, u32[]{:S(2)}, u32[]{:S(2)}) collective-permute-start(bf16[6,96,128]{2,1,0:T(8,128)(2,1)S(1)} %shard_map.46.phased), channel_id=1, source_target_pairs={{0,16},{8,24},{16,0},{24,8},{1,17},{9,25},{17,1},{25,9},{2,18},{10... | collective-permute-start | bytes 442376 | tf_op jit(solution)/shard_map/ppermute | solution.py:291
  29.8 1.9 %collective-permute-start.8 = (bf16[192,1152]{1,0:T(8,128)(2,1)S(1)}, bf16[192,1152]{1,0:T(8,128)(2,1)S(1)}, u32[]{:S(2)}, u32[]{:S(2)}) collective-permute-start(bf16[192,1152]{1,0:T(8,128)(2,1)S(1)} %get-tuple-element.26), channel_id=1, source_target_pairs={{0,1},{1,0},{2,3},{3,2},{4,5},{5,4},{6,7},{7,6},{8,9},{9,8},{10,11... | collective-permute-start | bytes 1327112 | tf_op jit(solution)/shard_map/ppermute | solution.py:364

commit v2 on v1

--- a/solution.py
+++ b/solution.py
@@ -307,7 +307,6 @@
     outer = lax.ppermute(joined, AXES, ring_pairs(outer_plane))
     before = from_y(own, 1)
     after = from_y(own, 3)
-    opposite = from_y(own, 2)
     phased = pl.pallas_call(
         phased_kernel,
         out_shape=jax.ShapeDtypeStruct((6, NEV, SITES), bf16),
@@ -319,7 +318,8 @@
     phased_before = from_y(phased, 1)
     phased_after = from_y(phased, 3)
     phased_opposite = from_y(phased, 2)
-    before, after, opposite = lax.optimization_barrier((before, after, opposite))
+    opposite = from_y(after, 3)
+    before, after = lax.optimization_barrier((before, after))
 
     crossed_shape = jax.ShapeDtypeStruct((4, 576, DEPTH), bf16)
     sums_shape = jax.ShapeDtypeStruct((4, 576, 192), f32)

time: 58.3 us -> 60 us (1.029)
  the two profiles are of different devices: /device:TPU:64 before, /device:TPU:24 now
where the time goes in v2:
time: 60 us; the launch traced here: 59.8 us
  blocking collectives  22.8 us (38%)
  starting transfers between devices  17.4 us (29%)
  Pallas kernels  11.4 us (19%)
  waiting for transfers between devices  4.8 us (8%)
  local copies, waits for them, and re-layouts  1.75 us (3%)
  other arithmetic  0.88 us (1%)
  between operations  0.77 us (1%)
    all_to_all x1, blocking collectives, on_device(): packed = lax.all_to_all(packed, ('x', 'zl', 'zh'), 0, 0, tiled=True)  22.8 us
    ppermute x6, starting transfers between devices, from_y(): return lax.ppermute(block, 'y', [(i, (i + by) % 4) for i in range(4)])  9.37 us
    ppermute x1, starting transfers between devices, on_device(): outer = lax.ppermute(joined, AXES, ring_pairs(outer_plane))  7.83 us
    pallas_call x3, Pallas kernels, both(): pl.pallas_call(both_kernel, out_shape=(crossed_shape, sums_shape), in_spe...  6.73 us
    ppermute x6, waiting for transfers between devices, from_y(): return lax.ppermute(block, 'y', [(i, (i + by) % 4) for i in range(4)])  3.01 us
    ppermute x1, waiting for transfers between devices, on_device(): received = lax.ppermute(sent, 'c', swap)  1.78 us
    pallas_call x1, Pallas kernels, on_device(): pl.pallas_call(crossed_kernel, out_shape=crossed_shape, in_specs=[vmem()]...  1.6 us
    pallas_call x1, Pallas kernels, on_device(): pl.pallas_call(last_kernel, out_shape=(jax.ShapeDtypeStruct((192, 1152),...  1.33 us
  transfers between devices with their start and end apart: 9, of which 3 were waited for; matrix products, arithmetic and copies ran while one was open for 1% of the time, Pallas kernels for 15%

profile of v2, /device:TPU:24, one launch (start us, length us, event | category | flops | bytes accessed | tf_op | source)
XLA Modules:
  0.0 59.8 jit_solution(10512096795852934883)
XLA Ops:
  0.0 0.9 %copy.5 = bf16[2,3,96,128]{3,2,1,0:T(8,128)(2,1)S(1)} copy(bf16[2,3,96,128]{3,0,1,2:T(2,128)(2,1)} %bitcast.12) | data formatting | bytes 294912 | tf_op jit(solution)/shard_map/transpose | solution.py:298
  0.9 0.7 %reshape.6 = bf16[54,128]{1,0:T(8,128)(2,1)S(1)} reshape(bf16[3,3,3,2,128]{4,3,2,1,0:T(2,128)(2,1)} %bitcast.13) | data formatting | bytes 27648 | tf_op jit(solution)/shard_map/reshape | solution.py:302
  1.7 0.1 pad.2.clone
  1.8 0.2 maximum_maximum_fusion.own
  1.9 7.8 %collective-permute-start = (bf16[640,128]{1,0:T(8,128)(2,1)S(1)}, bf16[640,128]{1,0:T(8,128)(2,1)S(1)}, u32[]{:S(2)}, u32[]{:S(2)}) collective-permute-start(bf16[640,128]{1,0:T(8,128)(2,1)S(1)} %maximum_maximum_fusion.own), channel_id=1, source_target_pairs={{0,31},{1,2},{2,1},{3,4},{4,3},{5,6},{6,5},{7,8},{8,7},{9,10},{10,... | collective-permute-start | bytes 491528 | tf_op jit(solution)/shard_map/ppermute | solution.py:307
  9.8 0.1 collective-permute-start.1
  9.9 0.5 collective-permute-start.3
  10.4 2.8 %collective-permute-start.6 = (bf16[6,96,128]{2,1,0:T(8,128)(2,1)S(1)}, bf16[6,96,128]{2,1,0:T(8,128)(2,1)S(1)}, u32[]{:S(2)}, u32[]{:S(2)}) collective-permute-start(bf16[6,96,128]{2,1,0:T(8,128)(2,1)S(1)} %bitcast.10), channel_id=1, source_target_pairs={{0,8},{8,16},{16,24},{24,0},{1,9},{9,17},{17,25},{25,1},{2,10},{10... | collective-permute-start | bytes 442376 | tf_op jit(solution)/shard_map/ppermute | solution.py:291
  13.8 0.7 %pad_add_fusion.numbers = s32[4]{0:T(128)S(1)} fusion(s32[1]{0:T(128)S(6)} %copy.7, s32[3]{0:T(128)} %param.6), kind=kLoop, calls=%fused_computation.1 | loop fusion | flops 4 | bytes 32 | tf_op jit(solution)/shard_map/concatenate | solution.py:317
  14.6 0.0 collective-permute-done.outer
  14.6 0.0 collective-permute-done.1.other
  14.6 0.5 shard_map.46.phased
  15.1 1.4 %collective-permute-start.7 = (bf16[6,96,128]{2,1,0:T(8,128)(2,1)S(1)}, bf16[6,96,128]{2,1,0:T(8,128)(2,1)S(1)}, u32[]{:S(2)}, u32[]{:S(2)}) collective-permute-start(bf16[6,96,128]{2,1,0:T(8,128)(2,1)S(1)} %shard_map.46.phased), channel_id=1, source_target_pairs={{0,8},{8,16},{16,24},{24,0},{1,9},{9,17},{17,25},{25,1},{2,10},{10... | collective-permute-start | bytes 442376 | tf_op jit(solution)/shard_map/ppermute | solution.py:291
  16.4 0.9 %collective-permute-done.3.source = bf16[6,96,128]{2,1,0:T(8,128)(2,1)S(1)} collective-permute-done((bf16[6,96,128]{2,1,0:T(8,128)(2,1)S(1)}, bf16[6,96,128]{2,1,0:T(8,128)(2,1)S(1)}, u32[]{:S(2)}, u32[]{:S(2)}) %collective-permute-start.3) | collective-permute-done | bytes 147488 | tf_op jit(solution)/shard_map/ppermute | solution.py:291
  17.3 0.0 collective-permute-start.4
  17.3 0.2 collective-permute-start.5
  17.6 4.5 %collective-permute-start.2 = (bf16[6,96,128]{2,1,0:T(8,128)(2,1)S(1)}, bf16[6,96,128]{2,1,0:T(8,128)(2,1)S(1)}, u32[]{:S(2)}, u32[]{:S(2)}) collective-permute-start(bf16[6,96,128]{2,1,0:T(8,128)(2,1)S(1)} %shard_map.46.phased), channel_id=1, source_target_pairs={{0,16},{8,24},{16,0},{24,8},{1,17},{9,25},{17,1},{25,9},{2,18},{10... | collective-permute-start | bytes 442376 | tf_op jit(solution)/shard_map/ppermute | solution.py:291
  22.0 1.6 %shard_map.47.previous = bf16[4,576,768]{2,1,0:T(8,128)(2,1)S(1)} custom-call(bf16[6,96,128]{2,1,0:T(8,128)(2,1)S(1)} %bitcast.11), custom_call_target="tpu_custom_call" | custom-call | tf_op jit(solution)/shard_map/pallas_call | solution.py:341
  23.6 0.0 collective-permute-done.6.source
  23.6 2.2 %shard_map.48 = (bf16[4,576,768]{2,1,0:T(8,128)(2,1)S(1)}, f32[4,576,192]{2,1,0:T(8,128)S(1)}) custom-call(bf16[6,96,128]{2,1,0:T(8,128)(2,1)S(1)} %collective-permute-done.6.source, bf16[6,96,128]{2,1,0:T(8,128)(2,1)S(1)} %shard_map.46.phased, bf16[4,576,768]{2,1,0:T(8,128)(2,1)S(1)} %shard_map.47.previous), custom_call_target="tpu_custom_call" | custom-call | tf_op jit(solution)/shard_map/pallas_call | solution.py:331
  25.9 0.0 collective-permute-done.7.phased
  25.9 2.2 %shard_map.49 = (bf16[4,576,768]{2,1,0:T(8,128)(2,1)S(1)}, f32[4,576,192]{2,1,0:T(8,128)S(1)}) custom-call(bf16[6,96,128]{2,1,0:T(8,128)(2,1)S(1)} %collective-permute-done.3.source, bf16[6,96,128]{2,1,0:T(8,128)(2,1)S(1)} %collective-permute-done.7.phased, bf16[4,576,768]{2,1,0:T(8,128)(2,1)S(1)} %get-tuple-element.17.previous, ...), custom_call_target="tpu_custom_call" | custom-call | tf_op jit(solution)/shard_map/pallas_call | solution.py:331
  28.2 0.0 collective-permute-done.4.source
  28.2 2.1 %collective-permute-done.5.phased = bf16[6,96,128]{2,1,0:T(8,128)(2,1)S(1)} collective-permute-done((bf16[6,96,128]{2,1,0:T(8,128)(2,1)S(1)}, bf16[6,96,128]{2,1,0:T(8,128)(2,1)S(1)}, u32[]{:S(2)}, u32[]{:S(2)}) %collective-permute-start.5) | collective-permute-done | bytes 147488 | tf_op jit(solution)/shard_map/ppermute | solution.py:291
  30.3 2.2 %shard_map.50 = (bf16[4,576,768]{2,1,0:T(8,128)(2,1)S(1)}, f32[4,576,192]{2,1,0:T(8,128)S(1)}) custom-call(bf16[6,96,128]{2,1,0:T(8,128)(2,1)S(1)} %collective-permute-done.4.source, bf16[6,96,128]{2,1,0:T(8,128)(2,1)S(1)} %collective-permute-done.5.phased, bf16[4,576,768]{2,1,0:T(8,128)(2,1)S(1)} %get-tuple-element.19.previous, ...), custom_call_target="tpu_custom_call" | custom-call | tf_op jit(solution)/shard_map/pallas_call | solution.py:331
  32.5 0.0 collective-permute-done.2.phased
  32.5 1.3 %shard_map.51 = (bf16[192,1152]{1,0:T(8,128)(2,1)S(1)}, f32[192,1152]{1,0:T(8,128)S(1)}) custom-call(bf16[6,96,128]{2,1,0:T(8,128)(2,1)S(1)} %collective-permute-done.2.phased, bf16[4,576,768]{2,1,0:T(8,128)(2,1)S(1)} %get-tuple-element.21.crossed, f32[4,576,192]{2,1,0:T(8,128)S(1)} %get-tuple-element.22.sums), custom_call_target="tpu_custom_call" | custom-call | tf_op jit(solution)/shard_map/pallas_call | solution.py:353
  33.9 0.1 collective-permute-start.8
  34.0 1.8 %collective-permute-done.8.received = bf16[192,1152]{1,0:T(8,128)(2,1)S(1)} collective-permute-done((bf16[192,1152]{1,0:T(8,128)(2,1)S(1)}, bf16[192,1152]{1,0:T(8,128)(2,1)S(1)}, u32[]{:S(2)}, u32[]{:S(2)}) %collective-permute-start.8) | collective-permute-done | bytes 442400 | tf_op jit(solution)/shard_map/ppermute | solution.py:364
  35.7 0.3 shard_map.52
  36.1 22.8 %all_to_all.5.parts = bf16[32,56,128]{2,1,0:T(8,128)(2,1)S(1)} all-to-all(bf16[32,56,128]{2,1,0:T(8,128)(2,1)S(1)} %shard_map.52), channel_id=1, replica_groups=mesh['x'=4,'zl'=2,'y'=4,'zh'=4,'c'=2] {'x','zl','zh'}, dimensions={0} | all-to-all | bytes 917504 | tf_op jit(solution)/shard_map/all_to_all | solution.py:373
  58.9 0.9 %shard_map.53 = f32[3,8,2,1152]{3,2,1,0:T(2,128)} custom-call(bf16[32,56,128]{2,1,0:T(8,128)(2,1)S(1)} %all_to_all.5.parts), custom_call_target="tpu_custom_call" | custom-call | tf_op jit(solution)/shard_map/pallas_call | solution.py:374
  (1 shorter events, 0.0 us)
Async XLA Ops:
  1.9 12.6 %collective-permute-start = (bf16[640,128]{1,0:T(8,128)(2,1)S(1)}, bf16[640,128]{1,0:T(8,128)(2,1)S(1)}, u32[]{:S(2)}, u32[]{:S(2)}) collective-permute-start(bf16[640,128]{1,0:T(8,128)(2,1)S(1)} %maximum_maximum_fusion.own), channel_id=1, source_target_pairs={{0,31},{1,2},{2,1},{3,4},{4,3},{5,6},{6,5},{7,8},{8,7},{9,10},{10,... | collective-permute-start | bytes 491528 | tf_op jit(solution)/shard_map/ppermute | solution.py:307
  9.8 4.8 %collective-permute-start.1 = (bf16[640,128]{1,0:T(8,128)(2,1)S(1)}, bf16[640,128]{1,0:T(8,128)(2,1)S(1)}, u32[]{:S(2)}, u32[]{:S(2)}) collective-permute-start(bf16[640,128]{1,0:T(8,128)(2,1)S(1)} %maximum_maximum_fusion.own), channel_id=1, source_target_pairs={{0,1},{1,0},{2,3},{3,2},{4,5},{5,4},{6,7},{7,6},{8,9},{9,8},{10,11... | collective-permute-start | bytes 491528 | tf_op jit(solution)/shard_map/ppermute | solution.py:306
  9.9 7.5 %collective-permute-start.3 = (bf16[6,96,128]{2,1,0:T(8,128)(2,1)S(1)}, bf16[6,96,128]{2,1,0:T(8,128)(2,1)S(1)}, u32[]{:S(2)}, u32[]{:S(2)}) collective-permute-start(bf16[6,96,128]{2,1,0:T(8,128)(2,1)S(1)} %bitcast.9), channel_id=1, source_target_pairs={{0,24},{8,0},{16,8},{24,16},{1,25},{9,1},{17,9},{25,17},{2,26},{10... | collective-permute-start | bytes 442376 | tf_op jit(solution)/shard_map/ppermute | solution.py:291
  10.4 13.3 %collective-permute-start.6 = (bf16[6,96,128]{2,1,0:T(8,128)(2,1)S(1)}, bf16[6,96,128]{2,1,0:T(8,128)(2,1)S(1)}, u32[]{:S(2)}, u32[]{:S(2)}) collective-permute-start(bf16[6,96,128]{2,1,0:T(8,128)(2,1)S(1)} %bitcast.10), channel_id=1, source_target_pairs={{0,8},{8,16},{16,24},{24,0},{1,9},{9,17},{17,25},{25,1},{2,10},{10... | collective-permute-start | bytes 442376 | tf_op jit(solution)/shard_map/ppermute | solution.py:291
  15.1 10.8 %collective-permute-start.7 = (bf16[6,96,128]{2,1,0:T(8,128)(2,1)S(1)}, bf16[6,96,128]{2,1,0:T(8,128)(2,1)S(1)}, u32[]{:S(2)}, u32[]{:S(2)}) collective-permute-start(bf16[6,96,128]{2,1,0:T(8,128)(2,1)S(1)} %shard_map.46.phased), channel_id=1, source_target_pairs={{0,8},{8,16},{16,24},{24,0},{1,9},{9,17},{17,25},{25,1},{2,10},{10... | collective-permute-start | bytes 442376 | tf_op jit(solution)/shard_map/ppermute | solution.py:291
  17.3 10.8 %collective-permute-start.4 = (bf16[6,96,128]{2,1,0:T(8,128)(2,1)S(1)}, bf16[6,96,128]{2,1,0:T(8,128)(2,1)S(1)}, u32[]{:S(2)}, u32[]{:S(2)}) collective-permute-start(bf16[6,96,128]{2,1,0:T(8,128)(2,1)S(1)} %collective-permute-done.3.source), channel_id=1, source_target_pairs={{0,24},{8,0},{16,8},{24,16},{1,25},{9,1},{17,9},{25,17},{2,26},{10... | collective-permute-start | bytes 442376 | tf_op jit(solution)/shard_map/ppermute | solution.py:291
  17.3 12.9 %collective-permute-start.5 = (bf16[6,96,128]{2,1,0:T(8,128)(2,1)S(1)}, bf16[6,96,128]{2,1,0:T(8,128)(2,1)S(1)}, u32[]{:S(2)}, u32[]{:S(2)}) collective-permute-start(bf16[6,96,128]{2,1,0:T(8,128)(2,1)S(1)} %shard_map.46.phased), channel_id=1, source_target_pairs={{0,24},{8,0},{16,8},{24,16},{1,25},{9,1},{17,9},{25,17},{2,26},{10... | collective-permute-start | bytes 442376 | tf_op jit(solution)/shard_map/ppermute | solution.py:291
  17.6 15.0 %collective-permute-start.2 = (bf16[6,96,128]{2,1,0:T(8,128)(2,1)S(1)}, bf16[6,96,128]{2,1,0:T(8,128)(2,1)S(1)}, u32[]{:S(2)}, u32[]{:S(2)}) collective-permute-start(bf16[6,96,128]{2,1,0:T(8,128)(2,1)S(1)} %shard_map.46.phased), channel_id=1, source_target_pairs={{0,16},{8,24},{16,0},{24,8},{1,17},{9,25},{17,1},{25,9},{2,18},{10... | collective-permute-start | bytes 442376 | tf_op jit(solution)/shard_map/ppermute | solution.py:291
  33.9 1.9 %collective-permute-start.8 = (bf16[192,1152]{1,0:T(8,128)(2,1)S(1)}, bf16[192,1152]{1,0:T(8,128)(2,1)S(1)}, u32[]{:S(2)}, u32[]{:S(2)}) collective-permute-start(bf16[192,1152]{1,0:T(8,128)(2,1)S(1)} %get-tuple-element.24), channel_id=1, source_target_pairs={{0,1},{1,0},{2,3},{3,2},{4,5},{5,4},{6,7},{7,6},{8,9},{9,8},{10,11... | collective-permute-start | bytes 1327112 | tf_op jit(solution)/shard_map/ppermute | solution.py:364

commit v3 on v0

--- a/solution.py
+++ b/solution.py
@@ -38,16 +38,17 @@
 
 def phased_kernel(numbers, own, other, outer, out, field, ahead, behind):
     links = own[6 * NEV :, :].astype(jnp.float32)
-    direction = numbers[3]
+    direction = jnp.bitwise_and(numbers[0], 3)
+    momentum = [lax.shift_right_arithmetic(numbers[d], 2) for d in range(3)]
     core = lax.axis_index("c")
     plane = (lax.axis_index("y") * 4 + lax.axis_index("zh")) * 2 + core
     lane = lax.broadcasted_iota(jnp.int32, (1, SITES), 1)
     x_coord = lane % LX
     y_coord = lane // LX
     turns = (
-        2 * jnp.bitwise_and(numbers[0] * x_coord, LX - 1)
-        + 4 * jnp.bitwise_and(numbers[1] * y_coord, LY - 1)
-        + jnp.bitwise_and(numbers[2] * plane, LZ - 1)
+        2 * jnp.bitwise_and(momentum[0] * x_coord, LX - 1)
+        + 4 * jnp.bitwise_and(momentum[1] * y_coord, LY - 1)
+        + jnp.bitwise_and(momentum[2] * plane, LZ - 1)
     )
     angle = (2.0 * math.pi / LZ) * jnp.bitwise_and(turns, LZ - 1).astype(jnp.float32)
     cos_part = jnp.cos(angle)
@@ -315,7 +316,7 @@
         out_specs=vmem(),
         scratch_shapes=[pltpu.VMEM((6, NEV, SITES), f32)] * 3,
         compiler_params=params(8),
-    )(jnp.concatenate([momentum, direction]), joined, other, outer)
+    )(4 * momentum + direction, joined, other, outer)
     phased_before = from_y(phased, 1)
     phased_after = from_y(phased, 3)
     phased_opposite = from_y(phased, 2)

time: 58.1 us -> 60.7 us (1.045)
  waiting for transfers between devices: 1.44 us -> 5.74 us
  starting transfers between devices: 14.8 us -> 12.2 us
  blocking collectives: 26.2 us -> 27.8 us
    ppermute x1, waiting for transfers between devices: 0.01 us -> 4.3 us  [on_device(): outer = lax.ppermute(joined, AXES, ring_pairs(outer_plane))]
    all_to_all x1, blocking collectives: 26.2 us -> 27.8 us  [on_device(): packed = lax.all_to_all(packed, ('x', 'zl', 'zh'), 0, 0, tiled=True)]
    ppermute x1, starting transfers between devices: 3.39 us -> 1.92 us  [on_device(): outer = lax.ppermute(joined, AXES, ring_pairs(outer_plane))]
    ppermute x1, starting transfers between devices: 2.38 us -> 1.21 us  [on_device(): received = lax.ppermute(sent, 'c', swap)]
    concatenate x1 -> x0, other arithmetic: 0.73 us -> none  [on_device(): jnp.concatenate([momentum, direction])]
    add x0 -> x1, other arithmetic: none -> 0.66 us  [on_device(): 4 * momentum + direction]
  transfers between devices with their start and end apart: 9 -> 9, of which waited for: 1 -> 2; matrix products, arithmetic and copies ran while one was open for 1% -> 3% of each run, Pallas kernels for 15% -> 15%
where the time goes in v3:
time: 60.7 us; the launch traced here: 60.4 us
  blocking collectives  27.8 us (46%)
  starting transfers between devices  12.2 us (20%)
  Pallas kernels  11.4 us (19%)
  waiting for transfers between devices  5.74 us (9%)
  local copies, waits for them, and re-layouts  1.75 us (3%)
  other arithmetic  0.81 us (1%)
  between operations  0.76 us (1%)
    all_to_all x1, blocking collectives, on_device(): packed = lax.all_to_all(packed, ('x', 'zl', 'zh'), 0, 0, tiled=True)  27.8 us
    ppermute x6, starting transfers between devices, from_y(): return lax.ppermute(block, 'y', [(i, (i + by) % 4) for i in range(4)])  8.95 us
    pallas_call x3, Pallas kernels, both(): pl.pallas_call(both_kernel, out_shape=(crossed_shape, sums_shape), in_spe...  6.7 us
    ppermute x1, waiting for transfers between devices, on_device(): outer = lax.ppermute(joined, AXES, ring_pairs(outer_plane))  4.3 us
    ppermute x1, starting transfers between devices, on_device(): outer = lax.ppermute(joined, AXES, ring_pairs(outer_plane))  1.92 us
    pallas_call x1, Pallas kernels, on_device(): pl.pallas_call(crossed_kernel, out_shape=crossed_shape, in_specs=[vmem()]...  1.6 us
    ppermute x1, waiting for transfers between devices, on_device(): received = lax.ppermute(sent, 'c', swap)  1.42 us
    pallas_call x1, Pallas kernels, on_device(): pl.pallas_call(last_kernel, out_shape=(jax.ShapeDtypeStruct((192, 1152),...  1.33 us
  transfers between devices with their start and end apart: 9, of which 2 were waited for; matrix products, arithmetic and copies ran while one was open for 3% of the time, Pallas kernels for 15%

profile of v3, /device:TPU:64, one launch (start us, length us, event | category | flops | bytes accessed | tf_op | source)
XLA Modules:
  0.0 60.4 jit_solution(15458159723688467718)
XLA Ops:
  0.0 0.9 %copy.5 = bf16[2,3,96,128]{3,2,1,0:T(8,128)(2,1)S(1)} copy(bf16[2,3,96,128]{3,0,1,2:T(2,128)(2,1)} %bitcast.15) | data formatting | bytes 294912 | tf_op jit(solution)/shard_map/transpose | solution.py:299
  0.9 1.7 %collective-permute-start.3 = (bf16[6,96,128]{2,1,0:T(8,128)(2,1)S(1)}, bf16[6,96,128]{2,1,0:T(8,128)(2,1)S(1)}, u32[]{:S(2)}, u32[]{:S(2)}) collective-permute-start(bf16[6,96,128]{2,1,0:T(8,128)(2,1)S(1)} %bitcast.10), channel_id=1, source_target_pairs={{0,8},{8,16},{16,24},{24,0},{1,9},{9,17},{17,25},{25,1},{2,10},{10... | collective-permute-start | bytes 442376 | tf_op jit(solution)/shard_map/ppermute | solution.py:292
  2.6 1.7 %collective-permute-start.4 = (bf16[6,96,128]{2,1,0:T(8,128)(2,1)S(1)}, bf16[6,96,128]{2,1,0:T(8,128)(2,1)S(1)}, u32[]{:S(2)}, u32[]{:S(2)}) collective-permute-start(bf16[6,96,128]{2,1,0:T(8,128)(2,1)S(1)} %bitcast.11), channel_id=1, source_target_pairs={{0,24},{8,0},{16,8},{24,16},{1,25},{9,1},{17,9},{25,17},{2,26},{10... | collective-permute-start | bytes 442376 | tf_op jit(solution)/shard_map/ppermute | solution.py:292
  4.2 2.0 %collective-permute-start.5 = (bf16[6,96,128]{2,1,0:T(8,128)(2,1)S(1)}, bf16[6,96,128]{2,1,0:T(8,128)(2,1)S(1)}, u32[]{:S(2)}, u32[]{:S(2)}) collective-permute-start(bf16[6,96,128]{2,1,0:T(8,128)(2,1)S(1)} %bitcast.12), channel_id=1, source_target_pairs={{0,16},{8,24},{16,0},{24,8},{1,17},{9,25},{17,1},{25,9},{2,18},{10... | collective-permute-start | bytes 442376 | tf_op jit(solution)/shard_map/ppermute | solution.py:292
  6.2 0.7 %reshape.6 = bf16[54,128]{1,0:T(8,128)(2,1)S(1)} reshape(bf16[3,3,3,2,128]{4,3,2,1,0:T(2,128)(2,1)} %bitcast.16) | data formatting | bytes 27648 | tf_op jit(solution)/shard_map/reshape | solution.py:303
  7.0 0.1 pad.2.clone
  7.1 0.2 maximum_maximum_fusion.own
  7.2 0.1 collective-permute-start
  7.3 1.9 %collective-permute-start.1 = (bf16[640,128]{1,0:T(8,128)(2,1)S(1)}, bf16[640,128]{1,0:T(8,128)(2,1)S(1)}, u32[]{:S(2)}, u32[]{:S(2)}) collective-permute-start(bf16[640,128]{1,0:T(8,128)(2,1)S(1)} %maximum_maximum_fusion.own), channel_id=1, source_target_pairs={{0,31},{1,2},{2,1},{3,4},{4,3},{5,6},{6,5},{7,8},{8,7},{9,10},{10,... | collective-permute-start | bytes 491528 | tf_op jit(solution)/shard_map/ppermute | solution.py:307
  9.9 0.7 %multiply_add_fusion.numbers = s32[3]{0:T(128)S(1)} fusion(s32[3]{0:T(128)} %param.6, s32[]{:T(128)} %bitcast.9), kind=kLoop, calls=%fused_computation.1 | loop fusion | flops 6 | bytes 28 | tf_op jit(solution)/shard_map/add | solution.py:319
  10.6 0.0 collective-permute-done.other
  10.6 4.3 %collective-permute-done.1.outer = bf16[640,128]{1,0:T(8,128)(2,1)S(1)} collective-permute-done((bf16[640,128]{1,0:T(8,128)(2,1)S(1)}, bf16[640,128]{1,0:T(8,128)(2,1)S(1)}, u32[]{:S(2)}, u32[]{:S(2)}) %collective-permute-start.1) | collective-permute-done | bytes 163872 | tf_op jit(solution)/shard_map/ppermute | solution.py:307
  14.9 0.5 shard_map.46.phased
  15.4 0.8 %collective-permute-start.7 = (bf16[6,96,128]{2,1,0:T(8,128)(2,1)S(1)}, bf16[6,96,128]{2,1,0:T(8,128)(2,1)S(1)}, u32[]{:S(2)}, u32[]{:S(2)}) collective-permute-start(bf16[6,96,128]{2,1,0:T(8,128)(2,1)S(1)} %shard_map.46.phased), channel_id=1, source_target_pairs={{0,8},{8,16},{16,24},{24,0},{1,9},{9,17},{17,25},{25,1},{2,10},{10... | collective-permute-start | bytes 442376 | tf_op jit(solution)/shard_map/ppermute | solution.py:292
  16.1 2.6 %collective-permute-start.6 = (bf16[6,96,128]{2,1,0:T(8,128)(2,1)S(1)}, bf16[6,96,128]{2,1,0:T(8,128)(2,1)S(1)}, u32[]{:S(2)}, u32[]{:S(2)}) collective-permute-start(bf16[6,96,128]{2,1,0:T(8,128)(2,1)S(1)} %shard_map.46.phased), channel_id=1, source_target_pairs={{0,24},{8,0},{16,8},{24,16},{1,25},{9,1},{17,9},{25,17},{2,26},{10... | collective-permute-start | bytes 442376 | tf_op jit(solution)/shard_map/ppermute | solution.py:292
  18.7 0.0 collective-permute-done.3.source
  18.7 0.3 collective-permute-start.2
  19.0 1.6 %shard_map.47.previous = bf16[4,576,768]{2,1,0:T(8,128)(2,1)S(1)} custom-call(bf16[6,96,128]{2,1,0:T(8,128)(2,1)S(1)} %bitcast.14), custom_call_target="tpu_custom_call" | custom-call | tf_op jit(solution)/shard_map/pallas_call | solution.py:342
  20.6 0.0 collective-permute-done.4.source
  20.6 0.0 collective-permute-done.5.source
  20.6 2.2 %shard_map.48 = (bf16[4,576,768]{2,1,0:T(8,128)(2,1)S(1)}, f32[4,576,192]{2,1,0:T(8,128)S(1)}) custom-call(bf16[6,96,128]{2,1,0:T(8,128)(2,1)S(1)} %collective-permute-done.3.source, bf16[6,96,128]{2,1,0:T(8,128)(2,1)S(1)} %shard_map.46.phased, bf16[4,576,768]{2,1,0:T(8,128)(2,1)S(1)} %shard_map.47.previous), custom_call_target="tpu_custom_call" | custom-call | tf_op jit(solution)/shard_map/pallas_call | solution.py:332
  22.9 0.0 collective-permute-done.7.phased
  22.9 2.2 %shard_map.49 = (bf16[4,576,768]{2,1,0:T(8,128)(2,1)S(1)}, f32[4,576,192]{2,1,0:T(8,128)S(1)}) custom-call(bf16[6,96,128]{2,1,0:T(8,128)(2,1)S(1)} %collective-permute-done.4.source, bf16[6,96,128]{2,1,0:T(8,128)(2,1)S(1)} %collective-permute-done.7.phased, bf16[4,576,768]{2,1,0:T(8,128)(2,1)S(1)} %get-tuple-element.19.previous, ...), custom_call_target="tpu_custom_call" | custom-call | tf_op jit(solution)/shard_map/pallas_call | solution.py:332
  25.1 0.0 collective-permute-done.6.phased
  25.1 2.2 %shard_map.50 = (bf16[4,576,768]{2,1,0:T(8,128)(2,1)S(1)}, f32[4,576,192]{2,1,0:T(8,128)S(1)}) custom-call(bf16[6,96,128]{2,1,0:T(8,128)(2,1)S(1)} %collective-permute-done.5.source, bf16[6,96,128]{2,1,0:T(8,128)(2,1)S(1)} %collective-permute-done.6.phased, bf16[4,576,768]{2,1,0:T(8,128)(2,1)S(1)} %get-tuple-element.21.previous, ...), custom_call_target="tpu_custom_call" | custom-call | tf_op jit(solution)/shard_map/pallas_call | solution.py:332
  27.4 0.0 collective-permute-done.2.phased
  27.4 1.3 %shard_map.51 = (bf16[192,1152]{1,0:T(8,128)(2,1)S(1)}, f32[192,1152]{1,0:T(8,128)S(1)}) custom-call(bf16[6,96,128]{2,1,0:T(8,128)(2,1)S(1)} %collective-permute-done.2.phased, bf16[4,576,768]{2,1,0:T(8,128)(2,1)S(1)} %get-tuple-element.23.crossed, f32[4,576,192]{2,1,0:T(8,128)S(1)} %get-tuple-element.24.sums), custom_call_target="tpu_custom_call" | custom-call | tf_op jit(solution)/shard_map/pallas_call | solution.py:354
  28.7 1.2 %collective-permute-start.8 = (bf16[192,1152]{1,0:T(8,128)(2,1)S(1)}, bf16[192,1152]{1,0:T(8,128)(2,1)S(1)}, u32[]{:S(2)}, u32[]{:S(2)}) collective-permute-start(bf16[192,1152]{1,0:T(8,128)(2,1)S(1)} %get-tuple-element.26), channel_id=1, source_target_pairs={{0,1},{1,0},{2,3},{3,2},{4,5},{5,4},{6,7},{7,6},{8,9},{9,8},{10,11... | collective-permute-start | bytes 1327112 | tf_op jit(solution)/shard_map/ppermute | solution.py:365
  29.9 1.4 %collective-permute-done.8.received = bf16[192,1152]{1,0:T(8,128)(2,1)S(1)} collective-permute-done((bf16[192,1152]{1,0:T(8,128)(2,1)S(1)}, bf16[192,1152]{1,0:T(8,128)(2,1)S(1)}, u32[]{:S(2)}, u32[]{:S(2)}) %collective-permute-start.8) | collective-permute-done | bytes 442400 | tf_op jit(solution)/shard_map/ppermute | solution.py:365
  31.3 0.3 shard_map.52
  31.7 27.8 %all_to_all.5.parts = bf16[32,56,128]{2,1,0:T(8,128)(2,1)S(1)} all-to-all(bf16[32,56,128]{2,1,0:T(8,128)(2,1)S(1)} %shard_map.52), channel_id=1, replica_groups=mesh['x'=4,'zl'=2,'y'=4,'zh'=4,'c'=2] {'x','zl','zh'}, dimensions={0} | all-to-all | bytes 917504 | tf_op jit(solution)/shard_map/all_to_all | solution.py:374
  59.5 0.9 %shard_map.53 = f32[3,8,2,1152]{3,2,1,0:T(2,128)} custom-call(bf16[32,56,128]{2,1,0:T(8,128)(2,1)S(1)} %all_to_all.5.parts), custom_call_target="tpu_custom_call" | custom-call | tf_op jit(solution)/shard_map/pallas_call | solution.py:375
  (1 shorter events, 0.0 us)
Async XLA Ops:
  0.9 17.7 %collective-permute-start.3 = (bf16[6,96,128]{2,1,0:T(8,128)(2,1)S(1)}, bf16[6,96,128]{2,1,0:T(8,128)(2,1)S(1)}, u32[]{:S(2)}, u32[]{:S(2)}) collective-permute-start(bf16[6,96,128]{2,1,0:T(8,128)(2,1)S(1)} %bitcast.10), channel_id=1, source_target_pairs={{0,8},{8,16},{16,24},{24,0},{1,9},{9,17},{17,25},{25,1},{2,10},{10... | collective-permute-start | bytes 442376 | tf_op jit(solution)/shard_map/ppermute | solution.py:292
  2.6 18.0 %collective-permute-start.4 = (bf16[6,96,128]{2,1,0:T(8,128)(2,1)S(1)}, bf16[6,96,128]{2,1,0:T(8,128)(2,1)S(1)}, u32[]{:S(2)}, u32[]{:S(2)}) collective-permute-start(bf16[6,96,128]{2,1,0:T(8,128)(2,1)S(1)} %bitcast.11), channel_id=1, source_target_pairs={{0,24},{8,0},{16,8},{24,16},{1,25},{9,1},{17,9},{25,17},{2,26},{10... | collective-permute-start | bytes 442376 | tf_op jit(solution)/shard_map/ppermute | solution.py:292
  4.2 16.4 %collective-permute-start.5 = (bf16[6,96,128]{2,1,0:T(8,128)(2,1)S(1)}, bf16[6,96,128]{2,1,0:T(8,128)(2,1)S(1)}, u32[]{:S(2)}, u32[]{:S(2)}) collective-permute-start(bf16[6,96,128]{2,1,0:T(8,128)(2,1)S(1)} %bitcast.12), channel_id=1, source_target_pairs={{0,16},{8,24},{16,0},{24,8},{1,17},{9,25},{17,1},{25,9},{2,18},{10... | collective-permute-start | bytes 442376 | tf_op jit(solution)/shard_map/ppermute | solution.py:292
  7.2 3.3 %collective-permute-start = (bf16[640,128]{1,0:T(8,128)(2,1)S(1)}, bf16[640,128]{1,0:T(8,128)(2,1)S(1)}, u32[]{:S(2)}, u32[]{:S(2)}) collective-permute-start(bf16[640,128]{1,0:T(8,128)(2,1)S(1)} %maximum_maximum_fusion.own), channel_id=1, source_target_pairs={{0,1},{1,0},{2,3},{3,2},{4,5},{5,4},{6,7},{7,6},{8,9},{9,8},{10,11... | collective-permute-start | bytes 491528 | tf_op jit(solution)/shard_map/ppermute | solution.py:308
  7.3 7.5 %collective-permute-start.1 = (bf16[640,128]{1,0:T(8,128)(2,1)S(1)}, bf16[640,128]{1,0:T(8,128)(2,1)S(1)}, u32[]{:S(2)}, u32[]{:S(2)}) collective-permute-start(bf16[640,128]{1,0:T(8,128)(2,1)S(1)} %maximum_maximum_fusion.own), channel_id=1, source_target_pairs={{0,31},{1,2},{2,1},{3,4},{4,3},{5,6},{6,5},{7,8},{8,7},{9,10},{10,... | collective-permute-start | bytes 491528 | tf_op jit(solution)/shard_map/ppermute | solution.py:307
  15.4 7.5 %collective-permute-start.7 = (bf16[6,96,128]{2,1,0:T(8,128)(2,1)S(1)}, bf16[6,96,128]{2,1,0:T(8,128)(2,1)S(1)}, u32[]{:S(2)}, u32[]{:S(2)}) collective-permute-start(bf16[6,96,128]{2,1,0:T(8,128)(2,1)S(1)} %shard_map.46.phased), channel_id=1, source_target_pairs={{0,8},{8,16},{16,24},{24,0},{1,9},{9,17},{17,25},{25,1},{2,10},{10... | collective-permute-start | bytes 442376 | tf_op jit(solution)/shard_map/ppermute | solution.py:292
  16.1 9.0 %collective-permute-start.6 = (bf16[6,96,128]{2,1,0:T(8,128)(2,1)S(1)}, bf16[6,96,128]{2,1,0:T(8,128)(2,1)S(1)}, u32[]{:S(2)}, u32[]{:S(2)}) collective-permute-start(bf16[6,96,128]{2,1,0:T(8,128)(2,1)S(1)} %shard_map.46.phased), channel_id=1, source_target_pairs={{0,24},{8,0},{16,8},{24,16},{1,25},{9,1},{17,9},{25,17},{2,26},{10... | collective-permute-start | bytes 442376 | tf_op jit(solution)/shard_map/ppermute | solution.py:292
  18.7 8.7 %collective-permute-start.2 = (bf16[6,96,128]{2,1,0:T(8,128)(2,1)S(1)}, bf16[6,96,128]{2,1,0:T(8,128)(2,1)S(1)}, u32[]{:S(2)}, u32[]{:S(2)}) collective-permute-start(bf16[6,96,128]{2,1,0:T(8,128)(2,1)S(1)} %shard_map.46.phased), channel_id=1, source_target_pairs={{0,16},{8,24},{16,0},{24,8},{1,17},{9,25},{17,1},{25,9},{2,18},{10... | collective-permute-start | bytes 442376 | tf_op jit(solution)/shard_map/ppermute | solution.py:292
  28.7 2.6 %collective-permute-start.8 = (bf16[192,1152]{1,0:T(8,128)(2,1)S(1)}, bf16[192,1152]{1,0:T(8,128)(2,1)S(1)}, u32[]{:S(2)}, u32[]{:S(2)}) collective-permute-start(bf16[192,1152]{1,0:T(8,128)(2,1)S(1)} %get-tuple-element.26), channel_id=1, source_target_pairs={{0,1},{1,0},{2,3},{3,2},{4,5},{5,4},{6,7},{7,6},{8,9},{9,8},{10,11... | collective-permute-start | bytes 1327112 | tf_op jit(solution)/shard_map/ppermute | solution.py:365

commit v4 on v0

--- a/solution.py
+++ b/solution.py
@@ -235,7 +235,7 @@
     for q in range(8):
         for zh in range(4):
             for half in range(2):
-                out[4 * q + zh, 24 * half : 24 * half + 24, :] = total[
+                out[8 * zh + 4 * (q % 2) + q // 2, 24 * half : 24 * half + 24, :] = total[
                     2 * zh + half, pl.ds(q, 24, 8), :
                 ].astype(jnp.bfloat16)
         tail = total[8, pl.ds(q, 24, 8), :]
@@ -244,15 +244,16 @@
             for g in range(3):
                 moved = pltpu.roll(tail[8 * g : 8 * g + 8], (32 * (g - zh)) % SITES, 1)
                 joined = jnp.where(lane // 32 == g, moved, joined)
-            out[4 * q + zh, 48:56, :] = joined.astype(jnp.bfloat16)
+            out[8 * zh + 4 * (q % 2) + q // 2, 48:56, :] = joined.astype(jnp.bfloat16)
 
 
 def final_kernel(parts, out, rows):
     scale = 1.0 / math.sqrt(LX * LY * LZ)
     for t in range(8):
-        total = parts[4 * t].astype(jnp.float32)
+        here = 4 * (t % 2) + t // 2
+        total = parts[here].astype(jnp.float32)
         for zh in range(1, 4):
-            total += parts[4 * t + zh].astype(jnp.float32)
+            total += parts[8 * zh + here].astype(jnp.float32)
         total *= scale
         rows[0, pl.ds(t, 24, 8), :] = total[:24]
         rows[1, pl.ds(t, 24, 8), :] = total[24:48]
@@ -370,7 +371,7 @@
         scratch_shapes=[pltpu.VMEM((9, 192, SITES), f32)],
         compiler_params=params(16),
     )(mine, received)
-    packed = lax.all_to_all(packed, ("x", "zl", "zh"), 0, 0, tiled=True)
+    packed = lax.all_to_all(packed, ("zh", "zl", "x"), 0, 0, tiled=True)
     return pl.pallas_call(
         final_kernel,
         out_shape=jax.ShapeDtypeStruct((3, 8, 2, 12 * NEV), f32),

time: 58.1 us -> 59.1 us (1.017)
  the two profiles are of different devices: /device:TPU:64 before, /device:TPU:16 now
where the time goes in v4:
time: 59.1 us; the launch traced here: 58.8 us
  blocking collectives  21.3 us (36%)
  starting transfers between devices  20.9 us (35%)
  Pallas kernels  11.4 us (19%)
  waiting for transfers between devices  1.8 us (3%)
  local copies, waits for them, and re-layouts  1.75 us (3%)
  other arithmetic  0.88 us (1%)
  between operations  0.78 us (1%)
    all_to_all x1, blocking collectives, on_device(): packed = lax.all_to_all(packed, ('zh', 'zl', 'x'), 0, 0, tiled=True)  21.3 us
    ppermute x6, starting transfers between devices, from_y(): return lax.ppermute(block, 'y', [(i, (i + by) % 4) for i in range(4)])  12.5 us
    ppermute x1, starting transfers between devices, on_device(): outer = lax.ppermute(joined, AXES, ring_pairs(outer_plane))  8.18 us
    pallas_call x3, Pallas kernels, both(): pl.pallas_call(both_kernel, out_shape=(crossed_shape, sums_shape), in_spe...  6.69 us
    ppermute x1, waiting for transfers between devices, on_device(): received = lax.ppermute(sent, 'c', swap)  1.78 us
    pallas_call x1, Pallas kernels, on_device(): pl.pallas_call(crossed_kernel, out_shape=crossed_shape, in_specs=[vmem()]...  1.59 us
    pallas_call x1, Pallas kernels, on_device(): pl.pallas_call(last_kernel, out_shape=(jax.ShapeDtypeStruct((192, 1152),...  1.33 us
  transfers between devices with their start and end apart: 9, of which 1 were waited for; matrix products, arithmetic and copies ran while one was open for 1% of the time, Pallas kernels for 15%

profile of v4, /device:TPU:16, one launch (start us, length us, event | category | flops | bytes accessed | tf_op | source)
XLA Modules:
  0.0 58.8 jit_solution(49197779858099323)
XLA Ops:
  0.0 0.9 %copy.5 = bf16[2,3,96,128]{3,2,1,0:T(8,128)(2,1)S(1)} copy(bf16[2,3,96,128]{3,0,1,2:T(2,128)(2,1)} %bitcast.13) | data formatting | bytes 294912 | tf_op jit(solution)/shard_map/transpose | solution.py:299
  0.9 0.7 %reshape.6 = bf16[54,128]{1,0:T(8,128)(2,1)S(1)} reshape(bf16[3,3,3,2,128]{4,3,2,1,0:T(2,128)(2,1)} %bitcast.14) | data formatting | bytes 27648 | tf_op jit(solution)/shard_map/reshape | solution.py:303
  1.7 0.1 pad.2.clone
  1.8 0.2 maximum_maximum_fusion.own
  1.9 0.1 collective-permute-start
  2.0 8.2 %collective-permute-start.1 = (bf16[640,128]{1,0:T(8,128)(2,1)S(1)}, bf16[640,128]{1,0:T(8,128)(2,1)S(1)}, u32[]{:S(2)}, u32[]{:S(2)}) collective-permute-start(bf16[640,128]{1,0:T(8,128)(2,1)S(1)} %maximum_maximum_fusion.own), channel_id=1, source_target_pairs={{0,31},{1,2},{2,1},{3,4},{4,3},{5,6},{6,5},{7,8},{8,7},{9,10},{10,... | collective-permute-start | bytes 491528 | tf_op jit(solution)/shard_map/ppermute | solution.py:307
  10.2 1.7 %collective-permute-start.3 = (bf16[6,96,128]{2,1,0:T(8,128)(2,1)S(1)}, bf16[6,96,128]{2,1,0:T(8,128)(2,1)S(1)}, u32[]{:S(2)}, u32[]{:S(2)}) collective-permute-start(bf16[6,96,128]{2,1,0:T(8,128)(2,1)S(1)} %bitcast.9), channel_id=1, source_target_pairs={{0,8},{8,16},{16,24},{24,0},{1,9},{9,17},{17,25},{25,1},{2,10},{10... | collective-permute-start | bytes 442376 | tf_op jit(solution)/shard_map/ppermute | solution.py:292
  11.9 0.4 collective-permute-start.4
  12.3 4.1 %collective-permute-start.5 = (bf16[6,96,128]{2,1,0:T(8,128)(2,1)S(1)}, bf16[6,96,128]{2,1,0:T(8,128)(2,1)S(1)}, u32[]{:S(2)}, u32[]{:S(2)}) collective-permute-start(bf16[6,96,128]{2,1,0:T(8,128)(2,1)S(1)} %bitcast.11), channel_id=1, source_target_pairs={{0,16},{8,24},{16,0},{24,8},{1,17},{9,25},{17,1},{25,9},{2,18},{10... | collective-permute-start | bytes 442376 | tf_op jit(solution)/shard_map/ppermute | solution.py:292
  17.1 0.7 %pad_add_fusion.numbers = s32[4]{0:T(128)S(1)} fusion(s32[1]{0:T(128)S(6)} %copy.7, s32[3]{0:T(128)} %param.6), kind=kLoop, calls=%fused_computation.1 | loop fusion | flops 4 | bytes 32 | tf_op jit(solution)/shard_map/concatenate | solution.py:319
  17.8 0.0 collective-permute-done.other
  17.8 0.0 collective-permute-done.1.outer
  17.8 0.5 shard_map.46.phased
  18.3 0.1 collective-permute-start.7
  18.4 2.0 %collective-permute-start.6 = (bf16[6,96,128]{2,1,0:T(8,128)(2,1)S(1)}, bf16[6,96,128]{2,1,0:T(8,128)(2,1)S(1)}, u32[]{:S(2)}, u32[]{:S(2)}) collective-permute-start(bf16[6,96,128]{2,1,0:T(8,128)(2,1)S(1)} %shard_map.46.phased), channel_id=1, source_target_pairs={{0,24},{8,0},{16,8},{24,16},{1,25},{9,1},{17,9},{25,17},{2,26},{10... | collective-permute-start | bytes 442376 | tf_op jit(solution)/shard_map/ppermute | solution.py:292
  20.4 0.0 collective-permute-done.3.source
  20.4 4.2 %collective-permute-start.2 = (bf16[6,96,128]{2,1,0:T(8,128)(2,1)S(1)}, bf16[6,96,128]{2,1,0:T(8,128)(2,1)S(1)}, u32[]{:S(2)}, u32[]{:S(2)}) collective-permute-start(bf16[6,96,128]{2,1,0:T(8,128)(2,1)S(1)} %shard_map.46.phased), channel_id=1, source_target_pairs={{0,16},{8,24},{16,0},{24,8},{1,17},{9,25},{17,1},{25,9},{2,18},{10... | collective-permute-start | bytes 442376 | tf_op jit(solution)/shard_map/ppermute | solution.py:292
  24.6 1.6 %shard_map.47.previous = bf16[4,576,768]{2,1,0:T(8,128)(2,1)S(1)} custom-call(bf16[6,96,128]{2,1,0:T(8,128)(2,1)S(1)} %bitcast.12), custom_call_target="tpu_custom_call" | custom-call | tf_op jit(solution)/shard_map/pallas_call | solution.py:342
  26.2 0.0 collective-permute-done.4.source
  26.2 0.0 collective-permute-done.5.source
  26.2 2.2 %shard_map.48 = (bf16[4,576,768]{2,1,0:T(8,128)(2,1)S(1)}, f32[4,576,192]{2,1,0:T(8,128)S(1)}) custom-call(bf16[6,96,128]{2,1,0:T(8,128)(2,1)S(1)} %collective-permute-done.3.source, bf16[6,96,128]{2,1,0:T(8,128)(2,1)S(1)} %shard_map.46.phased, bf16[4,576,768]{2,1,0:T(8,128)(2,1)S(1)} %shard_map.47.previous), custom_call_target="tpu_custom_call" | custom-call | tf_op jit(solution)/shard_map/pallas_call | solution.py:332
  28.5 0.0 collective-permute-done.7.phased
  28.5 2.2 %shard_map.49 = (bf16[4,576,768]{2,1,0:T(8,128)(2,1)S(1)}, f32[4,576,192]{2,1,0:T(8,128)S(1)}) custom-call(bf16[6,96,128]{2,1,0:T(8,128)(2,1)S(1)} %collective-permute-done.4.source, bf16[6,96,128]{2,1,0:T(8,128)(2,1)S(1)} %collective-permute-done.7.phased, bf16[4,576,768]{2,1,0:T(8,128)(2,1)S(1)} %get-tuple-element.19.previous, ...), custom_call_target="tpu_custom_call" | custom-call | tf_op jit(solution)/shard_map/pallas_call | solution.py:332
  30.7 0.0 collective-permute-done.6.phased
  30.7 2.2 %shard_map.50 = (bf16[4,576,768]{2,1,0:T(8,128)(2,1)S(1)}, f32[4,576,192]{2,1,0:T(8,128)S(1)}) custom-call(bf16[6,96,128]{2,1,0:T(8,128)(2,1)S(1)} %collective-permute-done.5.source, bf16[6,96,128]{2,1,0:T(8,128)(2,1)S(1)} %collective-permute-done.6.phased, bf16[4,576,768]{2,1,0:T(8,128)(2,1)S(1)} %get-tuple-element.21.previous, ...), custom_call_target="tpu_custom_call" | custom-call | tf_op jit(solution)/shard_map/pallas_call | solution.py:332
  33.0 0.0 collective-permute-done.2.phased
  33.0 1.3 %shard_map.51 = (bf16[192,1152]{1,0:T(8,128)(2,1)S(1)}, f32[192,1152]{1,0:T(8,128)S(1)}) custom-call(bf16[6,96,128]{2,1,0:T(8,128)(2,1)S(1)} %collective-permute-done.2.phased, bf16[4,576,768]{2,1,0:T(8,128)(2,1)S(1)} %get-tuple-element.23.crossed, f32[4,576,192]{2,1,0:T(8,128)S(1)} %get-tuple-element.24.sums), custom_call_target="tpu_custom_call" | custom-call | tf_op jit(solution)/shard_map/pallas_call | solution.py:354
  34.3 0.1 collective-permute-start.8
  34.4 1.8 %collective-permute-done.8.received = bf16[192,1152]{1,0:T(8,128)(2,1)S(1)} collective-permute-done((bf16[192,1152]{1,0:T(8,128)(2,1)S(1)}, bf16[192,1152]{1,0:T(8,128)(2,1)S(1)}, u32[]{:S(2)}, u32[]{:S(2)}) %collective-permute-start.8) | collective-permute-done | bytes 442400 | tf_op jit(solution)/shard_map/ppermute | solution.py:365
  36.2 0.3 shard_map.52
  36.5 21.3 %all_to_all.5.parts = bf16[32,56,128]{2,1,0:T(8,128)(2,1)S(1)} all-to-all(bf16[32,56,128]{2,1,0:T(8,128)(2,1)S(1)} %shard_map.52), channel_id=1, replica_groups=mesh['x'=4,'zl'=2,'y'=4,'zh'=4,'c'=2] {'zh','zl','x'}, dimensions={0} | all-to-all | bytes 917504 | tf_op jit(solution)/shard_map/all_to_all | solution.py:374
  57.9 0.9 %shard_map.53 = f32[3,8,2,1152]{3,2,1,0:T(2,128)} custom-call(bf16[32,56,128]{2,1,0:T(8,128)(2,1)S(1)} %all_to_all.5.parts), custom_call_target="tpu_custom_call" | custom-call | tf_op jit(solution)/shard_map/pallas_call | solution.py:375
  (1 shorter events, 0.0 us)
Async XLA Ops:
  1.9 15.9 %collective-permute-start = (bf16[640,128]{1,0:T(8,128)(2,1)S(1)}, bf16[640,128]{1,0:T(8,128)(2,1)S(1)}, u32[]{:S(2)}, u32[]{:S(2)}) collective-permute-start(bf16[640,128]{1,0:T(8,128)(2,1)S(1)} %maximum_maximum_fusion.own), channel_id=1, source_target_pairs={{0,1},{1,0},{2,3},{3,2},{4,5},{5,4},{6,7},{7,6},{8,9},{9,8},{10,11... | collective-permute-start | bytes 491528 | tf_op jit(solution)/shard_map/ppermute | solution.py:308
  2.0 15.8 %collective-permute-start.1 = (bf16[640,128]{1,0:T(8,128)(2,1)S(1)}, bf16[640,128]{1,0:T(8,128)(2,1)S(1)}, u32[]{:S(2)}, u32[]{:S(2)}) collective-permute-start(bf16[640,128]{1,0:T(8,128)(2,1)S(1)} %maximum_maximum_fusion.own), channel_id=1, source_target_pairs={{0,31},{1,2},{2,1},{3,4},{4,3},{5,6},{6,5},{7,8},{8,7},{9,10},{10,... | collective-permute-start | bytes 491528 | tf_op jit(solution)/shard_map/ppermute | solution.py:307
  10.2 10.2 %collective-permute-start.3 = (bf16[6,96,128]{2,1,0:T(8,128)(2,1)S(1)}, bf16[6,96,128]{2,1,0:T(8,128)(2,1)S(1)}, u32[]{:S(2)}, u32[]{:S(2)}) collective-permute-start(bf16[6,96,128]{2,1,0:T(8,128)(2,1)S(1)} %bitcast.9), channel_id=1, source_target_pairs={{0,8},{8,16},{16,24},{24,0},{1,9},{9,17},{17,25},{25,1},{2,10},{10... | collective-permute-start | bytes 442376 | tf_op jit(solution)/shard_map/ppermute | solution.py:292
  11.9 14.4 %collective-permute-start.4 = (bf16[6,96,128]{2,1,0:T(8,128)(2,1)S(1)}, bf16[6,96,128]{2,1,0:T(8,128)(2,1)S(1)}, u32[]{:S(2)}, u32[]{:S(2)}) collective-permute-start(bf16[6,96,128]{2,1,0:T(8,128)(2,1)S(1)} %bitcast.10), channel_id=1, source_target_pairs={{0,24},{8,0},{16,8},{24,16},{1,25},{9,1},{17,9},{25,17},{2,26},{10... | collective-permute-start | bytes 442376 | tf_op jit(solution)/shard_map/ppermute | solution.py:292
  12.3 13.9 %collective-permute-start.5 = (bf16[6,96,128]{2,1,0:T(8,128)(2,1)S(1)}, bf16[6,96,128]{2,1,0:T(8,128)(2,1)S(1)}, u32[]{:S(2)}, u32[]{:S(2)}) collective-permute-start(bf16[6,96,128]{2,1,0:T(8,128)(2,1)S(1)} %bitcast.11), channel_id=1, source_target_pairs={{0,16},{8,24},{16,0},{24,8},{1,17},{9,25},{17,1},{25,9},{2,18},{10... | collective-permute-start | bytes 442376 | tf_op jit(solution)/shard_map/ppermute | solution.py:292
  18.3 10.2 %collective-permute-start.7 = (bf16[6,96,128]{2,1,0:T(8,128)(2,1)S(1)}, bf16[6,96,128]{2,1,0:T(8,128)(2,1)S(1)}, u32[]{:S(2)}, u32[]{:S(2)}) collective-permute-start(bf16[6,96,128]{2,1,0:T(8,128)(2,1)S(1)} %shard_map.46.phased), channel_id=1, source_target_pairs={{0,8},{8,16},{16,24},{24,0},{1,9},{9,17},{17,25},{25,1},{2,10},{10... | collective-permute-start | bytes 442376 | tf_op jit(solution)/shard_map/ppermute | solution.py:292
  18.4 12.3 %collective-permute-start.6 = (bf16[6,96,128]{2,1,0:T(8,128)(2,1)S(1)}, bf16[6,96,128]{2,1,0:T(8,128)(2,1)S(1)}, u32[]{:S(2)}, u32[]{:S(2)}) collective-permute-start(bf16[6,96,128]{2,1,0:T(8,128)(2,1)S(1)} %shard_map.46.phased), channel_id=1, source_target_pairs={{0,24},{8,0},{16,8},{24,16},{1,25},{9,1},{17,9},{25,17},{2,26},{10... | collective-permute-start | bytes 442376 | tf_op jit(solution)/shard_map/ppermute | solution.py:292
  20.4 12.6 %collective-permute-start.2 = (bf16[6,96,128]{2,1,0:T(8,128)(2,1)S(1)}, bf16[6,96,128]{2,1,0:T(8,128)(2,1)S(1)}, u32[]{:S(2)}, u32[]{:S(2)}) collective-permute-start(bf16[6,96,128]{2,1,0:T(8,128)(2,1)S(1)} %shard_map.46.phased), channel_id=1, source_target_pairs={{0,16},{8,24},{16,0},{24,8},{1,17},{9,25},{17,1},{25,9},{2,18},{10... | collective-permute-start | bytes 442376 | tf_op jit(solution)/shard_map/ppermute | solution.py:292
  34.3 1.9 %collective-permute-start.8 = (bf16[192,1152]{1,0:T(8,128)(2,1)S(1)}, bf16[192,1152]{1,0:T(8,128)(2,1)S(1)}, u32[]{:S(2)}, u32[]{:S(2)}) collective-permute-start(bf16[192,1152]{1,0:T(8,128)(2,1)S(1)} %get-tuple-element.26), channel_id=1, source_target_pairs={{0,1},{1,0},{2,3},{3,2},{4,5},{5,4},{6,7},{7,6},{8,9},{9,8},{10,11... | collective-permute-start | bytes 1327112 | tf_op jit(solution)/shard_map/ppermute | solution.py:365

commit v5 on v4

--- a/solution.py
+++ b/solution.py
@@ -235,7 +235,7 @@
     for q in range(8):
         for zh in range(4):
             for half in range(2):
-                out[8 * zh + 4 * (q % 2) + q // 2, 24 * half : 24 * half + 24, :] = total[
+                out[8 * (q // 2) + 2 * zh + q % 2, 24 * half : 24 * half + 24, :] = total[
                     2 * zh + half, pl.ds(q, 24, 8), :
                 ].astype(jnp.bfloat16)
         tail = total[8, pl.ds(q, 24, 8), :]
@@ -244,16 +244,16 @@
             for g in range(3):
                 moved = pltpu.roll(tail[8 * g : 8 * g + 8], (32 * (g - zh)) % SITES, 1)
                 joined = jnp.where(lane // 32 == g, moved, joined)
-            out[8 * zh + 4 * (q % 2) + q // 2, 48:56, :] = joined.astype(jnp.bfloat16)
+            out[8 * (q // 2) + 2 * zh + q % 2, 48:56, :] = joined.astype(jnp.bfloat16)
 
 
 def final_kernel(parts, out, rows):
     scale = 1.0 / math.sqrt(LX * LY * LZ)
     for t in range(8):
-        here = 4 * (t % 2) + t // 2
+        here = 8 * (t // 2) + t % 2
         total = parts[here].astype(jnp.float32)
         for zh in range(1, 4):
-            total += parts[8 * zh + here].astype(jnp.float32)
+            total += parts[here + 2 * zh].astype(jnp.float32)
         total *= scale
         rows[0, pl.ds(t, 24, 8), :] = total[:24]
         rows[1, pl.ds(t, 24, 8), :] = total[24:48]
@@ -371,7 +371,7 @@
         scratch_shapes=[pltpu.VMEM((9, 192, SITES), f32)],
         compiler_params=params(16),
     )(mine, received)
-    packed = lax.all_to_all(packed, ("zh", "zl", "x"), 0, 0, tiled=True)
+    packed = lax.all_to_all(packed, ("x", "zh", "zl"), 0, 0, tiled=True)
     return pl.pallas_call(
         final_kernel,
         out_shape=jax.ShapeDtypeStruct((3, 8, 2, 12 * NEV), f32),

time: 59.1 us -> 58.7 us (level)
  the two profiles are of different devices: /device:TPU:16 before, /device:TPU:48 now
where the time goes in v5:
time: 58.7 us; the launch traced here: 58.5 us
  blocking collectives  31.9 us (54%)
  Pallas kernels  11.5 us (20%)
  starting transfers between devices  8.78 us (15%)
  waiting for transfers between devices  2.83 us (5%)
  local copies, waits for them, and re-layouts  1.75 us (3%)
  other arithmetic  0.88 us (1%)
  between operations  0.78 us (1%)
    all_to_all x1, blocking collectives, on_device(): packed = lax.all_to_all(packed, ('x', 'zh', 'zl'), 0, 0, tiled=True)  31.9 us
    ppermute x6, starting transfers between devices, from_y(): return lax.ppermute(block, 'y', [(i, (i + by) % 4) for i in range(4)])  7.92 us
    pallas_call x3, Pallas kernels, both(): pl.pallas_call(both_kernel, out_shape=(crossed_shape, sums_shape), in_spe...  6.69 us
    ppermute x1, waiting for transfers between devices, on_device(): received = lax.ppermute(sent, 'c', swap)  1.78 us
    pallas_call x1, Pallas kernels, on_device(): pl.pallas_call(crossed_kernel, out_shape=crossed_shape, in_specs=[vmem()]...  1.59 us
    pallas_call x1, Pallas kernels, on_device(): pl.pallas_call(last_kernel, out_shape=(jax.ShapeDtypeStruct((192, 1152),...  1.33 us
  transfers between devices with their start and end apart: 9, of which 2 were waited for; matrix products, arithmetic and copies ran while one was open for 1% of the time, Pallas kernels for 15%

profile of v5, /device:TPU:48, one launch (start us, length us, event | category | flops | bytes accessed | tf_op | source)
XLA Modules:
  0.0 58.5 jit_solution(9683294571993576604)
XLA Ops:
  0.0 0.9 %copy.5 = bf16[2,3,96,128]{3,2,1,0:T(8,128)(2,1)S(1)} copy(bf16[2,3,96,128]{3,0,1,2:T(2,128)(2,1)} %bitcast.13) | data formatting | bytes 294912 | tf_op jit(solution)/shard_map/transpose | solution.py:299
  0.9 0.7 %reshape.6 = bf16[54,128]{1,0:T(8,128)(2,1)S(1)} reshape(bf16[3,3,3,2,128]{4,3,2,1,0:T(2,128)(2,1)} %bitcast.14) | data formatting | bytes 27648 | tf_op jit(solution)/shard_map/reshape | solution.py:303
  1.7 0.1 pad.2.clone
  1.8 0.2 maximum_maximum_fusion.own
  1.9 0.1 collective-permute-start
  2.0 0.7 %collective-permute-start.1 = (bf16[640,128]{1,0:T(8,128)(2,1)S(1)}, bf16[640,128]{1,0:T(8,128)(2,1)S(1)}, u32[]{:S(2)}, u32[]{:S(2)}) collective-permute-start(bf16[640,128]{1,0:T(8,128)(2,1)S(1)} %maximum_maximum_fusion.own), channel_id=1, source_target_pairs={{0,31},{1,2},{2,1},{3,4},{4,3},{5,6},{6,5},{7,8},{8,7},{9,10},{10,... | collective-permute-start | bytes 491528 | tf_op jit(solution)/shard_map/ppermute | solution.py:307
  2.7 1.4 %collective-permute-start.3 = (bf16[6,96,128]{2,1,0:T(8,128)(2,1)S(1)}, bf16[6,96,128]{2,1,0:T(8,128)(2,1)S(1)}, u32[]{:S(2)}, u32[]{:S(2)}) collective-permute-start(bf16[6,96,128]{2,1,0:T(8,128)(2,1)S(1)} %bitcast.9), channel_id=1, source_target_pairs={{0,8},{8,16},{16,24},{24,0},{1,9},{9,17},{17,25},{25,1},{2,10},{10... | collective-permute-start | bytes 442376 | tf_op jit(solution)/shard_map/ppermute | solution.py:292
  4.1 0.7 %collective-permute-start.4 = (bf16[6,96,128]{2,1,0:T(8,128)(2,1)S(1)}, bf16[6,96,128]{2,1,0:T(8,128)(2,1)S(1)}, u32[]{:S(2)}, u32[]{:S(2)}) collective-permute-start(bf16[6,96,128]{2,1,0:T(8,128)(2,1)S(1)} %bitcast.10), channel_id=1, source_target_pairs={{0,24},{8,0},{16,8},{24,16},{1,25},{9,1},{17,9},{25,17},{2,26},{10... | collective-permute-start | bytes 442376 | tf_op jit(solution)/shard_map/ppermute | solution.py:292
  4.8 1.5 %collective-permute-start.5 = (bf16[6,96,128]{2,1,0:T(8,128)(2,1)S(1)}, bf16[6,96,128]{2,1,0:T(8,128)(2,1)S(1)}, u32[]{:S(2)}, u32[]{:S(2)}) collective-permute-start(bf16[6,96,128]{2,1,0:T(8,128)(2,1)S(1)} %bitcast.11), channel_id=1, source_target_pairs={{0,16},{8,24},{16,0},{24,8},{1,17},{9,25},{17,1},{25,9},{2,18},{10... | collective-permute-start | bytes 442376 | tf_op jit(solution)/shard_map/ppermute | solution.py:292
  7.0 0.7 %pad_add_fusion.numbers = s32[4]{0:T(128)S(1)} fusion(s32[1]{0:T(128)S(6)} %copy.7, s32[3]{0:T(128)} %param.6), kind=kLoop, calls=%fused_computation.1 | loop fusion | flops 4 | bytes 32 | tf_op jit(solution)/shard_map/concatenate | solution.py:319
  7.7 0.0 collective-permute-done.other
  7.7 0.0 collective-permute-done.1.outer
  7.7 0.7 %shard_map.46.phased = bf16[6,96,128]{2,1,0:T(8,128)(2,1)S(1)} custom-call(s32[4]{0:T(128)S(1)} %pad_add_fusion.numbers, bf16[640,128]{1,0:T(8,128)(2,1)S(1)} %maximum_maximum_fusion.own, bf16[640,128]{1,0:T(8,128)(2,1)S(1)} %collective-permute-done.other, bf16[640,128]{1,0:T(8,128)(2,1)S(1)} %collective-permute-done.1.outer), custom_call_target="tpu_custom_call" | custom-call | tf_op jit(solution)/shard_map/pallas_call | solution.py:312
  8.4 1.0 %collective-permute-start.7 = (bf16[6,96,128]{2,1,0:T(8,128)(2,1)S(1)}, bf16[6,96,128]{2,1,0:T(8,128)(2,1)S(1)}, u32[]{:S(2)}, u32[]{:S(2)}) collective-permute-start(bf16[6,96,128]{2,1,0:T(8,128)(2,1)S(1)} %shard_map.46.phased), channel_id=1, source_target_pairs={{0,8},{8,16},{16,24},{24,0},{1,9},{9,17},{17,25},{25,1},{2,10},{10... | collective-permute-start | bytes 442376 | tf_op jit(solution)/shard_map/ppermute | solution.py:292
  9.5 1.1 %collective-permute-start.6 = (bf16[6,96,128]{2,1,0:T(8,128)(2,1)S(1)}, bf16[6,96,128]{2,1,0:T(8,128)(2,1)S(1)}, u32[]{:S(2)}, u32[]{:S(2)}) collective-permute-start(bf16[6,96,128]{2,1,0:T(8,128)(2,1)S(1)} %shard_map.46.phased), channel_id=1, source_target_pairs={{0,24},{8,0},{16,8},{24,16},{1,25},{9,1},{17,9},{25,17},{2,26},{10... | collective-permute-start | bytes 442376 | tf_op jit(solution)/shard_map/ppermute | solution.py:292
  10.5 1.0 %collective-permute-done.3.source = bf16[6,96,128]{2,1,0:T(8,128)(2,1)S(1)} collective-permute-done((bf16[6,96,128]{2,1,0:T(8,128)(2,1)S(1)}, bf16[6,96,128]{2,1,0:T(8,128)(2,1)S(1)}, u32[]{:S(2)}, u32[]{:S(2)}) %collective-permute-start.3) | collective-permute-done | bytes 147488 | tf_op jit(solution)/shard_map/ppermute | solution.py:292
  11.6 2.2 %collective-permute-start.2 = (bf16[6,96,128]{2,1,0:T(8,128)(2,1)S(1)}, bf16[6,96,128]{2,1,0:T(8,128)(2,1)S(1)}, u32[]{:S(2)}, u32[]{:S(2)}) collective-permute-start(bf16[6,96,128]{2,1,0:T(8,128)(2,1)S(1)} %shard_map.46.phased), channel_id=1, source_target_pairs={{0,16},{8,24},{16,0},{24,8},{1,17},{9,25},{17,1},{25,9},{2,18},{10... | collective-permute-start | bytes 442376 | tf_op jit(solution)/shard_map/ppermute | solution.py:292
  13.7 1.6 %shard_map.47.previous = bf16[4,576,768]{2,1,0:T(8,128)(2,1)S(1)} custom-call(bf16[6,96,128]{2,1,0:T(8,128)(2,1)S(1)} %bitcast.12), custom_call_target="tpu_custom_call" | custom-call | tf_op jit(solution)/shard_map/pallas_call | solution.py:342
  15.3 0.0 collective-permute-done.4.source
  15.3 0.0 collective-permute-done.5.source
  15.3 2.2 %shard_map.48 = (bf16[4,576,768]{2,1,0:T(8,128)(2,1)S(1)}, f32[4,576,192]{2,1,0:T(8,128)S(1)}) custom-call(bf16[6,96,128]{2,1,0:T(8,128)(2,1)S(1)} %collective-permute-done.3.source, bf16[6,96,128]{2,1,0:T(8,128)(2,1)S(1)} %shard_map.46.phased, bf16[4,576,768]{2,1,0:T(8,128)(2,1)S(1)} %shard_map.47.previous), custom_call_target="tpu_custom_call" | custom-call | tf_op jit(solution)/shard_map/pallas_call | solution.py:332
  17.6 0.0 collective-permute-done.7.phased
  17.6 2.2 %shard_map.49 = (bf16[4,576,768]{2,1,0:T(8,128)(2,1)S(1)}, f32[4,576,192]{2,1,0:T(8,128)S(1)}) custom-call(bf16[6,96,128]{2,1,0:T(8,128)(2,1)S(1)} %collective-permute-done.4.source, bf16[6,96,128]{2,1,0:T(8,128)(2,1)S(1)} %collective-permute-done.7.phased, bf16[4,576,768]{2,1,0:T(8,128)(2,1)S(1)} %get-tuple-element.19.previous, ...), custom_call_target="tpu_custom_call" | custom-call | tf_op jit(solution)/shard_map/pallas_call | solution.py:332
  19.8 0.0 collective-permute-done.6.phased
  19.8 2.2 %shard_map.50 = (bf16[4,576,768]{2,1,0:T(8,128)(2,1)S(1)}, f32[4,576,192]{2,1,0:T(8,128)S(1)}) custom-call(bf16[6,96,128]{2,1,0:T(8,128)(2,1)S(1)} %collective-permute-done.5.source, bf16[6,96,128]{2,1,0:T(8,128)(2,1)S(1)} %collective-permute-done.6.phased, bf16[4,576,768]{2,1,0:T(8,128)(2,1)S(1)} %get-tuple-element.21.previous, ...), custom_call_target="tpu_custom_call" | custom-call | tf_op jit(solution)/shard_map/pallas_call | solution.py:332
  22.1 0.0 collective-permute-done.2.phased
  22.1 1.3 %shard_map.51 = (bf16[192,1152]{1,0:T(8,128)(2,1)S(1)}, f32[192,1152]{1,0:T(8,128)S(1)}) custom-call(bf16[6,96,128]{2,1,0:T(8,128)(2,1)S(1)} %collective-permute-done.2.phased, bf16[4,576,768]{2,1,0:T(8,128)(2,1)S(1)} %get-tuple-element.23.crossed, f32[4,576,192]{2,1,0:T(8,128)S(1)} %get-tuple-element.24.sums), custom_call_target="tpu_custom_call" | custom-call | tf_op jit(solution)/shard_map/pallas_call | solution.py:354
  23.4 0.1 collective-permute-start.8
  23.5 1.8 %collective-permute-done.8.received = bf16[192,1152]{1,0:T(8,128)(2,1)S(1)} collective-permute-done((bf16[192,1152]{1,0:T(8,128)(2,1)S(1)}, bf16[192,1152]{1,0:T(8,128)(2,1)S(1)}, u32[]{:S(2)}, u32[]{:S(2)}) %collective-permute-start.8) | collective-permute-done | bytes 442400 | tf_op jit(solution)/shard_map/ppermute | solution.py:365
  25.3 0.3 shard_map.52
  25.6 31.9 %all_to_all.5.parts = bf16[32,56,128]{2,1,0:T(8,128)(2,1)S(1)} all-to-all(bf16[32,56,128]{2,1,0:T(8,128)(2,1)S(1)} %shard_map.52), channel_id=1, replica_groups=mesh['x'=4,'zl'=2,'y'=4,'zh'=4,'c'=2] {'x','zh','zl'}, dimensions={0} | all-to-all | bytes 917504 | tf_op jit(solution)/shard_map/all_to_all | solution.py:374
  57.6 0.9 %shard_map.53 = f32[3,8,2,1152]{3,2,1,0:T(2,128)} custom-call(bf16[32,56,128]{2,1,0:T(8,128)(2,1)S(1)} %all_to_all.5.parts), custom_call_target="tpu_custom_call" | custom-call | tf_op jit(solution)/shard_map/pallas_call | solution.py:375
  (1 shorter events, 0.0 us)
Async XLA Ops:
  1.9 5.8 %collective-permute-start = (bf16[640,128]{1,0:T(8,128)(2,1)S(1)}, bf16[640,128]{1,0:T(8,128)(2,1)S(1)}, u32[]{:S(2)}, u32[]{:S(2)}) collective-permute-start(bf16[640,128]{1,0:T(8,128)(2,1)S(1)} %maximum_maximum_fusion.own), channel_id=1, source_target_pairs={{0,1},{1,0},{2,3},{3,2},{4,5},{5,4},{6,7},{7,6},{8,9},{9,8},{10,11... | collective-permute-start | bytes 491528 | tf_op jit(solution)/shard_map/ppermute | solution.py:308
  2.0 5.7 %collective-permute-start.1 = (bf16[640,128]{1,0:T(8,128)(2,1)S(1)}, bf16[640,128]{1,0:T(8,128)(2,1)S(1)}, u32[]{:S(2)}, u32[]{:S(2)}) collective-permute-start(bf16[640,128]{1,0:T(8,128)(2,1)S(1)} %maximum_maximum_fusion.own), channel_id=1, source_target_pairs={{0,31},{1,2},{2,1},{3,4},{4,3},{5,6},{6,5},{7,8},{8,7},{9,10},{10,... | collective-permute-start | bytes 491528 | tf_op jit(solution)/shard_map/ppermute | solution.py:307
  2.7 8.9 %collective-permute-start.3 = (bf16[6,96,128]{2,1,0:T(8,128)(2,1)S(1)}, bf16[6,96,128]{2,1,0:T(8,128)(2,1)S(1)}, u32[]{:S(2)}, u32[]{:S(2)}) collective-permute-start(bf16[6,96,128]{2,1,0:T(8,128)(2,1)S(1)} %bitcast.9), channel_id=1, source_target_pairs={{0,8},{8,16},{16,24},{24,0},{1,9},{9,17},{17,25},{25,1},{2,10},{10... | collective-permute-start | bytes 442376 | tf_op jit(solution)/shard_map/ppermute | solution.py:292
  4.1 11.3 %collective-permute-start.4 = (bf16[6,96,128]{2,1,0:T(8,128)(2,1)S(1)}, bf16[6,96,128]{2,1,0:T(8,128)(2,1)S(1)}, u32[]{:S(2)}, u32[]{:S(2)}) collective-permute-start(bf16[6,96,128]{2,1,0:T(8,128)(2,1)S(1)} %bitcast.10), channel_id=1, source_target_pairs={{0,24},{8,0},{16,8},{24,16},{1,25},{9,1},{17,9},{25,17},{2,26},{10... | collective-permute-start | bytes 442376 | tf_op jit(solution)/shard_map/ppermute | solution.py:292
  4.8 10.5 %collective-permute-start.5 = (bf16[6,96,128]{2,1,0:T(8,128)(2,1)S(1)}, bf16[6,96,128]{2,1,0:T(8,128)(2,1)S(1)}, u32[]{:S(2)}, u32[]{:S(2)}) collective-permute-start(bf16[6,96,128]{2,1,0:T(8,128)(2,1)S(1)} %bitcast.11), channel_id=1, source_target_pairs={{0,16},{8,24},{16,0},{24,8},{1,17},{9,25},{17,1},{25,9},{2,18},{10... | collective-permute-start | bytes 442376 | tf_op jit(solution)/shard_map/ppermute | solution.py:292
  8.4 9.1 %collective-permute-start.7 = (bf16[6,96,128]{2,1,0:T(8,128)(2,1)S(1)}, bf16[6,96,128]{2,1,0:T(8,128)(2,1)S(1)}, u32[]{:S(2)}, u32[]{:S(2)}) collective-permute-start(bf16[6,96,128]{2,1,0:T(8,128)(2,1)S(1)} %shard_map.46.phased), channel_id=1, source_target_pairs={{0,8},{8,16},{16,24},{24,0},{1,9},{9,17},{17,25},{25,1},{2,10},{10... | collective-permute-start | bytes 442376 | tf_op jit(solution)/shard_map/ppermute | solution.py:292
  9.5 10.4 %collective-permute-start.6 = (bf16[6,96,128]{2,1,0:T(8,128)(2,1)S(1)}, bf16[6,96,128]{2,1,0:T(8,128)(2,1)S(1)}, u32[]{:S(2)}, u32[]{:S(2)}) collective-permute-start(bf16[6,96,128]{2,1,0:T(8,128)(2,1)S(1)} %shard_map.46.phased), channel_id=1, source_target_pairs={{0,24},{8,0},{16,8},{24,16},{1,25},{9,1},{17,9},{25,17},{2,26},{10... | collective-permute-start | bytes 442376 | tf_op jit(solution)/shard_map/ppermute | solution.py:292
  11.6 10.5 %collective-permute-start.2 = (bf16[6,96,128]{2,1,0:T(8,128)(2,1)S(1)}, bf16[6,96,128]{2,1,0:T(8,128)(2,1)S(1)}, u32[]{:S(2)}, u32[]{:S(2)}) collective-permute-start(bf16[6,96,128]{2,1,0:T(8,128)(2,1)S(1)} %shard_map.46.phased), channel_id=1, source_target_pairs={{0,16},{8,24},{16,0},{24,8},{1,17},{9,25},{17,1},{25,9},{2,18},{10... | collective-permute-start | bytes 442376 | tf_op jit(solution)/shard_map/ppermute | solution.py:292
  23.4 1.9 %collective-permute-start.8 = (bf16[192,1152]{1,0:T(8,128)(2,1)S(1)}, bf16[192,1152]{1,0:T(8,128)(2,1)S(1)}, u32[]{:S(2)}, u32[]{:S(2)}) collective-permute-start(bf16[192,1152]{1,0:T(8,128)(2,1)S(1)} %get-tuple-element.26), channel_id=1, source_target_pairs={{0,1},{1,0},{2,3},{3,2},{4,5},{5,4},{6,7},{7,6},{8,9},{9,8},{10,11... | collective-permute-start | bytes 1327112 | tf_op jit(solution)/shard_map/ppermute | solution.py:365

commit v6 on v0

--- a/solution.py
+++ b/solution.py
@@ -1,3 +1,4 @@
+import functools
 import math
 
 import jax
@@ -147,7 +148,7 @@
     )
 
 
-def six_rows(step, vectors, out):
+def six_rows(step, vectors, out, slot):
     core = lax.axis_index("c")
     keeper = jnp.where(step < 2, 1 - core, core)
     first = 24 * lax.axis_index("y") + 12 * (step % 2) + 3 * keeper
@@ -171,11 +172,11 @@
                     real = shared - (my_im[b] * total[c] - my_im[c] * total[b])
                     imag = shared + (my_re[b] * gap[c] - my_re[c] * gap[b])
                     column = a * SITES
-                    out[step, at : at + 16, column : column + SITES] = real.astype(
+                    out[slot, at : at + 16, column : column + SITES] = real.astype(
                         jnp.bfloat16
                     )
                     column += 3 * SITES
-                    out[step, at : at + 16, column : column + SITES] = imag.astype(
+                    out[slot, at : at + 16, column : column + SITES] = imag.astype(
                         jnp.bfloat16
                     )
 
@@ -194,7 +195,7 @@
     spread(source, vectors)
 
     def one_step(step, carry):
-        six_rows(step, vectors, out)
+        six_rows(step, vectors, out, step)
         return carry
 
     lax.fori_loop(0, 4, one_step, 0)
@@ -209,22 +210,33 @@
     def one_step(step, carry):
         term = times(previous[step], left)
         total[step] = term if sums is None else sums[step] + term
-        six_rows(step, vectors, out)
+        six_rows(step, vectors, out, step)
         return carry
 
     lax.fori_loop(0, 4, one_step, 0)
 
 
-def last_kernel(phased, crossed, sums, theirs, mine, left):
+def half_kernel(half, source, phased, previous, sums, out, total, vectors, left):
+    spread(source, vectors)
     left_operand(phased, left)
-    for out, half in ((theirs, 0), (mine, 1)):
-        tails = []
-        for part in range(2):
-            step = 2 * half + part
-            total = sums[step] + times(crossed[step], left)
-            out[:, 512 * part : 512 * part + 512] = total[:512].T.astype(out.dtype)
-            tails.append(total[512:])
-        out[:, 1024:] = jnp.concatenate(tails, 0).T.astype(out.dtype)
+
+    def one_step(part, carry):
+        step = 2 * half + part
+        total[part] = sums[step] + times(previous[step], left)
+        six_rows(step, vectors, out, part)
+        return carry
+
+    lax.fori_loop(0, 2, one_step, 0)
+
+
+def last_kernel(phased, crossed, sums, out, left):
+    left_operand(phased, left)
+    tails = []
+    for part in range(2):
+        total = sums[part] + times(crossed[part], left)
+        out[:, 512 * part : 512 * part + 512] = total[:512].T.astype(out.dtype)
+        tails.append(total[512:])
+    out[:, 1024:] = jnp.concatenate(tails, 0).T.astype(out.dtype)
 
 
 def pack_kernel(mine, received, out, total):
@@ -349,19 +361,32 @@
     )(own)
     crossed, sums = both(before, phased, crossed)
     crossed, sums = both(after, phased_before, crossed, sums)
-    crossed, sums = both(opposite, phased_after, crossed, sums)
-    sent, mine = pl.pallas_call(
-        last_kernel,
-        out_shape=(
-            jax.ShapeDtypeStruct((192, 1152), bf16),
-            jax.ShapeDtypeStruct((192, 1152), f32),
-        ),
-        in_specs=[vmem()] * 3,
-        out_specs=(vmem(), vmem()),
-        scratch_shapes=[left_scratch],
-        compiler_params=params(6),
-    )(phased_opposite, crossed, sums)
+
+    def last(half, kind, crossed, sums):
+        half_crossed, half_sums = pl.pallas_call(
+            functools.partial(half_kernel, half),
+            out_shape=(
+                jax.ShapeDtypeStruct((2, 576, DEPTH), bf16),
+                jax.ShapeDtypeStruct((2, 576, 192), f32),
+            ),
+            in_specs=[vmem()] * 4,
+            out_specs=(vmem(), vmem()),
+            scratch_shapes=[spread_scratch, left_scratch],
+            compiler_params=params(6),
+        )(opposite, phased_after, crossed, sums)
+        return pl.pallas_call(
+            last_kernel,
+            out_shape=jax.ShapeDtypeStruct((192, 1152), kind),
+            in_specs=[vmem()] * 3,
+            out_specs=vmem(),
+            scratch_shapes=[left_scratch],
+            compiler_params=params(6),
+        )(phased_opposite, half_crossed, half_sums)
+
+    sent = last(0, bf16, crossed, sums)
+    sent, sums = lax.optimization_barrier((sent, sums))
     received = lax.ppermute(sent, "c", swap)
+    mine = last(1, f32, crossed, sums)
     packed = pl.pallas_call(
         pack_kernel,
         out_shape=jax.ShapeDtypeStruct((32, 56, SITES), bf16),

time: 58.1 us -> 57.1 us (0.983)
  waiting for transfers between devices: 1.44 us -> 0.02 us
    pallas_call x1 -> x4, Pallas kernels: 1.33 us -> 3.96 us  [the longest x2 2.31 us: last(): pl.pallas_call(functools.partial(half_kernel, half), out_shape=(jax.Shape...]
    pallas_call x3 -> x2, Pallas kernels: 6.7 us -> 4.47 us  [both(): pl.pallas_call(both_kernel, out_shape=(crossed_shape, sums_shape), in_spe...]
    ppermute x1, waiting for transfers between devices: 1.42 us -> 0.01 us  [on_device(): received = lax.ppermute(sent, 'c', swap)]
  transfers between devices with their start and end apart: 9 -> 9, of which waited for: 1 -> 0; matrix products, arithmetic and copies ran while one was open for 1% -> 1% of each run, Pallas kernels for 15% -> 17%
where the time goes in v6:
time: 57.1 us; the launch traced here: 56.2 us
  blocking collectives  26.1 us (46%)
  starting transfers between devices  14.8 us (26%)
  Pallas kernels  11.8 us (21%)
  local copies, waits for them, and re-layouts  1.75 us (3%)
  other arithmetic  0.88 us (2%)
  between operations  0.79 us (1%)
    all_to_all x1, blocking collectives, on_device(): packed = lax.all_to_all(packed, ('x', 'zl', 'zh'), 0, 0, tiled=True)  26.1 us
    ppermute x6, starting transfers between devices, from_y(): return lax.ppermute(block, 'y', [(i, (i + by) % 4) for i in range(4)])  8.95 us
    pallas_call x2, Pallas kernels, both(): pl.pallas_call(both_kernel, out_shape=(crossed_shape, sums_shape), in_spe...  4.47 us
    ppermute x1, starting transfers between devices, on_device(): outer = lax.ppermute(joined, AXES, ring_pairs(outer_plane))  3.39 us
    ppermute x1, starting transfers between devices, on_device(): received = lax.ppermute(sent, 'c', swap)  2.38 us
    pallas_call x2, Pallas kernels, last(): pl.pallas_call(functools.partial(half_kernel, half), out_shape=(jax.Shape...  2.31 us
    pallas_call x2, Pallas kernels, last(): pl.pallas_call(last_kernel, out_shape=jax.ShapeDtypeStruct((192, 1152), k...  1.65 us
    pallas_call x1, Pallas kernels, on_device(): pl.pallas_call(crossed_kernel, out_shape=crossed_shape, in_specs=[vmem()]...  1.6 us
  transfers between devices with their start and end apart: 9, of which 0 were waited for; matrix products, arithmetic and copies ran while one was open for 1% of the time, Pallas kernels for 17%

profile of v6, /device:TPU:64, one launch (start us, length us, event | category | flops | bytes accessed | tf_op | source)
XLA Modules:
  0.0 56.2 jit_solution(12971133966478256981)
XLA Ops:
  0.0 0.9 %copy.5 = bf16[2,3,96,128]{3,2,1,0:T(8,128)(2,1)S(1)} copy(bf16[2,3,96,128]{3,0,1,2:T(2,128)(2,1)} %bitcast.13) | data formatting | bytes 294912 | tf_op jit(solution)/shard_map/transpose | solution.py:310
  0.9 0.7 %reshape.6 = bf16[54,128]{1,0:T(8,128)(2,1)S(1)} reshape(bf16[3,3,3,2,128]{4,3,2,1,0:T(2,128)(2,1)} %bitcast.14) | data formatting | bytes 27648 | tf_op jit(solution)/shard_map/reshape | solution.py:314
  1.7 0.1 pad.2.clone
  1.8 0.2 maximum_maximum_fusion.own
  1.9 0.1 collective-permute-start
  2.0 3.4 %collective-permute-start.1 = (bf16[640,128]{1,0:T(8,128)(2,1)S(1)}, bf16[640,128]{1,0:T(8,128)(2,1)S(1)}, u32[]{:S(2)}, u32[]{:S(2)}) collective-permute-start(bf16[640,128]{1,0:T(8,128)(2,1)S(1)} %maximum_maximum_fusion.own), channel_id=1, source_target_pairs={{0,31},{1,2},{2,1},{3,4},{4,3},{5,6},{6,5},{7,8},{8,7},{9,10},{10,... | collective-permute-start | bytes 491528 | tf_op jit(solution)/shard_map/ppermute | solution.py:318
  5.4 0.2 collective-permute-start.3
  5.6 3.1 %collective-permute-start.4 = (bf16[6,96,128]{2,1,0:T(8,128)(2,1)S(1)}, bf16[6,96,128]{2,1,0:T(8,128)(2,1)S(1)}, u32[]{:S(2)}, u32[]{:S(2)}) collective-permute-start(bf16[6,96,128]{2,1,0:T(8,128)(2,1)S(1)} %bitcast.10), channel_id=1, source_target_pairs={{0,24},{8,0},{16,8},{24,16},{1,25},{9,1},{17,9},{25,17},{2,26},{10... | collective-permute-start | bytes 442376 | tf_op jit(solution)/shard_map/ppermute | solution.py:303
  8.7 0.5 collective-permute-start.5
  9.9 0.7 %pad_add_fusion.numbers = s32[4]{0:T(128)S(1)} fusion(s32[1]{0:T(128)S(6)} %copy.7, s32[3]{0:T(128)} %param.6), kind=kLoop, calls=%fused_computation.1 | loop fusion | flops 4 | bytes 32 | tf_op jit(solution)/shard_map/concatenate | solution.py:330
  10.6 0.0 collective-permute-done.other
  10.6 0.0 collective-permute-done.1.outer
  10.6 0.5 shard_map.46.phased
  11.1 0.8 %collective-permute-start.7 = (bf16[6,96,128]{2,1,0:T(8,128)(2,1)S(1)}, bf16[6,96,128]{2,1,0:T(8,128)(2,1)S(1)}, u32[]{:S(2)}, u32[]{:S(2)}) collective-permute-start(bf16[6,96,128]{2,1,0:T(8,128)(2,1)S(1)} %shard_map.46.phased), channel_id=1, source_target_pairs={{0,8},{8,16},{16,24},{24,0},{1,9},{9,17},{17,25},{25,1},{2,10},{10... | collective-permute-start | bytes 442376 | tf_op jit(solution)/shard_map/ppermute | solution.py:303
  11.9 2.6 %collective-permute-start.6 = (bf16[6,96,128]{2,1,0:T(8,128)(2,1)S(1)}, bf16[6,96,128]{2,1,0:T(8,128)(2,1)S(1)}, u32[]{:S(2)}, u32[]{:S(2)}) collective-permute-start(bf16[6,96,128]{2,1,0:T(8,128)(2,1)S(1)} %shard_map.46.phased), channel_id=1, source_target_pairs={{0,24},{8,0},{16,8},{24,16},{1,25},{9,1},{17,9},{25,17},{2,26},{10... | collective-permute-start | bytes 442376 | tf_op jit(solution)/shard_map/ppermute | solution.py:303
  14.5 0.0 collective-permute-done.3.source
  14.5 1.8 %collective-permute-start.2 = (bf16[6,96,128]{2,1,0:T(8,128)(2,1)S(1)}, bf16[6,96,128]{2,1,0:T(8,128)(2,1)S(1)}, u32[]{:S(2)}, u32[]{:S(2)}) collective-permute-start(bf16[6,96,128]{2,1,0:T(8,128)(2,1)S(1)} %shard_map.46.phased), channel_id=1, source_target_pairs={{0,16},{8,24},{16,0},{24,8},{1,17},{9,25},{17,1},{25,9},{2,18},{10... | collective-permute-start | bytes 442376 | tf_op jit(solution)/shard_map/ppermute | solution.py:303
  16.3 1.6 %shard_map.47.previous = bf16[4,576,768]{2,1,0:T(8,128)(2,1)S(1)} custom-call(bf16[6,96,128]{2,1,0:T(8,128)(2,1)S(1)} %bitcast.12), custom_call_target="tpu_custom_call" | custom-call | tf_op jit(solution)/shard_map/pallas_call | solution.py:353
  17.9 0.0 collective-permute-done.4.source
  17.9 0.0 collective-permute-done.5.source
  17.9 2.2 %shard_map.48 = (bf16[4,576,768]{2,1,0:T(8,128)(2,1)S(1)}, f32[4,576,192]{2,1,0:T(8,128)S(1)}) custom-call(bf16[6,96,128]{2,1,0:T(8,128)(2,1)S(1)} %collective-permute-done.3.source, bf16[6,96,128]{2,1,0:T(8,128)(2,1)S(1)} %shard_map.46.phased, bf16[4,576,768]{2,1,0:T(8,128)(2,1)S(1)} %shard_map.47.previous), custom_call_target="tpu_custom_call" | custom-call | tf_op jit(solution)/shard_map/pallas_call | solution.py:343
  20.1 0.0 collective-permute-done.7.phased
  20.1 2.2 %shard_map.49 = (bf16[4,576,768]{2,1,0:T(8,128)(2,1)S(1)}, f32[4,576,192]{2,1,0:T(8,128)S(1)}) custom-call(bf16[6,96,128]{2,1,0:T(8,128)(2,1)S(1)} %collective-permute-done.4.source, bf16[6,96,128]{2,1,0:T(8,128)(2,1)S(1)} %collective-permute-done.7.phased, bf16[4,576,768]{2,1,0:T(8,128)(2,1)S(1)} %get-tuple-element.21.previous, ...), custom_call_target="tpu_custom_call" | custom-call | tf_op jit(solution)/shard_map/pallas_call | solution.py:343
  22.4 0.0 collective-permute-done.6.phased
  22.4 1.2 %shard_map.50 = (bf16[2,576,768]{2,1,0:T(8,128)(2,1)S(1)}, f32[2,576,192]{2,1,0:T(8,128)S(1)}) custom-call(bf16[6,96,128]{2,1,0:T(8,128)(2,1)S(1)} %collective-permute-done.5.source, bf16[6,96,128]{2,1,0:T(8,128)(2,1)S(1)} %collective-permute-done.6.phased, bf16[4,576,768]{2,1,0:T(8,128)(2,1)S(1)} %get-tuple-element.23.previous, ...), custom_call_target="tpu_custom_call" | custom-call | tf_op jit(solution)/shard_map/pallas_call | solution.py:366
  23.6 0.0 collective-permute-done.2.phased
  23.6 0.8 %shard_map.51 = bf16[192,1152]{1,0:T(8,128)(2,1)S(1)} custom-call(bf16[6,96,128]{2,1,0:T(8,128)(2,1)S(1)} %collective-permute-done.2.phased, bf16[2,576,768]{2,1,0:T(8,128)(2,1)S(1)} %get-tuple-element.25.crossed, f32[2,576,192]{2,1,0:T(8,128)S(1)} %get-tuple-element.26.sums), custom_call_target="tpu_custom_call" | custom-call | tf_op jit(solution)/shard_map/pallas_call | solution.py:377
  24.4 2.4 %collective-permute-start.8 = (bf16[192,1152]{1,0:T(8,128)(2,1)S(1)}, bf16[192,1152]{1,0:T(8,128)(2,1)S(1)}, u32[]{:S(2)}, u32[]{:S(2)}) collective-permute-start(bf16[192,1152]{1,0:T(8,128)(2,1)S(1)} %shard_map.51), channel_id=1, source_target_pairs={{0,1},{1,0},{2,3},{3,2},{4,5},{5,4},{6,7},{7,6},{8,9},{9,8},{10,11... | collective-permute-start | bytes 1327112 | tf_op jit(solution)/shard_map/ppermute | solution.py:388
  26.7 1.2 %shard_map.52 = (bf16[2,576,768]{2,1,0:T(8,128)(2,1)S(1)}, f32[2,576,192]{2,1,0:T(8,128)S(1)}) custom-call(bf16[6,96,128]{2,1,0:T(8,128)(2,1)S(1)} %collective-permute-done.5.source, bf16[6,96,128]{2,1,0:T(8,128)(2,1)S(1)} %collective-permute-done.6.phased, bf16[4,576,768]{2,1,0:T(8,128)(2,1)S(1)} %get-tuple-element.23.previous, ...), custom_call_target="tpu_custom_call" | custom-call | tf_op jit(solution)/shard_map/pallas_call | solution.py:366
  27.9 0.9 %shard_map.53.mine = f32[192,1152]{1,0:T(8,128)S(1)} custom-call(bf16[6,96,128]{2,1,0:T(8,128)(2,1)S(1)} %collective-permute-done.2.phased, bf16[2,576,768]{2,1,0:T(8,128)(2,1)S(1)} %get-tuple-element.28.crossed, f32[2,576,192]{2,1,0:T(8,128)S(1)} %get-tuple-element.29.sums), custom_call_target="tpu_custom_call" | custom-call | tf_op jit(solution)/shard_map/pallas_call | solution.py:377
  28.8 0.0 collective-permute-done.8.received
  28.8 0.3 shard_map.54
  29.1 26.1 %all_to_all.5.parts = bf16[32,56,128]{2,1,0:T(8,128)(2,1)S(1)} all-to-all(bf16[32,56,128]{2,1,0:T(8,128)(2,1)S(1)} %shard_map.54), channel_id=1, replica_groups=mesh['x'=4,'zl'=2,'y'=4,'zh'=4,'c'=2] {'x','zl','zh'}, dimensions={0} | all-to-all | bytes 917504 | tf_op jit(solution)/shard_map/all_to_all | solution.py:398
  55.3 0.9 %shard_map.55 = f32[3,8,2,1152]{3,2,1,0:T(2,128)} custom-call(bf16[32,56,128]{2,1,0:T(8,128)(2,1)S(1)} %all_to_all.5.parts), custom_call_target="tpu_custom_call" | custom-call | tf_op jit(solution)/shard_map/pallas_call | solution.py:399
  (1 shorter events, 0.0 us)
Async XLA Ops:
  1.9 8.7 %collective-permute-start = (bf16[640,128]{1,0:T(8,128)(2,1)S(1)}, bf16[640,128]{1,0:T(8,128)(2,1)S(1)}, u32[]{:S(2)}, u32[]{:S(2)}) collective-permute-start(bf16[640,128]{1,0:T(8,128)(2,1)S(1)} %maximum_maximum_fusion.own), channel_id=1, source_target_pairs={{0,1},{1,0},{2,3},{3,2},{4,5},{5,4},{6,7},{7,6},{8,9},{9,8},{10,11... | collective-permute-start | bytes 491528 | tf_op jit(solution)/shard_map/ppermute | solution.py:319
  2.0 8.6 %collective-permute-start.1 = (bf16[640,128]{1,0:T(8,128)(2,1)S(1)}, bf16[640,128]{1,0:T(8,128)(2,1)S(1)}, u32[]{:S(2)}, u32[]{:S(2)}) collective-permute-start(bf16[640,128]{1,0:T(8,128)(2,1)S(1)} %maximum_maximum_fusion.own), channel_id=1, source_target_pairs={{0,31},{1,2},{2,1},{3,4},{4,3},{5,6},{6,5},{7,8},{8,7},{9,10},{10,... | collective-permute-start | bytes 491528 | tf_op jit(solution)/shard_map/ppermute | solution.py:318
  5.4 9.0 %collective-permute-start.3 = (bf16[6,96,128]{2,1,0:T(8,128)(2,1)S(1)}, bf16[6,96,128]{2,1,0:T(8,128)(2,1)S(1)}, u32[]{:S(2)}, u32[]{:S(2)}) collective-permute-start(bf16[6,96,128]{2,1,0:T(8,128)(2,1)S(1)} %bitcast.9), channel_id=1, source_target_pairs={{0,8},{8,16},{16,24},{24,0},{1,9},{9,17},{17,25},{25,1},{2,10},{10... | collective-permute-start | bytes 442376 | tf_op jit(solution)/shard_map/ppermute | solution.py:303
  5.6 12.3 %collective-permute-start.4 = (bf16[6,96,128]{2,1,0:T(8,128)(2,1)S(1)}, bf16[6,96,128]{2,1,0:T(8,128)(2,1)S(1)}, u32[]{:S(2)}, u32[]{:S(2)}) collective-permute-start(bf16[6,96,128]{2,1,0:T(8,128)(2,1)S(1)} %bitcast.10), channel_id=1, source_target_pairs={{0,24},{8,0},{16,8},{24,16},{1,25},{9,1},{17,9},{25,17},{2,26},{10... | collective-permute-start | bytes 442376 | tf_op jit(solution)/shard_map/ppermute | solution.py:303
  8.7 9.2 %collective-permute-start.5 = (bf16[6,96,128]{2,1,0:T(8,128)(2,1)S(1)}, bf16[6,96,128]{2,1,0:T(8,128)(2,1)S(1)}, u32[]{:S(2)}, u32[]{:S(2)}) collective-permute-start(bf16[6,96,128]{2,1,0:T(8,128)(2,1)S(1)} %bitcast.11), channel_id=1, source_target_pairs={{0,16},{8,24},{16,0},{24,8},{1,17},{9,25},{17,1},{25,9},{2,18},{10... | collective-permute-start | bytes 442376 | tf_op jit(solution)/shard_map/ppermute | solution.py:303
  11.1 9.0 %collective-permute-start.7 = (bf16[6,96,128]{2,1,0:T(8,128)(2,1)S(1)}, bf16[6,96,128]{2,1,0:T(8,128)(2,1)S(1)}, u32[]{:S(2)}, u32[]{:S(2)}) collective-permute-start(bf16[6,96,128]{2,1,0:T(8,128)(2,1)S(1)} %shard_map.46.phased), channel_id=1, source_target_pairs={{0,8},{8,16},{16,24},{24,0},{1,9},{9,17},{17,25},{25,1},{2,10},{10... | collective-permute-start | bytes 442376 | tf_op jit(solution)/shard_map/ppermute | solution.py:303
  11.9 10.5 %collective-permute-start.6 = (bf16[6,96,128]{2,1,0:T(8,128)(2,1)S(1)}, bf16[6,96,128]{2,1,0:T(8,128)(2,1)S(1)}, u32[]{:S(2)}, u32[]{:S(2)}) collective-permute-start(bf16[6,96,128]{2,1,0:T(8,128)(2,1)S(1)} %shard_map.46.phased), channel_id=1, source_target_pairs={{0,24},{8,0},{16,8},{24,16},{1,25},{9,1},{17,9},{25,17},{2,26},{10... | collective-permute-start | bytes 442376 | tf_op jit(solution)/shard_map/ppermute | solution.py:303
  14.5 9.1 %collective-permute-start.2 = (bf16[6,96,128]{2,1,0:T(8,128)(2,1)S(1)}, bf16[6,96,128]{2,1,0:T(8,128)(2,1)S(1)}, u32[]{:S(2)}, u32[]{:S(2)}) collective-permute-start(bf16[6,96,128]{2,1,0:T(8,128)(2,1)S(1)} %shard_map.46.phased), channel_id=1, source_target_pairs={{0,16},{8,24},{16,0},{24,8},{1,17},{9,25},{17,1},{25,9},{2,18},{10... | collective-permute-start | bytes 442376 | tf_op jit(solution)/shard_map/ppermute | solution.py:303
  24.4 4.4 %collective-permute-start.8 = (bf16[192,1152]{1,0:T(8,128)(2,1)S(1)}, bf16[192,1152]{1,0:T(8,128)(2,1)S(1)}, u32[]{:S(2)}, u32[]{:S(2)}) collective-permute-start(bf16[192,1152]{1,0:T(8,128)(2,1)S(1)} %shard_map.51), channel_id=1, source_target_pairs={{0,1},{1,0},{2,3},{3,2},{4,5},{5,4},{6,7},{7,6},{8,9},{9,8},{10,11... | collective-permute-start | bytes 1327112 | tf_op jit(solution)/shard_map/ppermute | solution.py:388

commit v7 on v6

--- a/solution.py
+++ b/solution.py
@@ -360,7 +360,7 @@
         cost_estimate=short,
     )(own)
     crossed, sums = both(before, phased, crossed)
-    crossed, sums = both(after, phased_before, crossed, sums)
+    crossed, sums = both(opposite, phased_before, crossed, sums)
 
     def last(half, kind, crossed, sums):
         half_crossed, half_sums = pl.pallas_call(
@@ -373,7 +373,7 @@
             out_specs=(vmem(), vmem()),
             scratch_shapes=[spread_scratch, left_scratch],
             compiler_params=params(6),
-        )(opposite, phased_after, crossed, sums)
+        )(after, phased_opposite, crossed, sums)
         return pl.pallas_call(
             last_kernel,
             out_shape=jax.ShapeDtypeStruct((192, 1152), kind),
@@ -381,7 +381,7 @@
             out_specs=vmem(),
             scratch_shapes=[left_scratch],
             compiler_params=params(6),
-        )(phased_opposite, half_crossed, half_sums)
+        )(phased_after, half_crossed, half_sums)
 
     sent = last(0, bf16, crossed, sums)
     sent, sums = lax.optimization_barrier((sent, sums))

time: 57.1 us -> 57.3 us (level)
  blocking collectives: 26.1 us -> 26.9 us
    ppermute x1, starting transfers between devices: 2.38 us -> 1.49 us  [on_device(): received = lax.ppermute(sent, 'c', swap)]
    all_to_all x1, blocking collectives: 26.1 us -> 26.9 us  [on_device(): packed = lax.all_to_all(packed, ('x', 'zl', 'zh'), 0, 0, tiled=True)]
    ppermute x6, starting transfers between devices: 8.95 us -> 9.55 us  [from_y(): return lax.ppermute(block, 'y', [(i, (i + by) % 4) for i in range(4)])]
  transfers between devices with their start and end apart: 9 -> 9, of which waited for: 0 -> 1; matrix products, arithmetic and copies ran while one was open for 1% -> 1% of each run, Pallas kernels for 17% -> 17%
where the time goes in v7:
time: 57.3 us; the launch traced here: 56.9 us
  blocking collectives  26.9 us (47%)
  starting transfers between devices  14.5 us (25%)
  Pallas kernels  11.8 us (21%)
  local copies, waits for them, and re-layouts  1.75 us (3%)
  other arithmetic  0.88 us (2%)
  between operations  0.78 us (1%)
    all_to_all x1, blocking collectives, on_device(): packed = lax.all_to_all(packed, ('x', 'zl', 'zh'), 0, 0, tiled=True)  26.9 us
    ppermute x6, starting transfers between devices, from_y(): return lax.ppermute(block, 'y', [(i, (i + by) % 4) for i in range(4)])  9.55 us
    pallas_call x2, Pallas kernels, both(): pl.pallas_call(both_kernel, out_shape=(crossed_shape, sums_shape), in_spe...  4.46 us
    ppermute x1, starting transfers between devices, on_device(): outer = lax.ppermute(joined, AXES, ring_pairs(outer_plane))  3.39 us
    pallas_call x2, Pallas kernels, last(): pl.pallas_call(functools.partial(half_kernel, half), out_shape=(jax.Shape...  2.31 us
    pallas_call x2, Pallas kernels, last(): pl.pallas_call(last_kernel, out_shape=jax.ShapeDtypeStruct((192, 1152), k...  1.65 us
    pallas_call x1, Pallas kernels, on_device(): pl.pallas_call(crossed_kernel, out_shape=crossed_shape, in_specs=[vmem()]...  1.6 us
    ppermute x1, starting transfers between devices, on_device(): received = lax.ppermute(sent, 'c', swap)  1.49 us
  transfers between devices with their start and end apart: 9, of which 1 were waited for; matrix products, arithmetic and copies ran while one was open for 1% of the time, Pallas kernels for 17%

profile of v7, /device:TPU:64, one launch (start us, length us, event | category | flops | bytes accessed | tf_op | source)
XLA Modules:
  0.0 56.9 jit_solution(44220459073557997)
XLA Ops:
  0.0 0.9 %copy.5 = bf16[2,3,96,128]{3,2,1,0:T(8,128)(2,1)S(1)} copy(bf16[2,3,96,128]{3,0,1,2:T(2,128)(2,1)} %bitcast.13) | data formatting | bytes 294912 | tf_op jit(solution)/shard_map/transpose | solution.py:310
  0.9 0.7 %reshape.6 = bf16[54,128]{1,0:T(8,128)(2,1)S(1)} reshape(bf16[3,3,3,2,128]{4,3,2,1,0:T(2,128)(2,1)} %bitcast.14) | data formatting | bytes 27648 | tf_op jit(solution)/shard_map/reshape | solution.py:314
  1.7 0.1 pad.2.clone
  1.8 0.2 maximum_maximum_fusion.own
  1.9 0.1 collective-permute-start
  2.0 3.4 %collective-permute-start.1 = (bf16[640,128]{1,0:T(8,128)(2,1)S(1)}, bf16[640,128]{1,0:T(8,128)(2,1)S(1)}, u32[]{:S(2)}, u32[]{:S(2)}) collective-permute-start(bf16[640,128]{1,0:T(8,128)(2,1)S(1)} %maximum_maximum_fusion.own), channel_id=1, source_target_pairs={{0,31},{1,2},{2,1},{3,4},{4,3},{5,6},{6,5},{7,8},{8,7},{9,10},{10,... | collective-permute-start | bytes 491528 | tf_op jit(solution)/shard_map/ppermute | solution.py:318
  5.4 0.2 collective-permute-start.3
  5.6 3.1 %collective-permute-start.4 = (bf16[6,96,128]{2,1,0:T(8,128)(2,1)S(1)}, bf16[6,96,128]{2,1,0:T(8,128)(2,1)S(1)}, u32[]{:S(2)}, u32[]{:S(2)}) collective-permute-start(bf16[6,96,128]{2,1,0:T(8,128)(2,1)S(1)} %bitcast.10), channel_id=1, source_target_pairs={{0,24},{8,0},{16,8},{24,16},{1,25},{9,1},{17,9},{25,17},{2,26},{10... | collective-permute-start | bytes 442376 | tf_op jit(solution)/shard_map/ppermute | solution.py:303
  8.7 0.5 collective-permute-start.5
  9.9 0.7 %pad_add_fusion.numbers = s32[4]{0:T(128)S(1)} fusion(s32[1]{0:T(128)S(6)} %copy.7, s32[3]{0:T(128)} %param.6), kind=kLoop, calls=%fused_computation.1 | loop fusion | flops 4 | bytes 32 | tf_op jit(solution)/shard_map/concatenate | solution.py:330
  10.6 0.0 collective-permute-done.other
  10.6 0.0 collective-permute-done.1.outer
  10.6 0.5 shard_map.46.phased
  11.1 0.8 %collective-permute-start.7 = (bf16[6,96,128]{2,1,0:T(8,128)(2,1)S(1)}, bf16[6,96,128]{2,1,0:T(8,128)(2,1)S(1)}, u32[]{:S(2)}, u32[]{:S(2)}) collective-permute-start(bf16[6,96,128]{2,1,0:T(8,128)(2,1)S(1)} %shard_map.46.phased), channel_id=1, source_target_pairs={{0,8},{8,16},{16,24},{24,0},{1,9},{9,17},{17,25},{25,1},{2,10},{10... | collective-permute-start | bytes 442376 | tf_op jit(solution)/shard_map/ppermute | solution.py:303
  11.9 2.7 %collective-permute-start.6 = (bf16[6,96,128]{2,1,0:T(8,128)(2,1)S(1)}, bf16[6,96,128]{2,1,0:T(8,128)(2,1)S(1)}, u32[]{:S(2)}, u32[]{:S(2)}) collective-permute-start(bf16[6,96,128]{2,1,0:T(8,128)(2,1)S(1)} %shard_map.46.phased), channel_id=1, source_target_pairs={{0,16},{8,24},{16,0},{24,8},{1,17},{9,25},{17,1},{25,9},{2,18},{10... | collective-permute-start | bytes 442376 | tf_op jit(solution)/shard_map/ppermute | solution.py:303
  14.6 0.0 collective-permute-done.3.source
  14.6 2.2 %collective-permute-start.2 = (bf16[6,96,128]{2,1,0:T(8,128)(2,1)S(1)}, bf16[6,96,128]{2,1,0:T(8,128)(2,1)S(1)}, u32[]{:S(2)}, u32[]{:S(2)}) collective-permute-start(bf16[6,96,128]{2,1,0:T(8,128)(2,1)S(1)} %shard_map.46.phased), channel_id=1, source_target_pairs={{0,24},{8,0},{16,8},{24,16},{1,25},{9,1},{17,9},{25,17},{2,26},{10... | collective-permute-start | bytes 442376 | tf_op jit(solution)/shard_map/ppermute | solution.py:303
  16.9 1.6 %shard_map.47.previous = bf16[4,576,768]{2,1,0:T(8,128)(2,1)S(1)} custom-call(bf16[6,96,128]{2,1,0:T(8,128)(2,1)S(1)} %bitcast.12), custom_call_target="tpu_custom_call" | custom-call | tf_op jit(solution)/shard_map/pallas_call | solution.py:353
  18.5 0.0 collective-permute-done.4.source
  18.5 0.0 collective-permute-done.5.source
  18.5 2.2 %shard_map.48 = (bf16[4,576,768]{2,1,0:T(8,128)(2,1)S(1)}, f32[4,576,192]{2,1,0:T(8,128)S(1)}) custom-call(bf16[6,96,128]{2,1,0:T(8,128)(2,1)S(1)} %collective-permute-done.3.source, bf16[6,96,128]{2,1,0:T(8,128)(2,1)S(1)} %shard_map.46.phased, bf16[4,576,768]{2,1,0:T(8,128)(2,1)S(1)} %shard_map.47.previous), custom_call_target="tpu_custom_call" | custom-call | tf_op jit(solution)/shard_map/pallas_call | solution.py:343
  20.7 0.0 collective-permute-done.7.phased
  20.7 2.2 %shard_map.49 = (bf16[4,576,768]{2,1,0:T(8,128)(2,1)S(1)}, f32[4,576,192]{2,1,0:T(8,128)S(1)}) custom-call(bf16[6,96,128]{2,1,0:T(8,128)(2,1)S(1)} %collective-permute-done.5.source, bf16[6,96,128]{2,1,0:T(8,128)(2,1)S(1)} %collective-permute-done.7.phased, bf16[4,576,768]{2,1,0:T(8,128)(2,1)S(1)} %get-tuple-element.21.previous, ...), custom_call_target="tpu_custom_call" | custom-call | tf_op jit(solution)/shard_map/pallas_call | solution.py:343
  23.0 0.3 collective-permute-done.6.phased
  23.3 1.2 %shard_map.50 = (bf16[2,576,768]{2,1,0:T(8,128)(2,1)S(1)}, f32[2,576,192]{2,1,0:T(8,128)S(1)}) custom-call(bf16[6,96,128]{2,1,0:T(8,128)(2,1)S(1)} %collective-permute-done.4.source, bf16[6,96,128]{2,1,0:T(8,128)(2,1)S(1)} %collective-permute-done.6.phased, bf16[4,576,768]{2,1,0:T(8,128)(2,1)S(1)} %get-tuple-element.23.previous, ...), custom_call_target="tpu_custom_call" | custom-call | tf_op jit(solution)/shard_map/pallas_call | solution.py:366
  24.4 0.0 collective-permute-done.2.phased
  24.4 0.8 %shard_map.51 = bf16[192,1152]{1,0:T(8,128)(2,1)S(1)} custom-call(bf16[6,96,128]{2,1,0:T(8,128)(2,1)S(1)} %collective-permute-done.2.phased, bf16[2,576,768]{2,1,0:T(8,128)(2,1)S(1)} %get-tuple-element.25.crossed, f32[2,576,192]{2,1,0:T(8,128)S(1)} %get-tuple-element.26.sums), custom_call_target="tpu_custom_call" | custom-call | tf_op jit(solution)/shard_map/pallas_call | solution.py:377
  25.2 1.5 %collective-permute-start.8 = (bf16[192,1152]{1,0:T(8,128)(2,1)S(1)}, bf16[192,1152]{1,0:T(8,128)(2,1)S(1)}, u32[]{:S(2)}, u32[]{:S(2)}) collective-permute-start(bf16[192,1152]{1,0:T(8,128)(2,1)S(1)} %shard_map.51), channel_id=1, source_target_pairs={{0,1},{1,0},{2,3},{3,2},{4,5},{5,4},{6,7},{7,6},{8,9},{9,8},{10,11... | collective-permute-start | bytes 1327112 | tf_op jit(solution)/shard_map/ppermute | solution.py:388
  26.7 1.2 %shard_map.52 = (bf16[2,576,768]{2,1,0:T(8,128)(2,1)S(1)}, f32[2,576,192]{2,1,0:T(8,128)S(1)}) custom-call(bf16[6,96,128]{2,1,0:T(8,128)(2,1)S(1)} %collective-permute-done.4.source, bf16[6,96,128]{2,1,0:T(8,128)(2,1)S(1)} %collective-permute-done.6.phased, bf16[4,576,768]{2,1,0:T(8,128)(2,1)S(1)} %get-tuple-element.23.previous, ...), custom_call_target="tpu_custom_call" | custom-call | tf_op jit(solution)/shard_map/pallas_call | solution.py:366
  27.9 0.9 %shard_map.53.mine = f32[192,1152]{1,0:T(8,128)S(1)} custom-call(bf16[6,96,128]{2,1,0:T(8,128)(2,1)S(1)} %collective-permute-done.2.phased, bf16[2,576,768]{2,1,0:T(8,128)(2,1)S(1)} %get-tuple-element.28.crossed, f32[2,576,192]{2,1,0:T(8,128)S(1)} %get-tuple-element.29.sums), custom_call_target="tpu_custom_call" | custom-call | tf_op jit(solution)/shard_map/pallas_call | solution.py:377
  28.8 0.0 collective-permute-done.8.received
  28.8 0.3 shard_map.54
  29.1 26.9 %all_to_all.5.parts = bf16[32,56,128]{2,1,0:T(8,128)(2,1)S(1)} all-to-all(bf16[32,56,128]{2,1,0:T(8,128)(2,1)S(1)} %shard_map.54), channel_id=1, replica_groups=mesh['x'=4,'zl'=2,'y'=4,'zh'=4,'c'=2] {'x','zl','zh'}, dimensions={0} | all-to-all | bytes 917504 | tf_op jit(solution)/shard_map/all_to_all | solution.py:398
  56.0 0.9 %shard_map.55 = f32[3,8,2,1152]{3,2,1,0:T(2,128)} custom-call(bf16[32,56,128]{2,1,0:T(8,128)(2,1)S(1)} %all_to_all.5.parts), custom_call_target="tpu_custom_call" | custom-call | tf_op jit(solution)/shard_map/pallas_call | solution.py:399
  (1 shorter events, 0.0 us)
Async XLA Ops:
  1.9 8.7 %collective-permute-start = (bf16[640,128]{1,0:T(8,128)(2,1)S(1)}, bf16[640,128]{1,0:T(8,128)(2,1)S(1)}, u32[]{:S(2)}, u32[]{:S(2)}) collective-permute-start(bf16[640,128]{1,0:T(8,128)(2,1)S(1)} %maximum_maximum_fusion.own), channel_id=1, source_target_pairs={{0,1},{1,0},{2,3},{3,2},{4,5},{5,4},{6,7},{7,6},{8,9},{9,8},{10,11... | collective-permute-start | bytes 491528 | tf_op jit(solution)/shard_map/ppermute | solution.py:319
  2.0 8.6 %collective-permute-start.1 = (bf16[640,128]{1,0:T(8,128)(2,1)S(1)}, bf16[640,128]{1,0:T(8,128)(2,1)S(1)}, u32[]{:S(2)}, u32[]{:S(2)}) collective-permute-start(bf16[640,128]{1,0:T(8,128)(2,1)S(1)} %maximum_maximum_fusion.own), channel_id=1, source_target_pairs={{0,31},{1,2},{2,1},{3,4},{4,3},{5,6},{6,5},{7,8},{8,7},{9,10},{10,... | collective-permute-start | bytes 491528 | tf_op jit(solution)/shard_map/ppermute | solution.py:318
  5.4 9.2 %collective-permute-start.3 = (bf16[6,96,128]{2,1,0:T(8,128)(2,1)S(1)}, bf16[6,96,128]{2,1,0:T(8,128)(2,1)S(1)}, u32[]{:S(2)}, u32[]{:S(2)}) collective-permute-start(bf16[6,96,128]{2,1,0:T(8,128)(2,1)S(1)} %bitcast.9), channel_id=1, source_target_pairs={{0,8},{8,16},{16,24},{24,0},{1,9},{9,17},{17,25},{25,1},{2,10},{10... | collective-permute-start | bytes 442376 | tf_op jit(solution)/shard_map/ppermute | solution.py:303
  5.6 12.9 %collective-permute-start.4 = (bf16[6,96,128]{2,1,0:T(8,128)(2,1)S(1)}, bf16[6,96,128]{2,1,0:T(8,128)(2,1)S(1)}, u32[]{:S(2)}, u32[]{:S(2)}) collective-permute-start(bf16[6,96,128]{2,1,0:T(8,128)(2,1)S(1)} %bitcast.10), channel_id=1, source_target_pairs={{0,24},{8,0},{16,8},{24,16},{1,25},{9,1},{17,9},{25,17},{2,26},{10... | collective-permute-start | bytes 442376 | tf_op jit(solution)/shard_map/ppermute | solution.py:303
  8.7 9.8 %collective-permute-start.5 = (bf16[6,96,128]{2,1,0:T(8,128)(2,1)S(1)}, bf16[6,96,128]{2,1,0:T(8,128)(2,1)S(1)}, u32[]{:S(2)}, u32[]{:S(2)}) collective-permute-start(bf16[6,96,128]{2,1,0:T(8,128)(2,1)S(1)} %bitcast.11), channel_id=1, source_target_pairs={{0,16},{8,24},{16,0},{24,8},{1,17},{9,25},{17,1},{25,9},{2,18},{10... | collective-permute-start | bytes 442376 | tf_op jit(solution)/shard_map/ppermute | solution.py:303
  11.1 9.6 %collective-permute-start.7 = (bf16[6,96,128]{2,1,0:T(8,128)(2,1)S(1)}, bf16[6,96,128]{2,1,0:T(8,128)(2,1)S(1)}, u32[]{:S(2)}, u32[]{:S(2)}) collective-permute-start(bf16[6,96,128]{2,1,0:T(8,128)(2,1)S(1)} %shard_map.46.phased), channel_id=1, source_target_pairs={{0,8},{8,16},{16,24},{24,0},{1,9},{9,17},{17,25},{25,1},{2,10},{10... | collective-permute-start | bytes 442376 | tf_op jit(solution)/shard_map/ppermute | solution.py:303
  11.9 11.4 %collective-permute-start.6 = (bf16[6,96,128]{2,1,0:T(8,128)(2,1)S(1)}, bf16[6,96,128]{2,1,0:T(8,128)(2,1)S(1)}, u32[]{:S(2)}, u32[]{:S(2)}) collective-permute-start(bf16[6,96,128]{2,1,0:T(8,128)(2,1)S(1)} %shard_map.46.phased), channel_id=1, source_target_pairs={{0,16},{8,24},{16,0},{24,8},{1,17},{9,25},{17,1},{25,9},{2,18},{10... | collective-permute-start | bytes 442376 | tf_op jit(solution)/shard_map/ppermute | solution.py:303
  14.6 9.8 %collective-permute-start.2 = (bf16[6,96,128]{2,1,0:T(8,128)(2,1)S(1)}, bf16[6,96,128]{2,1,0:T(8,128)(2,1)S(1)}, u32[]{:S(2)}, u32[]{:S(2)}) collective-permute-start(bf16[6,96,128]{2,1,0:T(8,128)(2,1)S(1)} %shard_map.46.phased), channel_id=1, source_target_pairs={{0,24},{8,0},{16,8},{24,16},{1,25},{9,1},{17,9},{25,17},{2,26},{10... | collective-permute-start | bytes 442376 | tf_op jit(solution)/shard_map/ppermute | solution.py:303
  25.2 3.5 %collective-permute-start.8 = (bf16[192,1152]{1,0:T(8,128)(2,1)S(1)}, bf16[192,1152]{1,0:T(8,128)(2,1)S(1)}, u32[]{:S(2)}, u32[]{:S(2)}) collective-permute-start(bf16[192,1152]{1,0:T(8,128)(2,1)S(1)} %shard_map.51), channel_id=1, source_target_pairs={{0,1},{1,0},{2,3},{3,2},{4,5},{5,4},{6,7},{7,6},{8,9},{9,8},{10,11... | collective-permute-start | bytes 1327112 | tf_op jit(solution)/shard_map/ppermute | solution.py:388

commit v8 on v6

--- a/solution.py
+++ b/solution.py
@@ -239,6 +239,11 @@
     out[:, 1024:] = jnp.concatenate(tails, 0).T.astype(out.dtype)
 
 
+def mine_kernel(source, phased, previous, sums, last, out, crossed, total, vectors, left):
+    half_kernel(1, source, phased, previous, sums, crossed, total, vectors, left)
+    last_kernel(last, crossed, total, out, left)
+
+
 def pack_kernel(mine, received, out, total):
     lane = lax.broadcasted_iota(jnp.int32, (8, SITES), 1)
     for tile in range(9):
@@ -386,7 +391,19 @@
     sent = last(0, bf16, crossed, sums)
     sent, sums = lax.optimization_barrier((sent, sums))
     received = lax.ppermute(sent, "c", swap)
-    mine = last(1, f32, crossed, sums)
+    mine = pl.pallas_call(
+        mine_kernel,
+        out_shape=jax.ShapeDtypeStruct((192, 1152), f32),
+        in_specs=[vmem()] * 5,
+        out_specs=vmem(),
+        scratch_shapes=[
+            pltpu.VMEM((2, 576, DEPTH), bf16),
+            pltpu.VMEM((2, 576, 192), f32),
+            spread_scratch,
+            left_scratch,
+        ],
+        compiler_params=params(10),
+    )(opposite, phased_after, crossed, sums, phased_opposite)
     packed = pl.pallas_call(
         pack_kernel,
         out_shape=jax.ShapeDtypeStruct((32, 56, SITES), bf16),

time: 57.1 us -> 57.1 us (level)
    pallas_call x0 -> x1, Pallas kernels: none -> 2.04 us  [on_device(): pl.pallas_call(mine_kernel, out_shape=jax.ShapeDtypeStruct((192, 1152), f...]
    pallas_call x2 -> x1, Pallas kernels: 2.31 us -> 1.16 us  [last(): pl.pallas_call(functools.partial(half_kernel, half), out_shape=(jax.Shape...]
    pallas_call x2 -> x1, Pallas kernels: 1.65 us -> 0.78 us  [last(): pl.pallas_call(last_kernel, out_shape=jax.ShapeDtypeStruct((192, 1152), k...]
where the time goes in v8:
time: 57.1 us; the launch traced here: 56.2 us
  blocking collectives  26.1 us (46%)
  starting transfers between devices  14.8 us (26%)
  Pallas kernels  11.8 us (21%)
  local copies, waits for them, and re-layouts  1.75 us (3%)
  other arithmetic  0.88 us (2%)
  between operations  0.78 us (1%)
    all_to_all x1, blocking collectives, on_device(): packed = lax.all_to_all(packed, ('x', 'zl', 'zh'), 0, 0, tiled=True)  26.1 us
    ppermute x6, starting transfers between devices, from_y(): return lax.ppermute(block, 'y', [(i, (i + by) % 4) for i in range(4)])  8.95 us
    pallas_call x2, Pallas kernels, both(): pl.pallas_call(both_kernel, out_shape=(crossed_shape, sums_shape), in_spe...  4.47 us
    ppermute x1, starting transfers between devices, on_device(): outer = lax.ppermute(joined, AXES, ring_pairs(outer_plane))  3.39 us
    ppermute x1, starting transfers between devices, on_device(): received = lax.ppermute(sent, 'c', swap)  2.38 us
    pallas_call x1, Pallas kernels, on_device(): pl.pallas_call(mine_kernel, out_shape=jax.ShapeDtypeStruct((192, 1152), f...  2.04 us
    pallas_call x1, Pallas kernels, on_device(): pl.pallas_call(crossed_kernel, out_shape=crossed_shape, in_specs=[vmem()]...  1.6 us
    pallas_call x1, Pallas kernels, last(): pl.pallas_call(functools.partial(half_kernel, half), out_shape=(jax.Shape...  1.16 us
  transfers between devices with their start and end apart: 9, of which 0 were waited for; matrix products, arithmetic and copies ran while one was open for 1% of the time, Pallas kernels for 17%

profile of v8, /device:TPU:64, one launch (start us, length us, event | category | flops | bytes accessed | tf_op | source)
XLA Modules:
  0.0 56.2 jit_solution(11732482473692419839)
XLA Ops:
  0.0 0.9 %copy.5 = bf16[2,3,96,128]{3,2,1,0:T(8,128)(2,1)S(1)} copy(bf16[2,3,96,128]{3,0,1,2:T(2,128)(2,1)} %bitcast.13) | data formatting | bytes 294912 | tf_op jit(solution)/shard_map/transpose | solution.py:315
  0.9 0.7 %reshape.7 = bf16[54,128]{1,0:T(8,128)(2,1)S(1)} reshape(bf16[3,3,3,2,128]{4,3,2,1,0:T(2,128)(2,1)} %bitcast.14) | data formatting | bytes 27648 | tf_op jit(solution)/shard_map/reshape | solution.py:319
  1.7 0.1 pad.2.clone
  1.8 0.2 maximum_maximum_fusion.own
  1.9 0.1 collective-permute-start.3
  2.0 3.4 %collective-permute-start.4 = (bf16[640,128]{1,0:T(8,128)(2,1)S(1)}, bf16[640,128]{1,0:T(8,128)(2,1)S(1)}, u32[]{:S(2)}, u32[]{:S(2)}) collective-permute-start(bf16[640,128]{1,0:T(8,128)(2,1)S(1)} %maximum_maximum_fusion.own), channel_id=1, source_target_pairs={{0,31},{1,2},{2,1},{3,4},{4,3},{5,6},{6,5},{7,8},{8,7},{9,10},{10,... | collective-permute-start | bytes 491528 | tf_op jit(solution)/shard_map/ppermute | solution.py:323
  5.4 0.2 collective-permute-start
  5.6 3.1 %collective-permute-start.1 = (bf16[6,96,128]{2,1,0:T(8,128)(2,1)S(1)}, bf16[6,96,128]{2,1,0:T(8,128)(2,1)S(1)}, u32[]{:S(2)}, u32[]{:S(2)}) collective-permute-start(bf16[6,96,128]{2,1,0:T(8,128)(2,1)S(1)} %bitcast.10), channel_id=1, source_target_pairs={{0,24},{8,0},{16,8},{24,16},{1,25},{9,1},{17,9},{25,17},{2,26},{10... | collective-permute-start | bytes 442376 | tf_op jit(solution)/shard_map/ppermute | solution.py:308
  8.7 0.5 collective-permute-start.2
  9.9 0.7 %pad_add_fusion.numbers = s32[4]{0:T(128)S(1)} fusion(s32[1]{0:T(128)S(6)} %copy.7, s32[3]{0:T(128)} %param.6), kind=kLoop, calls=%fused_computation.1 | loop fusion | flops 4 | bytes 32 | tf_op jit(solution)/shard_map/concatenate | solution.py:335
  10.6 0.0 collective-permute-done.3.other
  10.6 0.0 collective-permute-done.4.outer
  10.6 0.5 shard_map.46.phased
  11.1 0.8 %collective-permute-start.6 = (bf16[6,96,128]{2,1,0:T(8,128)(2,1)S(1)}, bf16[6,96,128]{2,1,0:T(8,128)(2,1)S(1)}, u32[]{:S(2)}, u32[]{:S(2)}) collective-permute-start(bf16[6,96,128]{2,1,0:T(8,128)(2,1)S(1)} %shard_map.46.phased), channel_id=1, source_target_pairs={{0,8},{8,16},{16,24},{24,0},{1,9},{9,17},{17,25},{25,1},{2,10},{10... | collective-permute-start | bytes 442376 | tf_op jit(solution)/shard_map/ppermute | solution.py:308
  11.9 2.6 %collective-permute-start.5 = (bf16[6,96,128]{2,1,0:T(8,128)(2,1)S(1)}, bf16[6,96,128]{2,1,0:T(8,128)(2,1)S(1)}, u32[]{:S(2)}, u32[]{:S(2)}) collective-permute-start(bf16[6,96,128]{2,1,0:T(8,128)(2,1)S(1)} %shard_map.46.phased), channel_id=1, source_target_pairs={{0,24},{8,0},{16,8},{24,16},{1,25},{9,1},{17,9},{25,17},{2,26},{10... | collective-permute-start | bytes 442376 | tf_op jit(solution)/shard_map/ppermute | solution.py:308
  14.5 0.0 collective-permute-done.source
  14.5 1.8 %collective-permute-start.7 = (bf16[6,96,128]{2,1,0:T(8,128)(2,1)S(1)}, bf16[6,96,128]{2,1,0:T(8,128)(2,1)S(1)}, u32[]{:S(2)}, u32[]{:S(2)}) collective-permute-start(bf16[6,96,128]{2,1,0:T(8,128)(2,1)S(1)} %shard_map.46.phased), channel_id=1, source_target_pairs={{0,16},{8,24},{16,0},{24,8},{1,17},{9,25},{17,1},{25,9},{2,18},{10... | collective-permute-start | bytes 442376 | tf_op jit(solution)/shard_map/ppermute | solution.py:308
  16.3 1.6 %shard_map.47.previous = bf16[4,576,768]{2,1,0:T(8,128)(2,1)S(1)} custom-call(bf16[6,96,128]{2,1,0:T(8,128)(2,1)S(1)} %bitcast.12), custom_call_target="tpu_custom_call" | custom-call | tf_op jit(solution)/shard_map/pallas_call | solution.py:358
  17.9 0.0 collective-permute-done.1.source
  17.9 0.0 collective-permute-done.2.source
  17.9 2.2 %shard_map.48 = (bf16[4,576,768]{2,1,0:T(8,128)(2,1)S(1)}, f32[4,576,192]{2,1,0:T(8,128)S(1)}) custom-call(bf16[6,96,128]{2,1,0:T(8,128)(2,1)S(1)} %collective-permute-done.source, bf16[6,96,128]{2,1,0:T(8,128)(2,1)S(1)} %shard_map.46.phased, bf16[4,576,768]{2,1,0:T(8,128)(2,1)S(1)} %shard_map.47.previous), custom_call_target="tpu_custom_call" | custom-call | tf_op jit(solution)/shard_map/pallas_call | solution.py:348
  20.1 0.0 collective-permute-done.6.phased
  20.1 2.2 %shard_map.49 = (bf16[4,576,768]{2,1,0:T(8,128)(2,1)S(1)}, f32[4,576,192]{2,1,0:T(8,128)S(1)}) custom-call(bf16[6,96,128]{2,1,0:T(8,128)(2,1)S(1)} %collective-permute-done.1.source, bf16[6,96,128]{2,1,0:T(8,128)(2,1)S(1)} %collective-permute-done.6.phased, bf16[4,576,768]{2,1,0:T(8,128)(2,1)S(1)} %get-tuple-element.19.previous, ...), custom_call_target="tpu_custom_call" | custom-call | tf_op jit(solution)/shard_map/pallas_call | solution.py:348
  22.4 0.0 collective-permute-done.5.phased
  22.4 1.2 %shard_map.50 = (bf16[2,576,768]{2,1,0:T(8,128)(2,1)S(1)}, f32[2,576,192]{2,1,0:T(8,128)S(1)}) custom-call(bf16[6,96,128]{2,1,0:T(8,128)(2,1)S(1)} %collective-permute-done.2.source, bf16[6,96,128]{2,1,0:T(8,128)(2,1)S(1)} %collective-permute-done.5.phased, bf16[4,576,768]{2,1,0:T(8,128)(2,1)S(1)} %get-tuple-element.21.previous, ...), custom_call_target="tpu_custom_call" | custom-call | tf_op jit(solution)/shard_map/pallas_call | solution.py:371
  23.5 0.0 collective-permute-done.7.phased.last
  23.6 0.8 %shard_map.51 = bf16[192,1152]{1,0:T(8,128)(2,1)S(1)} custom-call(bf16[6,96,128]{2,1,0:T(8,128)(2,1)S(1)} %collective-permute-done.7.phased.last, bf16[2,576,768]{2,1,0:T(8,128)(2,1)S(1)} %get-tuple-element.23.crossed, f32[2,576,192]{2,1,0:T(8,128)S(1)} %get-tuple-element.24.sums), custom_call_target="tpu_custom_call" | custom-call | tf_op jit(solution)/shard_map/pallas_call | solution.py:382
  24.3 2.4 %collective-permute-start.8 = (bf16[192,1152]{1,0:T(8,128)(2,1)S(1)}, bf16[192,1152]{1,0:T(8,128)(2,1)S(1)}, u32[]{:S(2)}, u32[]{:S(2)}) collective-permute-start(bf16[192,1152]{1,0:T(8,128)(2,1)S(1)} %shard_map.51), channel_id=1, source_target_pairs={{0,1},{1,0},{2,3},{3,2},{4,5},{5,4},{6,7},{7,6},{8,9},{9,8},{10,11... | collective-permute-start | bytes 1327112 | tf_op jit(solution)/shard_map/ppermute | solution.py:393
  26.7 2.0 %shard_map.52.mine = f32[192,1152]{1,0:T(8,128)S(1)} custom-call(bf16[6,96,128]{2,1,0:T(8,128)(2,1)S(1)} %collective-permute-done.2.source, bf16[6,96,128]{2,1,0:T(8,128)(2,1)S(1)} %collective-permute-done.5.phased, bf16[4,576,768]{2,1,0:T(8,128)(2,1)S(1)} %get-tuple-element.21.previous, f32[4,576,192]{2,1,0:T(8,128)S(1)} %get-tuple-element.25.sums, ...), custom_call_target="tpu_custom_call" | custom-call | tf_op jit(solution)/shard_map/pallas_call | solution.py:394
  28.8 0.0 collective-permute-done.8.received
  28.8 0.3 shard_map.53
  29.1 26.1 %all_to_all.5.parts = bf16[32,56,128]{2,1,0:T(8,128)(2,1)S(1)} all-to-all(bf16[32,56,128]{2,1,0:T(8,128)(2,1)S(1)} %shard_map.53), channel_id=1, replica_groups=mesh['x'=4,'zl'=2,'y'=4,'zh'=4,'c'=2] {'x','zl','zh'}, dimensions={0} | all-to-all | bytes 917504 | tf_op jit(solution)/shard_map/all_to_all | solution.py:415
  55.3 0.9 %shard_map.54 = f32[3,8,2,1152]{3,2,1,0:T(2,128)} custom-call(bf16[32,56,128]{2,1,0:T(8,128)(2,1)S(1)} %all_to_all.5.parts), custom_call_target="tpu_custom_call" | custom-call | tf_op jit(solution)/shard_map/pallas_call | solution.py:416
  (1 shorter events, 0.0 us)
Async XLA Ops:
  1.9 8.7 %collective-permute-start.3 = (bf16[640,128]{1,0:T(8,128)(2,1)S(1)}, bf16[640,128]{1,0:T(8,128)(2,1)S(1)}, u32[]{:S(2)}, u32[]{:S(2)}) collective-permute-start(bf16[640,128]{1,0:T(8,128)(2,1)S(1)} %maximum_maximum_fusion.own), channel_id=1, source_target_pairs={{0,1},{1,0},{2,3},{3,2},{4,5},{5,4},{6,7},{7,6},{8,9},{9,8},{10,11... | collective-permute-start | bytes 491528 | tf_op jit(solution)/shard_map/ppermute | solution.py:324
  2.0 8.6 %collective-permute-start.4 = (bf16[640,128]{1,0:T(8,128)(2,1)S(1)}, bf16[640,128]{1,0:T(8,128)(2,1)S(1)}, u32[]{:S(2)}, u32[]{:S(2)}) collective-permute-start(bf16[640,128]{1,0:T(8,128)(2,1)S(1)} %maximum_maximum_fusion.own), channel_id=1, source_target_pairs={{0,31},{1,2},{2,1},{3,4},{4,3},{5,6},{6,5},{7,8},{8,7},{9,10},{10,... | collective-permute-start | bytes 491528 | tf_op jit(solution)/shard_map/ppermute | solution.py:323
  5.4 9.0 %collective-permute-start = (bf16[6,96,128]{2,1,0:T(8,128)(2,1)S(1)}, bf16[6,96,128]{2,1,0:T(8,128)(2,1)S(1)}, u32[]{:S(2)}, u32[]{:S(2)}) collective-permute-start(bf16[6,96,128]{2,1,0:T(8,128)(2,1)S(1)} %bitcast.9), channel_id=1, source_target_pairs={{0,8},{8,16},{16,24},{24,0},{1,9},{9,17},{17,25},{25,1},{2,10},{10... | collective-permute-start | bytes 442376 | tf_op jit(solution)/shard_map/ppermute | solution.py:308
  5.6 12.3 %collective-permute-start.1 = (bf16[6,96,128]{2,1,0:T(8,128)(2,1)S(1)}, bf16[6,96,128]{2,1,0:T(8,128)(2,1)S(1)}, u32[]{:S(2)}, u32[]{:S(2)}) collective-permute-start(bf16[6,96,128]{2,1,0:T(8,128)(2,1)S(1)} %bitcast.10), channel_id=1, source_target_pairs={{0,24},{8,0},{16,8},{24,16},{1,25},{9,1},{17,9},{25,17},{2,26},{10... | collective-permute-start | bytes 442376 | tf_op jit(solution)/shard_map/ppermute | solution.py:308
  8.7 9.1 %collective-permute-start.2 = (bf16[6,96,128]{2,1,0:T(8,128)(2,1)S(1)}, bf16[6,96,128]{2,1,0:T(8,128)(2,1)S(1)}, u32[]{:S(2)}, u32[]{:S(2)}) collective-permute-start(bf16[6,96,128]{2,1,0:T(8,128)(2,1)S(1)} %bitcast.11), channel_id=1, source_target_pairs={{0,16},{8,24},{16,0},{24,8},{1,17},{9,25},{17,1},{25,9},{2,18},{10... | collective-permute-start | bytes 442376 | tf_op jit(solution)/shard_map/ppermute | solution.py:308
  11.1 9.0 %collective-permute-start.6 = (bf16[6,96,128]{2,1,0:T(8,128)(2,1)S(1)}, bf16[6,96,128]{2,1,0:T(8,128)(2,1)S(1)}, u32[]{:S(2)}, u32[]{:S(2)}) collective-permute-start(bf16[6,96,128]{2,1,0:T(8,128)(2,1)S(1)} %shard_map.46.phased), channel_id=1, source_target_pairs={{0,8},{8,16},{16,24},{24,0},{1,9},{9,17},{17,25},{25,1},{2,10},{10... | collective-permute-start | bytes 442376 | tf_op jit(solution)/shard_map/ppermute | solution.py:308
  11.9 10.5 %collective-permute-start.5 = (bf16[6,96,128]{2,1,0:T(8,128)(2,1)S(1)}, bf16[6,96,128]{2,1,0:T(8,128)(2,1)S(1)}, u32[]{:S(2)}, u32[]{:S(2)}) collective-permute-start(bf16[6,96,128]{2,1,0:T(8,128)(2,1)S(1)} %shard_map.46.phased), channel_id=1, source_target_pairs={{0,24},{8,0},{16,8},{24,16},{1,25},{9,1},{17,9},{25,17},{2,26},{10... | collective-permute-start | bytes 442376 | tf_op jit(solution)/shard_map/ppermute | solution.py:308
  14.5 9.1 %collective-permute-start.7 = (bf16[6,96,128]{2,1,0:T(8,128)(2,1)S(1)}, bf16[6,96,128]{2,1,0:T(8,128)(2,1)S(1)}, u32[]{:S(2)}, u32[]{:S(2)}) collective-permute-start(bf16[6,96,128]{2,1,0:T(8,128)(2,1)S(1)} %shard_map.46.phased), channel_id=1, source_target_pairs={{0,16},{8,24},{16,0},{24,8},{1,17},{9,25},{17,1},{25,9},{2,18},{10... | collective-permute-start | bytes 442376 | tf_op jit(solution)/shard_map/ppermute | solution.py:308
  24.3 4.4 %collective-permute-start.8 = (bf16[192,1152]{1,0:T(8,128)(2,1)S(1)}, bf16[192,1152]{1,0:T(8,128)(2,1)S(1)}, u32[]{:S(2)}, u32[]{:S(2)}) collective-permute-start(bf16[192,1152]{1,0:T(8,128)(2,1)S(1)} %shard_map.51), channel_id=1, source_target_pairs={{0,1},{1,0},{2,3},{3,2},{4,5},{5,4},{6,7},{7,6},{8,9},{9,8},{10,11... | collective-permute-start | bytes 1327112 | tf_op jit(solution)/shard_map/ppermute | solution.py:393
